TPU v7x, 1024 devices: a whole 4x8x16 slice. The times are simulated.
1024 devices in a mesh: gx: 64 (over y, x, core), gy: 16 (over z).
Axes of the slice: x: 4, y: 8, z: 16, core: 2. Of those that a mesh axis runs over, the one named last changes fastest.
Arguments:
- trial: bfloat16 [256, 64, 8, 4, 256], P('gx', 'gy'), may hold values from -6 to 6
- positions: float32 [3, 256, 64, 8], P(None, 'gx', 'gy'), as said below
- pair_atoms: int32 [64, 16, 2, 512], P('gx', 'gy'), may hold values from 0 to 127, as said below
- pair_owner: int32 [64, 16, 512], P('gx', 'gy'), may hold values from 0 to 1023, as said below
- pair_image: int32 [64, 16, 3, 512], P('gx', 'gy'), may hold values from -1 to 1, as said below
- pair_count: int32 [64, 16], P('gx', 'gy'), may hold values from 128 to 512, as said below
Outputs:
- product: float32 [256, 64, 8, 4, 256], P('gx', 'gy')
Inputs may be any that keep to these rules, and one draw needn't show every extreme that they name: `pair_atoms`: row 0 holds atom i and row 1 atom j, each as index (x * 4 + y) * 8 + z of its lattice place inside its owner's block of 4 x 4 x 8 sites; atom i belongs to the device holding the list. The lattice sites of i and j differ by at most one step along each direction, counted periodically over the 256 x 64 x 8 sites, and not by zero along all three. Padding slots hold pairs of the same form. `pair_owner`: the owner of atom j is the listing device or one of its eight neighbours in the periodic grid of devices. `pair_image`: the number of whole box periods added to atom j's coordinates so that it lies beside atom i. `pair_count`: slots at or beyond a device's count are padding; some device's list is full. `positions`: each coordinate is 1.6 times the lattice index plus a displacement of at most 0.24.
All inputs are finite; a program needn't handle non-finite values.
Results may differ from a plain program's by a relative error of at most 0.0027.
Values may be sent and summed in bfloat16 or wider, within the bound.
No kernel may reach another device: no remote copies, remote signals or barrier semaphores. Data moves between devices by JAX's collectives and lax.ppermute only.
A program may use at most 32 MiB of HBM per device.

v0:
```python
import jax
import jax.numpy as jnp
from jax import lax
from jax.sharding import PartitionSpec as P

ONSITE_S = -0.22
ONSITE_P = 0.27
HOP_SS = -0.37
HOP_SP = 0.35
HOP_PPS = 0.4
HOP_PPP = -0.114
BOND_LENGTH = 1.536
LATTICE_STEP = 1.6


def padded_2(block, sides, width):
    for axis, dim in sides:
        count = lax.axis_size(axis)
        forward = [(i, i + 1) for i in range(count - 1)]
        forward.append((count - 1, 0))
        backward = [(target, source) for source, target in forward]
        low = lax.ppermute(
            lax.slice_in_dim(block, block.shape[dim] - width, None, axis=dim), axis, forward
        )
        high = lax.ppermute(lax.slice_in_dim(block, 0, width, axis=dim), axis, backward)
        block = jnp.concatenate([low, block, high], axis=dim)
    return block


def hopping(displacement):
    distance = jnp.sqrt(jnp.sum(displacement * displacement, axis=0))
    cosines = displacement / distance
    radial = (BOND_LENGTH / distance) ** 2 * jnp.exp(1.0 - distance / BOND_LENGTH)
    upper_row = [HOP_SS * radial] + [HOP_SP * radial * cosines[a] for a in range(3)]
    block_rows = [jnp.stack(upper_row)]
    for a in range(3):
        entries = [-HOP_SP * radial * cosines[a]]
        for b in range(3):
            diagonal_part = HOP_PPP if a == b else 0.0
            entries.append(((HOP_PPS - HOP_PPP) * cosines[a] * cosines[b] + diagonal_part) * radial)
        block_rows.append(jnp.stack(entries))
    return jnp.stack(block_rows)


def spread_rows(targets, targets_total, blocks, gathered, transpose_blocks):
    width = targets.shape[0]
    vectors = gathered.shape[2]
    selector = (targets[:, None] == jnp.arange(targets_total, dtype=jnp.int32)[None, :]).astype(
        jnp.bfloat16
    )
    if transpose_blocks:
        mixing = jnp.einsum("pn,bap->napb", selector, blocks)
    else:
        mixing = jnp.einsum("pn,abp->napb", selector, blocks)
    mixing = mixing.reshape(targets_total * 4, width * 4)
    summed = jnp.dot(
        mixing, gathered.reshape(width * 4, vectors), preferred_element_type=jnp.float32
    )
    return summed.reshape(targets_total, 4, vectors)


def shards(trial, positions, pair_atoms, pair_owner, pair_image, pair_count):
    side_x, side_y, depth_z = (trial.shape[0], trial.shape[1], trial.shape[2])
    vectors = trial.shape[4]
    per_device = side_x * side_y * depth_z
    slot_total = pair_owner.shape[2]
    slot_width = 64
    across_x = lax.axis_size("gx")
    across_y = lax.axis_size("gy")
    place_x = lax.axis_index("gx")
    place_y = lax.axis_index("gy")
    wide_y = side_y + 2
    ghost_total = (side_x + 2) * wide_y * depth_z
    period = jnp.array(
        [
            LATTICE_STEP * (side_x * across_x),
            LATTICE_STEP * (side_y * across_y),
            LATTICE_STEP * depth_z,
        ],
        jnp.float32,
    )
    onsite = jnp.array([ONSITE_S, ONSITE_P, ONSITE_P, ONSITE_P], jnp.float32)

    def ghost_index(cell_x, cell_y, cell_z):
        return ((cell_x + 1) * wide_y + cell_y + 1) * depth_z + cell_z

    def split_local(local_index):
        return (
            local_index // (side_y * depth_z),
            local_index // depth_z % side_y,
            local_index % depth_z,
        )

    ghost_pos = padded_2(positions, (("gx", 1), ("gy", 2)), 1).reshape(3, ghost_total)
    ghost_vec = padded_2(trial, (("gx", 0), ("gy", 1)), 1).reshape(ghost_total, 4, vectors)
    local_vec = trial.reshape(per_device, 4, vectors)
    first_all = pair_atoms[0, 0, 0]
    second_all = pair_atoms[0, 0, 1]
    owner_all = pair_owner[0, 0]
    image_all = pair_image[0, 0]
    pair_total = pair_count[0, 0]

    def slot_block(turn, running):
        result, ghost_terms = running
        begin_slot = turn * slot_width
        first_atom = lax.dynamic_slice_in_dim(first_all, begin_slot, slot_width)
        second_atom = lax.dynamic_slice_in_dim(second_all, begin_slot, slot_width)
        owner_ids = lax.dynamic_slice_in_dim(owner_all, begin_slot, slot_width)
        image_shift = lax.dynamic_slice_in_dim(image_all, begin_slot, slot_width, 1)
        live_mask = begin_slot + jnp.arange(slot_width, dtype=jnp.int32) < pair_total
        step_x = (owner_ids // across_y - place_x + 1) % across_x - 1
        step_y = (owner_ids % across_y - place_y + 1) % across_y - 1
        first_x, first_y, first_z = split_local(first_atom)
        second_x, second_y, second_z = split_local(second_atom)
        second_ghost = ghost_index(second_x + step_x * side_x, second_y + step_y * side_y, second_z)
        first_ghost = ghost_index(first_x, first_y, first_z)
        displacement = (
            ghost_pos[:, second_ghost]
            + image_shift.astype(jnp.float32) * period[:, None]
            - ghost_pos[:, first_ghost]
        )
        blocks = (hopping(displacement) * live_mask.astype(jnp.float32)).astype(jnp.bfloat16)
        result = result + spread_rows(
            first_atom, per_device, blocks, ghost_vec[second_ghost], False
        )
        ghost_terms = ghost_terms + spread_rows(
            second_ghost, ghost_total, blocks, local_vec[first_atom], True
        )
        return (result, ghost_terms)

    result = onsite[None, :, None] * local_vec.astype(jnp.float32)
    ghost_terms = jnp.zeros((ghost_total, 4, vectors), jnp.float32)
    running = (result, ghost_terms)
    running = lax.fori_loop(0, slot_total // slot_width, slot_block, running)
    result, ghost_terms = running
    ghost_grid = ghost_terms.reshape(side_x + 2, wide_y, depth_z, 4, vectors)
    padded = padded_2(ghost_grid.astype(jnp.bfloat16), (("gx", 0), ("gy", 1)), 1).astype(
        jnp.float32
    )
    returned = ghost_grid[1 : side_x + 1, 1 : side_y + 1]
    returned = (
        returned.at[0]
        .add(padded[0, 2 : side_y + 2])
        .at[side_x - 1]
        .add(padded[side_x + 3, 2 : side_y + 2])
    )
    returned = (
        returned.at[:, 0]
        .add(padded[2 : side_x + 2, 0])
        .at[:, side_y - 1]
        .add(padded[2 : side_x + 2, side_y + 3])
    )
    returned = returned.at[0, 0].add(padded[0, 0]).at[0, side_y - 1].add(padded[0, side_y + 3])
    returned = (
        returned.at[side_x - 1, 0]
        .add(padded[side_x + 3, 0])
        .at[side_x - 1, side_y - 1]
        .add(padded[side_x + 3, side_y + 3])
    )
    return result.reshape(side_x, side_y, depth_z, 4, vectors) + returned


def solution(mesh):
    in_specs = (
        P("gx", "gy", None, None, None),
        P(None, "gx", "gy", None),
        P("gx", "gy", None, None),
        P("gx", "gy", None),
        P("gx", "gy", None, None),
        P("gx", "gy"),
    )
    out_specs = P("gx", "gy", None, None, None)
    return jax.shard_map(shards, mesh=mesh, in_specs=in_specs, out_specs=out_specs, check_vma=False)
```

profile of v0, /device:TPU:31, one launch (start us, length us, event | category | flops | bytes accessed | tf_op | source)
XLA Modules:
  0.0 128.1 jit_solution(1993266869488233630)
XLA Ops:
  0.0 1.0 fusion.53
  1.0 4.9 %collective-permute-start.4 = (bf16[1,4,8,4,256]{4,3,2,1,0:T(4,128)(2,1)S(1)}, bf16[1,4,8,4,256]{4,3,2,1,0:T(4,128)(2,1)S(1)}, u32[]{:S(2)}, u32[]{:S(2)}) collective-permute-start(bf16[1,4,8,4,256]{4,3,2,1,0:T(4,128)(2,1)S(1)} %get-tuple-element.681), channel_id=1, source_target_pairs={{0,16},{16,32},{32,48},{48,64},{64,80},{80,96},{96,112},{112,128},... | collective-permute-start | bytes 196616 | tf_op jit(solution)/shard_map/ppermute | solution.py:22
  5.9 1.9 %collective-permute-start.5 = (bf16[1,4,8,4,256]{4,3,2,1,0:T(4,128)(2,1)S(1)}, bf16[1,4,8,4,256]{4,3,2,1,0:T(4,128)(2,1)S(1)}, u32[]{:S(2)}, u32[]{:S(2)}) collective-permute-start(bf16[1,4,8,4,256]{4,3,2,1,0:T(4,128)(2,1)S(1)} %get-tuple-element.680), channel_id=1, source_target_pairs={{16,0},{32,16},{48,32},{64,48},{80,64},{96,80},{112,96},{128,112},... | collective-permute-start | bytes 196616 | tf_op jit(solution)/shard_map/ppermute | solution.py:25
  8.5 7.0 %collective-permute-start = (f32[3,1,4,8]{3,2,1,0:T(4,128)S(1)}, f32[3,1,4,8]{3,2,1,0:T(4,128)S(1)}, u32[]{:S(2)}, u32[]{:S(2)}) collective-permute-start(f32[3,1,4,8]{3,2,1,0:T(4,128)S(1)} %get-tuple-element.685), channel_id=1, source_target_pairs={{0,16},{16,32},{32,48},{48,64},{64,80},{80,96},{96,112},{112,128},... | collective-permute-start | bytes 1160 | tf_op jit(solution)/shard_map/ppermute | solution.py:22
  15.5 1.9 %collective-permute-start.1 = (f32[3,1,4,8]{3,2,1,0:T(4,128)S(1)}, f32[3,1,4,8]{3,2,1,0:T(4,128)S(1)}, u32[]{:S(2)}, u32[]{:S(2)}) collective-permute-start(f32[3,1,4,8]{3,2,1,0:T(4,128)S(1)} %get-tuple-element.684), channel_id=1, source_target_pairs={{16,0},{32,16},{48,32},{64,48},{80,64},{96,80},{112,96},{128,112},... | collective-permute-start | bytes 1160 | tf_op jit(solution)/shard_map/ppermute | solution.py:25
  18.2 1.1 convert_multiply_fusion
  19.5 4.3 %collective-permute-done.1 = f32[3,1,4,8]{3,2,1,0:T(4,128)S(1)} collective-permute-done((f32[3,1,4,8]{3,2,1,0:T(4,128)S(1)}, f32[3,1,4,8]{3,2,1,0:T(4,128)S(1)}, u32[]{:S(2)}, u32[]{:S(2)}) %collective-permute-start.1) | collective-permute-done | bytes 416 | tf_op jit(solution)/shard_map/ppermute | solution.py:25
  23.8 4.0 %collective-permute-start.2 = (f32[3,6,1,8]{3,2,1,0:T(1,128)S(1)}, f32[3,6,1,8]{3,2,1,0:T(1,128)S(1)}, u32[]{:S(2)}, u32[]{:S(2)}) collective-permute-start(f32[3,6,1,8]{3,2,1,0:T(1,128)S(1)} %get-tuple-element.682), channel_id=1, source_target_pairs={{0,1},{1,2},{2,3},{3,4},{4,5},{5,6},{6,7},{7,8},{8,9},{9,10},{10,1... | collective-permute-start | bytes 1736 | tf_op jit(solution)/shard_map/ppermute | solution.py:22
  27.8 15.9 %collective-permute-start.3 = (f32[3,6,1,8]{3,2,1,0:T(1,128)S(1)}, f32[3,6,1,8]{3,2,1,0:T(1,128)S(1)}, u32[]{:S(2)}, u32[]{:S(2)}) collective-permute-start(f32[3,6,1,8]{3,2,1,0:T(1,128)S(1)} %get-tuple-element.683), channel_id=1, source_target_pairs={{1,0},{2,1},{3,2},{4,3},{5,4},{6,5},{7,6},{8,7},{9,8},{10,9},{11,1... | collective-permute-start | bytes 1736 | tf_op jit(solution)/shard_map/ppermute | solution.py:25
  44.0 1.9 %collective-permute-start.6 = (bf16[6,1,8,4,256]{4,3,2,1,0:T(4,128)(2,1)S(1)}, bf16[6,1,8,4,256]{4,3,2,1,0:T(4,128)(2,1)S(1)}, u32[]{:S(2)}, u32[]{:S(2)}) collective-permute-start(bf16[6,1,8,4,256]{4,3,2,1,0:T(4,128)(2,1)S(1)} %get-tuple-element.678), channel_id=1, source_target_pairs={{0,1},{1,2},{2,3},{3,4},{4,5},{5,6},{6,7},{7,8},{8,9},{9,10},{10,1... | collective-permute-start | bytes 294920 | tf_op jit(solution)/shard_map/ppermute | solution.py:22
  45.9 4.6 %collective-permute-start.7 = (bf16[6,1,8,4,256]{4,3,2,1,0:T(4,128)(2,1)S(1)}, bf16[6,1,8,4,256]{4,3,2,1,0:T(4,128)(2,1)S(1)}, u32[]{:S(2)}, u32[]{:S(2)}) collective-permute-start(bf16[6,1,8,4,256]{4,3,2,1,0:T(4,128)(2,1)S(1)} %get-tuple-element.679), channel_id=1, source_target_pairs={{1,0},{2,1},{3,2},{4,3},{5,4},{6,5},{7,6},{8,7},{9,8},{10,9},{11,1... | collective-permute-start | bytes 294920 | tf_op jit(solution)/shard_map/ppermute | solution.py:25
  50.9 1.3 collective-permute-done.7
  52.6 48.3 %while.28 = (s32[]{:T(128)}, f32[128,4,256]{2,0,1:T(8,128)S(1)}, f32[288,4,256]{2,0,1:T(8,128)S(1)}, s32[512]{0:T(512)S(1)}, s32[512]{0:T(512)}, /*index=5*/s32[...) while((s32[]{:T(128)}, f32[128,4,256]{2,0,1:T(8,128)S(1)}, ...), condition=%wide.region_2.3_spmd.clone.clone, body=%wide.region_0.2_spmd.sunk.clone.clone.sunk | while | flops 219328960 | bytes 4359169 | solution.py:134
  56.5 0.8 fusion.79
  62.5 0.8 fusion.79
  74.6 0.8 fusion.79
  98.8 0.8 fusion.79
  102.0 4.1 %collective-permute-start.8 = (bf16[1,6,8,4,256]{4,3,2,1,0:T(4,128)(2,1)S(1)}, bf16[1,6,8,4,256]{4,3,2,1,0:T(4,128)(2,1)S(1)}, u32[]{:S(2)}, u32[]{:S(2)}) collective-permute-start(bf16[1,6,8,4,256]{4,3,2,1,0:T(4,128)(2,1)S(1)} %get-tuple-element.676), channel_id=1, source_target_pairs={{0,16},{16,32},{32,48},{48,64},{64,80},{80,96},{96,112},{112,128},... | collective-permute-start | bytes 294920 | tf_op jit(solution)/shard_map/ppermute | solution.py:22
  106.2 1.9 %collective-permute-start.9 = (bf16[1,6,8,4,256]{4,3,2,1,0:T(4,128)(2,1)S(1)}, bf16[1,6,8,4,256]{4,3,2,1,0:T(4,128)(2,1)S(1)}, u32[]{:S(2)}, u32[]{:S(2)}) collective-permute-start(bf16[1,6,8,4,256]{4,3,2,1,0:T(4,128)(2,1)S(1)} %get-tuple-element.677), channel_id=1, source_target_pairs={{16,0},{32,16},{48,32},{64,48},{80,64},{96,80},{112,96},{128,112},... | collective-permute-start | bytes 294920 | tf_op jit(solution)/shard_map/ppermute | solution.py:25
  108.1 7.3 %collective-permute-done.9 = bf16[1,6,8,4,256]{4,3,2,1,0:T(4,128)(2,1)S(1)} collective-permute-done((bf16[1,6,8,4,256]{4,3,2,1,0:T(4,128)(2,1)S(1)}, bf16[1,6,8,4,256]{4,3,2,1,0:T(4,128)(2,1)S(1)}, u32[]{:S(2)}, u32[]{:S(2)}) %collective-permute-start.9) | collective-permute-done | bytes 98336 | tf_op jit(solution)/shard_map/ppermute | solution.py:25
  115.6 1.9 %collective-permute-start.10 = (bf16[8,1,8,4,256]{4,3,2,1,0:T(4,128)(2,1)S(1)}, bf16[8,1,8,4,256]{4,3,2,1,0:T(4,128)(2,1)S(1)}, u32[]{:S(2)}, u32[]{:S(2)}) collective-permute-start(bf16[8,1,8,4,256]{4,3,2,1,0:T(4,128)(2,1)S(1)} %get-tuple-element.674), channel_id=1, source_target_pairs={{0,1},{1,2},{2,3},{3,4},{4,5},{5,6},{6,7},{7,8},{8,9},{9,10},{10,1... | collective-permute-start | bytes 393224 | tf_op jit(solution)/shard_map/ppermute | solution.py:22
  117.5 5.2 %collective-permute-start.11 = (bf16[8,1,8,4,256]{4,3,2,1,0:T(4,128)(2,1)S(1)}, bf16[8,1,8,4,256]{4,3,2,1,0:T(4,128)(2,1)S(1)}, u32[]{:S(2)}, u32[]{:S(2)}) collective-permute-start(bf16[8,1,8,4,256]{4,3,2,1,0:T(4,128)(2,1)S(1)} %get-tuple-element.675), channel_id=1, source_target_pairs={{1,0},{2,1},{3,2},{4,3},{5,4},{6,5},{7,6},{8,7},{9,8},{10,9},{11,1... | collective-permute-start | bytes 393224 | tf_op jit(solution)/shard_map/ppermute | solution.py:25
  125.2 1.9 %fusion.45 = f32[4,4,8,4,256]{4,3,2,1,0:T(4,128)S(1)} fusion(f32[4,4,8,4,256]{4,3,2,1,0:T(4,128)S(1)} %fusion.48, s32[]{:T(128)} %bitcast.9, s32[]{:T(128)} %bitcast.10, bf16[8,1,8,4,256]{4,3,2,1,0:T(4,128)(2,1)S(1)} %collective-permute-done.11, bf16[8,1,8,4,256]{4,3,2,1,0:T(4,128)(2,1)S(1)} %collective-permute-done.10, ...), kind=kLoop, calls=%fused_computation.126 | loop fusion | flops 98304 | bytes 1114121 | tf_op jit(solution)/shard_map/scatter-add | solution.py:153
  127.2 0.9 add.492
  (271 shorter events, 50.2 us)
Async XLA Ops:
  0.0 43.7 %copy-start = (bf16[4,4,8,4,256]{4,3,2,1,0:T(4,128)(2,1)S(1)}, bf16[4,4,8,4,256]{4,3,2,1,0:T(4,128)(2,1)}, u32[]{:S(2)}) copy-start(bf16[4,4,8,4,256]{4,3,2,1,0:T(4,128)(2,1)} %param.26) | copy-start | bytes 786436
  0.0 19.5 %copy-start.1 = (f32[3,4,4,8]{3,2,1,0:T(4,128)S(1)}, f32[3,4,4,8]{3,2,1,0:T(4,128)}, u32[]{:S(2)}) copy-start(f32[3,4,4,8]{3,2,1,0:T(4,128)} %param.27) | copy-start | bytes 4612
  0.0 19.4 %copy-start.3 = (s32[1,1,3,512]{3,1,2,0:T(1,128)S(1)}, s32[1,1,3,512]{3,1,2,0:T(1,128)}, u32[]{:S(2)}) copy-start(s32[1,1,3,512]{3,1,2,0:T(1,128)} %param.30) | copy-start | bytes 18436
  1.0 42.7 %collective-permute-start.4 = (bf16[1,4,8,4,256]{4,3,2,1,0:T(4,128)(2,1)S(1)}, bf16[1,4,8,4,256]{4,3,2,1,0:T(4,128)(2,1)S(1)}, u32[]{:S(2)}, u32[]{:S(2)}) collective-permute-start(bf16[1,4,8,4,256]{4,3,2,1,0:T(4,128)(2,1)S(1)} %get-tuple-element.681), channel_id=1, source_target_pairs={{0,16},{16,32},{32,48},{48,64},{64,80},{80,96},{96,112},{112,128},... | collective-permute-start | bytes 196616 | tf_op jit(solution)/shard_map/ppermute | solution.py:22
  5.9 38.0 %collective-permute-start.5 = (bf16[1,4,8,4,256]{4,3,2,1,0:T(4,128)(2,1)S(1)}, bf16[1,4,8,4,256]{4,3,2,1,0:T(4,128)(2,1)S(1)}, u32[]{:S(2)}, u32[]{:S(2)}) collective-permute-start(bf16[1,4,8,4,256]{4,3,2,1,0:T(4,128)(2,1)S(1)} %get-tuple-element.680), channel_id=1, source_target_pairs={{16,0},{32,16},{48,32},{64,48},{80,64},{96,80},{112,96},{128,112},... | collective-permute-start | bytes 196616 | tf_op jit(solution)/shard_map/ppermute | solution.py:25
  8.5 10.9 %collective-permute-start = (f32[3,1,4,8]{3,2,1,0:T(4,128)S(1)}, f32[3,1,4,8]{3,2,1,0:T(4,128)S(1)}, u32[]{:S(2)}, u32[]{:S(2)}) collective-permute-start(f32[3,1,4,8]{3,2,1,0:T(4,128)S(1)} %get-tuple-element.685), channel_id=1, source_target_pairs={{0,16},{16,32},{32,48},{48,64},{64,80},{80,96},{96,112},{112,128},... | collective-permute-start | bytes 1160 | tf_op jit(solution)/shard_map/ppermute | solution.py:22
  15.5 8.3 %collective-permute-start.1 = (f32[3,1,4,8]{3,2,1,0:T(4,128)S(1)}, f32[3,1,4,8]{3,2,1,0:T(4,128)S(1)}, u32[]{:S(2)}, u32[]{:S(2)}) collective-permute-start(f32[3,1,4,8]{3,2,1,0:T(4,128)S(1)} %get-tuple-element.684), channel_id=1, source_target_pairs={{16,0},{32,16},{48,32},{64,48},{80,64},{96,80},{112,96},{128,112},... | collective-permute-start | bytes 1160 | tf_op jit(solution)/shard_map/ppermute | solution.py:25
  23.8 26.7 %collective-permute-start.2 = (f32[3,6,1,8]{3,2,1,0:T(1,128)S(1)}, f32[3,6,1,8]{3,2,1,0:T(1,128)S(1)}, u32[]{:S(2)}, u32[]{:S(2)}) collective-permute-start(f32[3,6,1,8]{3,2,1,0:T(1,128)S(1)} %get-tuple-element.682), channel_id=1, source_target_pairs={{0,1},{1,2},{2,3},{3,4},{4,5},{5,6},{6,7},{7,8},{8,9},{9,10},{10,1... | collective-permute-start | bytes 1736 | tf_op jit(solution)/shard_map/ppermute | solution.py:22
  27.8 22.7 %collective-permute-start.3 = (f32[3,6,1,8]{3,2,1,0:T(1,128)S(1)}, f32[3,6,1,8]{3,2,1,0:T(1,128)S(1)}, u32[]{:S(2)}, u32[]{:S(2)}) collective-permute-start(f32[3,6,1,8]{3,2,1,0:T(1,128)S(1)} %get-tuple-element.683), channel_id=1, source_target_pairs={{1,0},{2,1},{3,2},{4,3},{5,4},{6,5},{7,6},{8,7},{9,8},{10,9},{11,1... | collective-permute-start | bytes 1736 | tf_op jit(solution)/shard_map/ppermute | solution.py:25
  43.7 8.8 %copy-start.2 = (f32[3]{0:T(128)S(1)}, f32[3]{0:T(128)}, u32[]{:S(2)}) copy-start(f32[3]{0:T(128)} %constant.632.clone..sunk.3) | copy-start | bytes 40
  44.0 6.9 %collective-permute-start.6 = (bf16[6,1,8,4,256]{4,3,2,1,0:T(4,128)(2,1)S(1)}, bf16[6,1,8,4,256]{4,3,2,1,0:T(4,128)(2,1)S(1)}, u32[]{:S(2)}, u32[]{:S(2)}) collective-permute-start(bf16[6,1,8,4,256]{4,3,2,1,0:T(4,128)(2,1)S(1)} %get-tuple-element.678), channel_id=1, source_target_pairs={{0,1},{1,2},{2,3},{3,4},{4,5},{5,6},{6,7},{7,8},{8,9},{9,10},{10,1... | collective-permute-start | bytes 294920 | tf_op jit(solution)/shard_map/ppermute | solution.py:22
  45.9 6.2 %collective-permute-start.7 = (bf16[6,1,8,4,256]{4,3,2,1,0:T(4,128)(2,1)S(1)}, bf16[6,1,8,4,256]{4,3,2,1,0:T(4,128)(2,1)S(1)}, u32[]{:S(2)}, u32[]{:S(2)}) collective-permute-start(bf16[6,1,8,4,256]{4,3,2,1,0:T(4,128)(2,1)S(1)} %get-tuple-element.679), channel_id=1, source_target_pairs={{1,0},{2,1},{3,2},{4,3},{5,4},{6,5},{7,6},{8,7},{9,8},{10,9},{11,1... | collective-permute-start | bytes 294920 | tf_op jit(solution)/shard_map/ppermute | solution.py:25
  101.7 21.7 %copy-start.4 = (s32[5]{0:T(128)S(1)}, s32[5]{0:T(128)}, u32[]{:S(2)}) copy-start(s32[5]{0:T(128)} %constant.630.clone.1) | copy-start | bytes 64
  102.0 6.1 %collective-permute-start.8 = (bf16[1,6,8,4,256]{4,3,2,1,0:T(4,128)(2,1)S(1)}, bf16[1,6,8,4,256]{4,3,2,1,0:T(4,128)(2,1)S(1)}, u32[]{:S(2)}, u32[]{:S(2)}) collective-permute-start(bf16[1,6,8,4,256]{4,3,2,1,0:T(4,128)(2,1)S(1)} %get-tuple-element.676), channel_id=1, source_target_pairs={{0,16},{16,32},{32,48},{48,64},{64,80},{80,96},{96,112},{112,128},... | collective-permute-start | bytes 294920 | tf_op jit(solution)/shard_map/ppermute | solution.py:22
  106.2 9.3 %collective-permute-start.9 = (bf16[1,6,8,4,256]{4,3,2,1,0:T(4,128)(2,1)S(1)}, bf16[1,6,8,4,256]{4,3,2,1,0:T(4,128)(2,1)S(1)}, u32[]{:S(2)}, u32[]{:S(2)}) collective-permute-start(bf16[1,6,8,4,256]{4,3,2,1,0:T(4,128)(2,1)S(1)} %get-tuple-element.677), channel_id=1, source_target_pairs={{16,0},{32,16},{48,32},{64,48},{80,64},{96,80},{112,96},{128,112},... | collective-permute-start | bytes 294920 | tf_op jit(solution)/shard_map/ppermute | solution.py:25
  115.6 8.9 %collective-permute-start.10 = (bf16[8,1,8,4,256]{4,3,2,1,0:T(4,128)(2,1)S(1)}, bf16[8,1,8,4,256]{4,3,2,1,0:T(4,128)(2,1)S(1)}, u32[]{:S(2)}, u32[]{:S(2)}) collective-permute-start(bf16[8,1,8,4,256]{4,3,2,1,0:T(4,128)(2,1)S(1)} %get-tuple-element.674), channel_id=1, source_target_pairs={{0,1},{1,2},{2,3},{3,4},{4,5},{5,6},{6,7},{7,8},{8,9},{9,10},{10,1... | collective-permute-start | bytes 393224 | tf_op jit(solution)/shard_map/ppermute | solution.py:22
  117.5 7.2 %collective-permute-start.11 = (bf16[8,1,8,4,256]{4,3,2,1,0:T(4,128)(2,1)S(1)}, bf16[8,1,8,4,256]{4,3,2,1,0:T(4,128)(2,1)S(1)}, u32[]{:S(2)}, u32[]{:S(2)}) collective-permute-start(bf16[8,1,8,4,256]{4,3,2,1,0:T(4,128)(2,1)S(1)} %get-tuple-element.675), channel_id=1, source_target_pairs={{1,0},{2,1},{3,2},{4,3},{5,4},{6,5},{7,6},{8,7},{9,8},{10,9},{11,1... | collective-permute-start | bytes 393224 | tf_op jit(solution)/shard_map/ppermute | solution.py:25
where the time goes:
time: 129 us; the launch traced here: 128 us
  starting transfers between devices  55.3 us (43%)
  local copies, waits for them, and re-layouts  26.9 us (21%)
  other arithmetic  20.8 us (16%)
  waiting for transfers between devices  13.1 us (10%)
  matrix products  10.5 us (8%)
    ppermute x6, starting transfers between devices, padded_2(): lax.ppermute(lax.slice_in_dim(block, 0, width, axis=dim), axis, backward)  31.4 us
    ppermute x6, starting transfers between devices, padded_2(): lax.ppermute(lax.slice_in_dim(block, block.shape[dim] - width, None, axis...  23.8 us
    ppermute x6, waiting for transfers between devices, padded_2(): lax.ppermute(lax.slice_in_dim(block, 0, width, axis=dim), axis, backward)  13.1 us
    dot_general x16, matrix products, spread_rows(): jnp.dot(mixing, gathered.reshape(width * 4, vectors), preferred_element_t...  10.5 us
    select_n x8, other arithmetic, slot_block(): ghost_pos[:, second_ghost]  6.33 us
    gather x8, local copies, waits for them, and re-layouts, slot_block(): local_vec[first_atom]  5.54 us
    gather x8, local copies, waits for them, and re-layouts, slot_block(): ghost_vec[second_ghost]  5.54 us
    gather x16, local copies, waits for them, and re-layouts, slot_block(): ghost_pos[:, second_ghost]  5.42 us
  transfers between devices with their start and end apart: 12, of which 4 were waited for; matrix products, arithmetic and copies ran while one was open for 4% of the time, Pallas kernels for 0%

commit v1 on v0

v1 whole, which is shorter than its diff:
```python
import jax
import jax.numpy as jnp
from jax import lax
from jax.experimental import pallas as pl
from jax.experimental.pallas import tpu as pltpu
from jax.sharding import PartitionSpec as P

ONSITE_S = -0.22
ONSITE_P = 0.27
HOP_SS = -0.37
HOP_SP = 0.35
HOP_PPS = 0.4
HOP_PPP = -0.114
BOND_LENGTH = 1.536
LATTICE_STEP = 1.6

SIDE = 4
DEPTH = 8
ATOMS = SIDE * SIDE * DEPTH
FACE = SIDE * DEPTH
WIDE = FACE + 2 * DEPTH
NV = 256
POS_ROWS = 9
LIST_ROWS = 6
Y_AUX = 4
X_AUX = 7
F32 = jnp.float32
BF16 = jnp.bfloat16


def iota(shape, axis):
    return lax.broadcasted_iota(jnp.int32, shape, axis)


def onehot(values, expected):
    wide = [jnp.where(row == expected, 1.0, 0.0).astype(BF16) for row in values]
    return wide[0] if len(wide) == 1 else jnp.concatenate(wide, axis=1)


def dot_nt(a, b):
    return lax.dot_general(a, b, (((1,), (1,)), ((), ())), preferred_element_type=F32)


def dot(a, b):
    return jnp.dot(a, b, preferred_element_type=F32)


def list_of(rows):
    first = [rows[k : k + 1] for k in range(2)]
    key = [rows[4 + k : 5 + k] * float(ATOMS) + rows[2 + k : 3 + k] for k in range(2)]
    return first, key


def code(step_x, step_y):
    return (step_x + 1) * 3 + step_y + 1


def hopping(dx, dy, dz, count):
    square = jnp.maximum(dx * dx + dy * dy + dz * dz, 0.5)
    inverse = lax.rsqrt(square)
    cosines = [d * inverse for d in (dx, dy, dz)]
    ratio = BOND_LENGTH * inverse
    radial = ratio * ratio * jnp.exp(1.0 - square * inverse * (1.0 / BOND_LENGTH))

    def final(value):
        return (value.astype(BF16).astype(F32) * count).astype(BF16)

    grid = [[None] * 4 for _ in range(4)]
    grid[0][0] = final(HOP_SS * radial)
    for a in range(3):
        across = final(HOP_SP * radial * cosines[a])
        grid[0][1 + a] = across
        grid[1 + a][0] = -across
        for b in range(a, 3):
            entry = (HOP_PPS - HOP_PPP) * cosines[a] * cosines[b]
            if a == b:
                entry = entry + HOP_PPP
            grid[1 + a][1 + b] = grid[1 + b][1 + a] = final(entry * radial)
    return grid


def interleave(grid, rows, columns):
    total = None
    for b in range(4):
        stacked = jnp.concatenate([grid[a][b] for a in range(4)], axis=0)
        at = (iota((columns, 4 * columns), 1) == 4 * iota((columns, 4 * columns), 0) + b)
        part = dot(stacked, jnp.where(at, 1.0, 0.0).astype(BF16))
        total = part if total is None else total + part
    target = iota((4 * rows, 4 * rows), 0)
    source = (target & 3) * rows + (target >> 2)
    turn = jnp.where(iota((4 * rows, 4 * rows), 1) == source, 1.0, 0.0).astype(BF16)
    return dot(turn, total.astype(BF16)).astype(BF16)


def joined(block):
    n = block.shape[0]
    wide = block.astype(F32).reshape(n // 2, 2, 4, NV)
    return jnp.concatenate([wide[:, 0], wide[:, 1]], axis=1).reshape(4 * n, NV)


def z_shift(zi, zj, period):
    step = zj - zi
    return jnp.where(step > 1.5, -period, jnp.where(step < -1.5, period, 0.0))


def pack_y(trial, pos, lists, low, high, aux):
    for face, out in ((0, low), (SIDE - 1, high)):
        for x in range(SIDE):
            begin = (x * SIDE + face) * DEPTH
            out[x * DEPTH : (x + 1) * DEPTH] = trial[begin : begin + DEPTH]
        aux[...] = jnp.zeros_like(aux)
        points = jnp.concatenate(
            [
                pos[:, (x * SIDE + face) * DEPTH : (x * SIDE + face + 1) * DEPTH]
                for x in range(SIDE)
            ],
            axis=1,
        )
        for part in range(3):
            piece = points.astype(BF16).astype(F32)
            aux[3 * part : 3 * part + 3, :FACE] = piece
            points = points - piece
        aux[POS_ROWS : POS_ROWS + LIST_ROWS] = lists[...]
        for k in range(Y_AUX):
            out[FACE + k] = aux[4 * k : 4 * k + 4].astype(BF16)


def pack_x(trial, pos, lists, from_low, from_high, low, high, aux):
    sides = [
        jnp.concatenate([m[FACE + k].astype(F32) for k in range(Y_AUX)], axis=0)
        for m in (from_low, from_high)
    ]
    for face, out in ((0, low), (SIDE - 1, high)):
        out[:FACE] = trial[face * FACE : (face + 1) * FACE]
        column = slice(face * DEPTH, (face + 1) * DEPTH)
        out[FACE : FACE + DEPTH] = from_low[column]
        out[FACE + DEPTH : WIDE] = from_high[column]
        aux[...] = jnp.zeros_like(aux)
        points = pos[:, face * FACE : (face + 1) * FACE]
        for part in range(3):
            piece = points.astype(BF16).astype(F32)
            rows = slice(3 * part, 3 * part + 3)
            aux[rows, :WIDE] = jnp.concatenate(
                [piece] + [side[rows, column] for side in sides], axis=1
            )
            points = points - piece
        aux[POS_ROWS : POS_ROWS + LIST_ROWS] = lists[...]
        for n, side in enumerate(sides):
            begin = POS_ROWS + (n + 1) * LIST_ROWS
            aux[begin : begin + LIST_ROWS] = side[POS_ROWS : POS_ROWS + LIST_ROWS]
        for k in range(X_AUX):
            out[WIDE + k] = aux[4 * k : 4 * k + 4].astype(BF16)


def aux_rows(message, first, count):
    return jnp.concatenate([message[first + k].astype(F32) for k in range(count)], axis=0)


def ghost_points(rows, columns):
    return rows[0:3, :columns] + rows[3:6, :columns] + rows[6:9, :columns]


def assemble(periods, places, trial, pos, pos_t, lists, y_low, y_high, x_low, x_high, out, acc):
    own_first, own_key = list_of(lists[...])
    at_x, at_y = places[0], places[1]
    wrap_low_x = jnp.where(at_x == 0, -periods[0], 0.0)
    wrap_high_x = jnp.where(at_x == places[2] - 1, periods[0], 0.0)
    wrap_low_y = jnp.where(at_y == 0, -periods[1], 0.0)
    wrap_high_y = jnp.where(at_y == places[3] - 1, periods[1], 0.0)
    col = lambda n: iota((n, 1), 0)

    wave = joined(trial[...])
    here = float(code(0, 0) * ATOMS)
    atom = col(ATOMS).astype(F32)
    is_first = onehot(own_first, atom)
    is_second = onehot(own_key, atom + here)
    count = dot_nt(is_first, is_second) + dot_nt(is_second, is_first)
    dx, dy, dz = (pos[a : a + 1, :] - pos_t[:, a : a + 1] for a in range(3))
    zi = (col(ATOMS) & (DEPTH - 1)).astype(F32)
    zj = (iota((1, ATOMS), 1) & (DEPTH - 1)).astype(F32)
    dz = (pos[2:3, :] + z_shift(zi, zj, periods[2])) - pos_t[:, 2:3]
    matrix = interleave(hopping(dx, dy, dz, count), ATOMS, ATOMS)
    orbital = iota((4 * ATOMS, 1), 0) & 3
    onsite = jnp.where(orbital == 0, ONSITE_S, ONSITE_P)
    acc[...] = onsite * wave + dot(matrix, wave.astype(BF16))

    zi = (col(FACE) & (DEPTH - 1)).astype(F32)

    for side, message in ((-1, y_low), (1, y_high)):
        mine = 0 if side < 0 else SIDE - 1
        theirs = SIDE - 1 - mine
        rows = aux_rows(message, FACE, Y_AUX)
        first, key = list_of(rows[POS_ROWS : POS_ROWS + LIST_ROWS])
        k = col(FACE)
        line = (k >> 3) * (SIDE * DEPTH) + (k & (DEPTH - 1))
        my_atom = (line + mine * DEPTH).astype(F32)
        their_atom = (line + theirs * DEPTH).astype(F32)
        left = onehot(own_first + key, my_atom)
        left = jnp.concatenate(
            [
                onehot(own_first, my_atom),
                onehot(key, my_atom + float(code(0, -side) * ATOMS)),
            ],
            axis=1,
        )
        right = jnp.concatenate(
            [
                onehot(own_key, their_atom + float(code(0, side) * ATOMS)),
                onehot(first, their_atom),
            ],
            axis=1,
        )
        count = dot_nt(left, right)
        points = ghost_points(rows, FACE)
        mine_t = jnp.concatenate(
            [
                pos_t[(x * SIDE + mine) * DEPTH : (x * SIDE + mine + 1) * DEPTH, :]
                for x in range(SIDE)
            ],
            axis=0,
        )
        zj = (iota((1, FACE), 1) & (DEPTH - 1)).astype(F32)
        dx = points[0:1] - mine_t[:, 0:1]
        dy = (points[1:2] + (wrap_low_y if side < 0 else wrap_high_y)) - mine_t[:, 1:2]
        dz = (points[2:3] + z_shift(zi, zj, periods[2])) - mine_t[:, 2:3]
        matrix = interleave(hopping(dx, dy, dz, count), FACE, FACE)
        part = dot(matrix, joined(message[:FACE]).astype(BF16))
        for x in range(SIDE):
            begin = (x * SIDE + mine) * DEPTH * 4
            acc[begin : begin + 4 * DEPTH] += part[x * 4 * DEPTH : (x + 1) * 4 * DEPTH]

    for side, message in ((-1, x_low), (1, x_high)):
        mine = 0 if side < 0 else SIDE - 1
        theirs = SIDE - 1 - mine
        rows = aux_rows(message, WIDE, X_AUX)
        k = col(WIDE)
        corner = (SIDE - 1) * DEPTH
        their_atom = theirs * FACE + jnp.where(
            k < FACE, k, jnp.where(k < FACE + DEPTH, k - FACE + corner, k - FACE - DEPTH)
        )
        belongs = jnp.where(k < FACE, 0, jnp.where(k < FACE + DEPTH, -1, 1))
        my_atom = (col(FACE) + mine * FACE).astype(F32)
        target = (their_atom + code(side, belongs) * ATOMS).astype(F32)
        left = [onehot(own_first, my_atom)]
        right = [onehot(own_key, target)]
        for n, step in enumerate((0, -1, 1)):
            begin = POS_ROWS + n * LIST_ROWS
            first, key = list_of(rows[begin : begin + LIST_ROWS])
            left.append(onehot(key, my_atom + float(code(-side, -step) * ATOMS)))
            right.append(onehot(first, jnp.where(belongs == step, their_atom, -2).astype(F32)))
        count = dot_nt(jnp.concatenate(left, axis=1), jnp.concatenate(right, axis=1))
        points = ghost_points(rows, WIDE)
        lane = iota((1, WIDE), 1)
        zj = (lane & (DEPTH - 1)).astype(F32)
        shift_y = jnp.where(
            lane < FACE, 0.0, jnp.where(lane < FACE + DEPTH, wrap_low_y, wrap_high_y)
        )
        mine_t = pos_t[mine * FACE : (mine + 1) * FACE, :]
        dx = (points[0:1] + (wrap_low_x if side < 0 else wrap_high_x)) - mine_t[:, 0:1]
        dy = (points[1:2] + shift_y) - mine_t[:, 1:2]
        dz = (points[2:3] + z_shift(zi, zj, periods[2])) - mine_t[:, 2:3]
        matrix = interleave(hopping(dx, dy, dz, count), FACE, WIDE)
        part = dot(matrix, joined(message[:WIDE]).astype(BF16))
        acc[mine * 4 * FACE : (mine + 1) * 4 * FACE] += part

    total = acc[...].reshape(ATOMS // 2, 8, NV)
    out[...] = jnp.stack([total[:, :4], total[:, 4:]], axis=1).reshape(ATOMS, 4, NV)


def ring(count, step):
    return [(i, (i + step) % count) for i in range(count)]


def exchange(low, high, axis):
    count = lax.axis_size(axis)
    from_low = lax.ppermute(high, axis, ring(count, 1))
    from_high = lax.ppermute(low, axis, ring(count, -1))
    return from_low, from_high


def shards(trial, positions, pair_atoms, pair_owner, pair_image, pair_count):
    across_x = lax.axis_size("gx")
    across_y = lax.axis_size("gy")
    place_x = lax.axis_index("gx")
    place_y = lax.axis_index("gy")
    periods = (
        LATTICE_STEP * (SIDE * across_x),
        LATTICE_STEP * (SIDE * across_y),
        LATTICE_STEP * DEPTH,
    )
    vmem = pl.BlockSpec(memory_space=pltpu.VMEM)
    smem = pl.BlockSpec(memory_space=pltpu.SMEM)
    mine = trial.reshape(ATOMS, 4, NV)
    pos = positions.reshape(3, ATOMS)
    owner = pair_owner[0, 0]
    step_x = (owner // across_y - place_x + 1) % across_x - 1
    step_y = (owner % across_y - place_y + 1) % across_y - 1
    slot = jnp.arange(owner.shape[0], dtype=jnp.int32)
    first = jnp.where(slot < pair_count[0, 0], pair_atoms[0, 0, 0], -1)
    lists = jnp.stack([first, pair_atoms[0, 0, 1], code(step_x, step_y)])
    lists = lists.astype(F32).reshape(LIST_ROWS, NV)
    places = jnp.stack(
        [place_x, place_y, jnp.int32(across_x), jnp.int32(across_y)]
    ).astype(jnp.int32)

    def message(sites):
        return jax.ShapeDtypeStruct((sites, 4, NV), BF16)

    low, high = pl.pallas_call(
        pack_y,
        out_shape=[message(FACE + Y_AUX)] * 2,
        in_specs=[vmem] * 3,
        out_specs=[vmem] * 2,
        scratch_shapes=[pltpu.VMEM((4 * Y_AUX, NV), F32)],
    )(mine, pos, lists)
    y_low, y_high = exchange(low, high, "gy")
    low, high = pl.pallas_call(
        pack_x,
        out_shape=[message(WIDE + X_AUX)] * 2,
        in_specs=[vmem] * 5,
        out_specs=[vmem] * 2,
        scratch_shapes=[pltpu.VMEM((4 * X_AUX, NV), F32)],
    )(mine, pos, lists, y_low, y_high)
    x_low, x_high = exchange(low, high, "gx")
    product = pl.pallas_call(
        lambda *refs: assemble(periods, *refs),
        out_shape=jax.ShapeDtypeStruct((ATOMS, 4, NV), F32),
        in_specs=[smem] + [vmem] * 8,
        out_specs=vmem,
        scratch_shapes=[pltpu.VMEM((4 * ATOMS, NV), F32)],
        compiler_params=pltpu.CompilerParams(vmem_limit_bytes=32 * 1024 * 1024),
    )(places, mine, pos, pos.T, lists, y_low, y_high, x_low, x_high)
    return product.reshape(trial.shape)


def solution(mesh):
    in_specs = (
        P("gx", "gy", None, None, None),
        P(None, "gx", "gy", None),
        P("gx", "gy", None, None),
        P("gx", "gy", None),
        P("gx", "gy", None, None),
        P("gx", "gy"),
    )
    out_specs = P("gx", "gy", None, None, None)
    return jax.shard_map(shards, mesh=mesh, in_specs=in_specs, out_specs=out_specs, check_vma=False)
```

time: 129 us -> 51.2 us (0.40)
  starting transfers between devices: 55.3 us -> 27.8 us
  local copies, waits for them, and re-layouts: 26.9 us -> 3.86 us
  other arithmetic: 20.8 us -> 0.14 us
  matrix products: 10.5 us -> 0 us
  Pallas kernels: 0 us -> 8.86 us
  waiting for transfers between devices: 13.1 us -> 9.29 us
    ppermute x12 -> x4, starting transfers between devices: 55.3 us -> 27.8 us  [the longest x2 17.8 us: exchange(): from_high = lax.ppermute(low, axis, ring(count, -1))]
    gather x48 -> x0, local copies, waits for them, and re-layouts: 21.9 us -> none  [the longest x8 5.54 us: slot_block(): local_vec[first_atom]]
    dot_general x16 -> x0, matrix products: 10.5 us -> none  [spread_rows(): jnp.dot(mixing, gathered.reshape(width * 4, vectors), preferred_element_t...]
    pallas_call x0 -> x3, Pallas kernels: none -> 8.86 us  [the longest x1 5.35 us: shards(): pl.pallas_call(lambda *refs: assemble(periods, *refs), out_shape=jax.Shap...]
    select_n x16 -> x1, other arithmetic: 6.51 us -> 0.05 us  [shards(): first = jnp.where(slot < pair_count[0, 0], pair_atoms[0, 0, 0], -1)]
    convert_element_type x17 -> x1, other arithmetic: 5.53 us -> 0.01 us  [shards(): lists = lists.astype(F32).reshape(LIST_ROWS, NV)]
    ppermute x12 -> x4, waiting for transfers between devices: 13.1 us -> 9.29 us  [the longest x2 9.23 us: exchange(): from_high = lax.ppermute(low, axis, ring(count, -1))]
    slice x7 -> x0, local copies, waits for them, and re-layouts: 2.67 us -> none  [the longest x2 1.69 us: padded_2(): lax.slice_in_dim(block, 0, width, axis=dim)]
  transfers between devices with their start and end apart: 12 -> 4, of which waited for: 4 -> 2; matrix products, arithmetic and copies ran while one was open for 4% -> 0% of each run, Pallas kernels for 0% -> 0%
where the time goes in v1:
time: 51.2 us; the launch traced here: 50.7 us
  starting transfers between devices  27.8 us (54%)
  waiting for transfers between devices  9.29 us (18%)
  Pallas kernels  8.86 us (17%)
  local copies, waits for them, and re-layouts  3.86 us (8%)
  between operations  0.8 us (2%)
    ppermute x2, starting transfers between devices, exchange(): from_high = lax.ppermute(low, axis, ring(count, -1))  17.8 us
    ppermute x2, starting transfers between devices, exchange(): from_low = lax.ppermute(high, axis, ring(count, 1))  9.98 us
    ppermute x2, waiting for transfers between devices, exchange(): from_high = lax.ppermute(low, axis, ring(count, -1))  9.23 us
    pallas_call x1, Pallas kernels, shards(): pl.pallas_call(lambda *refs: assemble(periods, *refs), out_shape=jax.Shap...  5.35 us
    unnamed x21, local copies, waits for them, and re-layouts  2.61 us
    pallas_call x1, Pallas kernels, shards(): pl.pallas_call(pack_x, out_shape=[message(WIDE + X_AUX)] * 2, in_specs=[v...  1.81 us
    pallas_call x1, Pallas kernels, shards(): pl.pallas_call(pack_y, out_shape=[message(FACE + Y_AUX)] * 2, in_specs=[v...  1.71 us
  transfers between devices with their start and end apart: 4, of which 2 were waited for; matrix products, arithmetic and copies ran while one was open for 0% of the time, Pallas kernels for 0%

profile of v1, /device:TPU:31, one launch (start us, length us, event | category | flops | bytes accessed | tf_op | source)
XLA Modules:
  0.0 50.7 jit_solution(12604062753170720592)
XLA Ops:
  0.7 0.0 copy-done.8
  0.7 0.0 copy-start.7
  0.7 0.0 copy-done.9
  0.8 0.6 %convert_element_type.8.lists.refs_4_ = f32[6,256]{1,0:T(8,128)} reshape(f32[3,512]{1,0:T(4,128)S(1)} %add_convert_fusion) | data formatting | bytes 12288 | tf_op jit(solution)/shard_map/convert_element_type | solution.py:301
  1.4 0.0 copy-done.7
  1.4 0.2 copy.6
  1.6 0.6 %copy.9.pos.refs_2_ = f32[3,128]{1,0:T(4,128)} copy(f32[3,128]{0,1:T(8,128)S(1)} %bitcast.31) | data formatting | bytes 3072 | tf_op jit(solution)/shard_map/reshape | solution.py:294
  2.2 1.7 %shard_map.55 = (bf16[36,4,256]{2,1,0:T(4,128)(2,1)}, bf16[36,4,256]{2,1,0:T(4,128)(2,1)}) custom-call(bf16[128,4,256]{2,1,0:T(4,128)(2,1)} %bitcast.28, f32[3,128]{1,0:T(4,128)} %copy.9.pos.refs_2_, f32[6,256]{1,0:T(8,128)} %convert_element_type.8.lists.refs_4_), custom_call_target="tpu_custom_call" | custom-call | tf_op jit(solution)/shard_map/pallas_call | solution.py:309
  4.0 4.1 %collective-permute-start = (bf16[36,4,256]{2,1,0:T(4,128)(2,1)}, bf16[36,4,256]{2,1,0:T(4,128)(2,1)S(1)}, u32[]{:S(2)}, u32[]{:S(2)}) collective-permute-start(bf16[36,4,256]{2,1,0:T(4,128)(2,1)} %get-tuple-element.9), channel_id=1, source_target_pairs={{0,1},{1,2},{2,3},{3,4},{4,5},{5,6},{6,7},{7,8},{8,9},{9,10},{10,1... | collective-permute-start | bytes 221192 | tf_op jit(solution)/shard_map/ppermute | solution.py:276
  8.1 15.9 %collective-permute-start.1 = (bf16[36,4,256]{2,1,0:T(4,128)(2,1)}, bf16[36,4,256]{2,1,0:T(4,128)(2,1)S(1)}, u32[]{:S(2)}, u32[]{:S(2)}) collective-permute-start(bf16[36,4,256]{2,1,0:T(4,128)(2,1)} %get-tuple-element.10), channel_id=1, source_target_pairs={{0,15},{1,0},{2,1},{3,2},{4,3},{5,4},{6,5},{7,6},{8,7},{9,8},{10,9... | collective-permute-start | bytes 221192 | tf_op jit(solution)/shard_map/ppermute | solution.py:277
  24.0 0.0 collective-permute-done.from_low.refs_5_
  24.0 0.0 copy-start.1
  24.0 1.7 %collective-permute-done.1.from_high.refs_6_ = bf16[36,4,256]{2,1,0:T(4,128)(2,1)S(1)} collective-permute-done((bf16[36,4,256]{2,1,0:T(4,128)(2,1)}, bf16[36,4,256]{2,1,0:T(4,128)(2,1)S(1)}, u32[]{:S(2)}, u32[]{:S(2)}) %collective-permute-start.1) | collective-permute-done | bytes 73760 | tf_op jit(solution)/shard_map/ppermute | solution.py:277
  25.7 0.6 %copy-done.3 = bf16[36,4,256]{2,1,0:T(4,128)(2,1)} copy-done((bf16[36,4,256]{2,1,0:T(4,128)(2,1)}, bf16[36,4,256]{2,1,0:T(4,128)(2,1)S(1)}, u32[]{:S(2)}) %copy-start.3) | copy-done | bytes 73752
  26.3 1.8 %shard_map.56 = (bf16[55,4,256]{2,1,0:T(4,128)(2,1)}, bf16[55,4,256]{2,1,0:T(4,128)(2,1)}) custom-call(bf16[128,4,256]{2,1,0:T(4,128)(2,1)} %bitcast.29, f32[3,128]{1,0:T(4,128)} %copy.9.pos.refs_2_, f32[6,256]{1,0:T(8,128)} %convert_element_type.8.lists.refs_4_, bf16[36,4,256]{2,1,0:T(4,128)(2,1)} %copy-done.1, bf16[36,4,256]{2,1,0:T(4,128)(2,1)} %copy-done.3), custom_call_target="tpu_custom_call" | custom-call | tf_op jit(solution)/shard_map/pallas_call | solution.py:317
  28.1 5.9 %collective-permute-start.2 = (bf16[55,4,256]{2,1,0:T(4,128)(2,1)}, bf16[55,4,256]{2,1,0:T(4,128)(2,1)S(1)}, u32[]{:S(2)}, u32[]{:S(2)}) collective-permute-start(bf16[55,4,256]{2,1,0:T(4,128)(2,1)} %get-tuple-element.11), channel_id=1, source_target_pairs={{0,16},{16,32},{32,48},{48,64},{64,80},{80,96},{96,112},{112,128},... | collective-permute-start | bytes 337928 | tf_op jit(solution)/shard_map/ppermute | solution.py:276
  34.0 1.9 %collective-permute-start.3 = (bf16[55,4,256]{2,1,0:T(4,128)(2,1)}, bf16[55,4,256]{2,1,0:T(4,128)(2,1)S(1)}, u32[]{:S(2)}, u32[]{:S(2)}) collective-permute-start(bf16[55,4,256]{2,1,0:T(4,128)(2,1)} %get-tuple-element.12), channel_id=1, source_target_pairs={{0,1008},{16,0},{32,16},{48,32},{64,48},{80,64},{96,80},{112,96},{... | collective-permute-start | bytes 337928 | tf_op jit(solution)/shard_map/ppermute | solution.py:277
  35.9 0.0 copy-start.6
  35.9 0.1 pad_add_fusion.refs_0_
  36.0 0.0 collective-permute-done.2.refs_7_
  36.0 7.6 %collective-permute-done.3.refs_8_ = bf16[55,4,256]{2,1,0:T(4,128)(2,1)S(1)} collective-permute-done((bf16[55,4,256]{2,1,0:T(4,128)(2,1)}, bf16[55,4,256]{2,1,0:T(4,128)(2,1)S(1)}, u32[]{:S(2)}, u32[]{:S(2)}) %collective-permute-start.3) | collective-permute-done | bytes 112672 | tf_op jit(solution)/shard_map/ppermute | solution.py:277
  43.6 0.9 %copy-done.2 = bf16[36,4,256]{2,1,0:T(4,128)(2,1)S(1)} copy-done((bf16[36,4,256]{2,1,0:T(4,128)(2,1)S(1)}, bf16[36,4,256]{2,1,0:T(4,128)(2,1)}, u32[]{:S(2)}) %copy-start.2) | copy-done | bytes 73752
  44.5 0.9 %copy-done.4 = bf16[36,4,256]{2,1,0:T(4,128)(2,1)S(1)} copy-done((bf16[36,4,256]{2,1,0:T(4,128)(2,1)S(1)}, bf16[36,4,256]{2,1,0:T(4,128)(2,1)}, u32[]{:S(2)}) %copy-start.4) | copy-done | bytes 73752
  45.4 5.3 %shard_map.57 = f32[128,4,256]{2,1,0:T(4,128)} custom-call(s32[4]{0:T(128)S(1)} %pad_add_fusion.refs_0_, bf16[128,4,256]{2,1,0:T(4,128)(2,1)S(1)} %bitcast.30, f32[3,128]{1,0:T(4,128)S(1)} %copy-done.6, f32[128,3]{1,0:T(8,128)S(1)} %bitcast.32, f32[6,256]{1,0:T(8,128)S(1)} %copy-done.5, bf16[36,4,256]{2,1,0:T(4,128)(2,1)S(1)} %copy-done.2, ...), custom_call_target="tpu_custom_call" | custom-call | tf_op jit(solution)/shard_map/pallas_call | solution.py:325
  (14 shorter events, 0.1 us)
Async XLA Ops:
  0.0 0.7 %copy-start.8 = (s32[1,1,2,512]{3,2,1,0:T(2,128)S(1)}, s32[1,1,2,512]{3,2,1,0:T(2,128)}, u32[]{:S(2)}) copy-start(s32[1,1,2,512]{3,2,1,0:T(2,128)} %param.8) | copy-start | bytes 12292
  0.0 0.7 %copy-start.9 = (s32[1,1,512]{2,1,0:T(1,128)S(1)}, s32[1,1,512]{2,1,0:T(1,128)}, u32[]{:S(2)}) copy-start(s32[1,1,512]{2,1,0:T(1,128)} %param.9) | copy-start | bytes 6148
  0.7 0.7 %copy-start.7 = (f32[3,4,4,8]{3,2,1,0:T(4,128)S(1)}, f32[3,4,4,8]{3,2,1,0:T(4,128)}, u32[]{:S(2)}) copy-start(f32[3,4,4,8]{3,2,1,0:T(4,128)} %param.7) | copy-start | bytes 4612
  4.0 39.6 %copy-start = (bf16[4,4,8,4,256]{4,3,2,1,0:T(4,128)(2,1)S(1)}, bf16[4,4,8,4,256]{4,3,2,1,0:T(4,128)(2,1)}, u32[]{:S(2)}) copy-start(bf16[4,4,8,4,256]{4,3,2,1,0:T(4,128)(2,1)} %param.6) | copy-start | bytes 786436
  4.0 20.0 %collective-permute-start = (bf16[36,4,256]{2,1,0:T(4,128)(2,1)}, bf16[36,4,256]{2,1,0:T(4,128)(2,1)S(1)}, u32[]{:S(2)}, u32[]{:S(2)}) collective-permute-start(bf16[36,4,256]{2,1,0:T(4,128)(2,1)} %get-tuple-element.9), channel_id=1, source_target_pairs={{0,1},{1,2},{2,3},{3,4},{4,5},{5,6},{6,7},{7,8},{8,9},{9,10},{10,1... | collective-permute-start | bytes 221192 | tf_op jit(solution)/shard_map/ppermute | solution.py:276
  8.1 17.6 %collective-permute-start.1 = (bf16[36,4,256]{2,1,0:T(4,128)(2,1)}, bf16[36,4,256]{2,1,0:T(4,128)(2,1)S(1)}, u32[]{:S(2)}, u32[]{:S(2)}) collective-permute-start(bf16[36,4,256]{2,1,0:T(4,128)(2,1)} %get-tuple-element.10), channel_id=1, source_target_pairs={{0,15},{1,0},{2,1},{3,2},{4,3},{5,4},{6,5},{7,6},{8,7},{9,8},{10,9... | collective-permute-start | bytes 221192 | tf_op jit(solution)/shard_map/ppermute | solution.py:277
  24.0 1.7 %copy-start.1 = (bf16[36,4,256]{2,1,0:T(4,128)(2,1)}, bf16[36,4,256]{2,1,0:T(4,128)(2,1)S(1)}, u32[]{:S(2)}) copy-start(bf16[36,4,256]{2,1,0:T(4,128)(2,1)S(1)} %collective-permute-done.from_low.refs_5_) | copy-start | bytes 221188
  25.7 0.6 %copy-start.3 = (bf16[36,4,256]{2,1,0:T(4,128)(2,1)}, bf16[36,4,256]{2,1,0:T(4,128)(2,1)S(1)}, u32[]{:S(2)}) copy-start(bf16[36,4,256]{2,1,0:T(4,128)(2,1)S(1)} %collective-permute-done.1.from_high.refs_6_) | copy-start | bytes 221188
  28.1 15.5 %copy-start.5 = (f32[6,256]{1,0:T(8,128)S(1)}, f32[6,256]{1,0:T(8,128)}, u32[]{:S(2)}) copy-start(f32[6,256]{1,0:T(8,128)} %convert_element_type.8.lists.refs_4_) | copy-start | bytes 18436
  28.1 7.9 %collective-permute-start.2 = (bf16[55,4,256]{2,1,0:T(4,128)(2,1)}, bf16[55,4,256]{2,1,0:T(4,128)(2,1)S(1)}, u32[]{:S(2)}, u32[]{:S(2)}) collective-permute-start(bf16[55,4,256]{2,1,0:T(4,128)(2,1)} %get-tuple-element.11), channel_id=1, source_target_pairs={{0,16},{16,32},{32,48},{48,64},{64,80},{80,96},{96,112},{112,128},... | collective-permute-start | bytes 337928 | tf_op jit(solution)/shard_map/ppermute | solution.py:276
  34.0 9.6 %collective-permute-start.3 = (bf16[55,4,256]{2,1,0:T(4,128)(2,1)}, bf16[55,4,256]{2,1,0:T(4,128)(2,1)S(1)}, u32[]{:S(2)}, u32[]{:S(2)}) collective-permute-start(bf16[55,4,256]{2,1,0:T(4,128)(2,1)} %get-tuple-element.12), channel_id=1, source_target_pairs={{0,1008},{16,0},{32,16},{48,32},{64,48},{80,64},{96,80},{112,96},{... | collective-permute-start | bytes 337928 | tf_op jit(solution)/shard_map/ppermute | solution.py:277
  35.9 7.7 %copy-start.6 = (f32[3,128]{1,0:T(4,128)S(1)}, f32[3,128]{1,0:T(4,128)}, u32[]{:S(2)}) copy-start(f32[3,128]{1,0:T(4,128)} %copy.9.pos.refs_2_) | copy-start | bytes 4612
  43.6 0.9 %copy-start.2 = (bf16[36,4,256]{2,1,0:T(4,128)(2,1)S(1)}, bf16[36,4,256]{2,1,0:T(4,128)(2,1)}, u32[]{:S(2)}) copy-start(bf16[36,4,256]{2,1,0:T(4,128)(2,1)} %copy-done.1) | copy-start | bytes 221188
  44.5 0.9 %copy-start.4 = (bf16[36,4,256]{2,1,0:T(4,128)(2,1)S(1)}, bf16[36,4,256]{2,1,0:T(4,128)(2,1)}, u32[]{:S(2)}) copy-start(bf16[36,4,256]{2,1,0:T(4,128)(2,1)} %copy-done.3) | copy-start | bytes 221188

commit v2 on v1

v2 whole, which is shorter than its diff:
```python
import jax
import jax.numpy as jnp
from jax import lax
from jax.experimental import pallas as pl
from jax.experimental.pallas import tpu as pltpu
from jax.sharding import PartitionSpec as P

ONSITE_S = -0.22
ONSITE_P = 0.27
HOP_SS = -0.37
HOP_SP = 0.35
HOP_PPS = 0.4
HOP_PPP = -0.114
BOND_LENGTH = 1.536
LATTICE_STEP = 1.6

SIDE = 4
DEPTH = 8
ATOMS = SIDE * SIDE * DEPTH
FACE = SIDE * DEPTH
WIDE = FACE + 2 * DEPTH
NV = 256
POS_ROWS = 9
LIST_ROWS = 6
AUX = 4
Y_SITES = FACE + AUX
X_SITES = WIDE + 3 * AUX
STEPS = [(x, y) for x in (-1, 0, 1) for y in (-1, 0, 1)]
F32 = jnp.float32
BF16 = jnp.bfloat16


def iota(shape, axis):
    return lax.broadcasted_iota(jnp.int32, shape, axis)


def onehot(values, expected):
    wide = [jnp.where(row == expected, 1.0, 0.0).astype(BF16) for row in values]
    return wide[0] if len(wide) == 1 else jnp.concatenate(wide, axis=1)


def dot_nt(a, b):
    return lax.dot_general(a, b, (((1,), (1,)), ((), ())), preferred_element_type=F32)


def dot(a, b):
    return jnp.dot(a, b, preferred_element_type=F32)


def list_of(rows):
    first = [rows[k : k + 1] for k in range(2)]
    key = [rows[4 + k : 5 + k] * float(ATOMS) + rows[2 + k : 3 + k] for k in range(2)]
    return first, key


def code(step_x, step_y):
    return (step_x + 1) * 3 + step_y + 1


def hopping(dx, dy, dz, count):
    square = jnp.maximum(dx * dx + dy * dy + dz * dz, 0.5)
    inverse = lax.rsqrt(square)
    cosines = [d * inverse for d in (dx, dy, dz)]
    ratio = BOND_LENGTH * inverse
    radial = ratio * ratio * jnp.exp(1.0 - square * inverse * (1.0 / BOND_LENGTH))

    def final(value):
        return (value.astype(BF16).astype(F32) * count).astype(BF16)

    grid = [[None] * 4 for _ in range(4)]
    grid[0][0] = final(HOP_SS * radial)
    for a in range(3):
        across = final(HOP_SP * radial * cosines[a])
        grid[0][1 + a] = across
        grid[1 + a][0] = -across
        for b in range(a, 3):
            entry = (HOP_PPS - HOP_PPP) * cosines[a] * cosines[b]
            if a == b:
                entry = entry + HOP_PPP
            grid[1 + a][1 + b] = grid[1 + b][1 + a] = final(entry * radial)
    return grid


def interleave(grid, rows, columns):
    total = None
    for b in range(4):
        stacked = jnp.concatenate([grid[a][b] for a in range(4)], axis=0)
        at = (iota((columns, 4 * columns), 1) == 4 * iota((columns, 4 * columns), 0) + b)
        part = dot(stacked, jnp.where(at, 1.0, 0.0).astype(BF16))
        total = part if total is None else total + part
    target = iota((4 * rows, 4 * rows), 0)
    source = (target & 3) * rows + (target >> 2)
    turn = jnp.where(iota((4 * rows, 4 * rows), 1) == source, 1.0, 0.0).astype(BF16)
    return dot(turn, total.astype(BF16)).astype(BF16)


def joined(block):
    n = block.shape[0]
    wide = block.astype(F32).reshape(n // 2, 2, 4, NV)
    return jnp.concatenate([wide[:, 0], wide[:, 1]], axis=1).reshape(4 * n, NV)


def turned(points):
    n = points.shape[1]
    return jnp.concatenate([points, jnp.zeros((5, n), F32)], axis=0).T


def picked_rows(pick, points):
    total = None
    for _ in range(3):
        piece = points.astype(BF16)
        part = dot(pick, piece)
        total = part if total is None else total + part
        points = points - piece.astype(F32)
    return total


def z_shift(zi, zj):
    step = zj - zi
    period = LATTICE_STEP * DEPTH
    return jnp.where(step > 1.5, -period, jnp.where(step < -1.5, period, 0.0))


def wrap(place, across, side, period):
    high = jnp.where((side > 0) & (place == across - 1), period, 0.0)
    return jnp.where((side < 0) & (place == 0), -period, high)


def side_of(place):
    first = 1 - 2 * (place & 1)
    return first, -first


def faces_of(side):
    mine = jnp.where(side > 0, SIDE - 1, 0)
    return mine, SIDE - 1 - mine


def aux_of(message, first):
    return jnp.concatenate([message[first + k].astype(F32) for k in range(AUX)], axis=0)


def points_of(rows):
    return rows[0:3] + rows[3:6] + rows[6:9]


def pack_y(places, count, trial, positions, atoms, owner, one, two, aux):
    at_x, at_y, across_x, across_y = (places[k] for k in range(4))
    rest = positions[...]
    parts = []
    for _ in range(3):
        piece = rest.astype(BF16)
        parts.append(piece)
        rest = rest - piece.astype(F32)
    rows = 3 * SIDE * SIDE
    tile = (iota((DEPTH, ATOMS), 1) & (DEPTH - 1)) == iota((DEPTH, ATOMS), 0)
    spread = dot(jnp.concatenate(parts, axis=0), jnp.where(tile, 1.0, 0.0).astype(BF16))
    row = iota((3 * rows, ATOMS), 0)
    keep = (row & (SIDE * SIDE - 1)) == (iota((3 * rows, ATOMS), 1) >> 3)
    spread = jnp.where(keep, spread, 0.0).astype(BF16)
    gather = (iota((16, 3 * rows), 1) >> 4) == iota((16, 3 * rows), 0)
    aux[:, :ATOMS] = dot(jnp.where(gather, 1.0, 0.0).astype(BF16), spread)
    aux[:, ATOMS:] = jnp.zeros((4 * AUX, NV - ATOMS), F32)
    owners = owner[...]
    step = jnp.zeros(owners.shape, F32)
    for x, y in STEPS:
        whose = lax.rem(at_x + x + across_x, across_x) * across_y
        whose = whose + lax.rem(at_y + y + across_y, across_y)
        step = jnp.where(owners == whose, float(code(x, y)), step)
    live = iota(owners.shape, 1) < count[0, 0]
    first = jnp.where(live, atoms[0:1], -1).astype(F32)
    second = atoms[1:2].astype(F32)
    for k, values in enumerate((first, second, step)):
        for h in range(2):
            at = POS_ROWS + 2 * k + h
            aux[at : at + 1] = values[:, h * NV : (h + 1) * NV]
    sites = [aux[4 * k : 4 * k + 4].astype(BF16) for k in range(AUX)]
    for side, out in zip(side_of(at_y), (one, two)):
        face, _ = faces_of(side)
        for x in range(SIDE):
            begin = (x * SIDE + face) * DEPTH
            out[x * DEPTH : (x + 1) * DEPTH] = trial[pl.ds(begin, DEPTH)]
        for k in range(AUX):
            out[FACE + k] = sites[k]


def own(places, trial, message, acc, one, two):
    rows = aux_of(message, FACE)
    first, key = list_of(rows[POS_ROWS : POS_ROWS + LIST_ROWS])
    wave = joined(trial[...])
    atom = iota((ATOMS, 1), 0)
    is_first = onehot(first, atom.astype(F32))
    is_second = onehot(key, (atom + code(0, 0) * ATOMS).astype(F32))
    count = dot_nt(is_first, is_second) + dot_nt(is_second, is_first)
    pos = points_of(rows)[:, :ATOMS]
    pos_t = turned(pos)
    zi = (atom & (DEPTH - 1)).astype(F32)
    zj = (iota((1, ATOMS), 1) & (DEPTH - 1)).astype(F32)
    dx, dy = (pos[a : a + 1] - pos_t[:, a : a + 1] for a in range(2))
    dz = (pos[2:3] + z_shift(zi, zj)) - pos_t[:, 2:3]
    matrix = interleave(hopping(dx, dy, dz, count), ATOMS, ATOMS)
    orbital = iota((4 * ATOMS, 1), 0) & 3
    onsite = jnp.where(orbital == 0, ONSITE_S, ONSITE_P)
    acc[...] = onsite * wave + dot(matrix, wave.astype(BF16))
    for side, out in zip(side_of(places[0]), (one, two)):
        face, _ = faces_of(side)
        out[:FACE] = trial[pl.ds(face * FACE, FACE)]
        out[FACE:WIDE] = jnp.zeros((2 * DEPTH, 4, NV), BF16)
        for k in range(AUX):
            out[WIDE + k] = message[FACE + k]
        out[WIDE + AUX :] = jnp.zeros((2 * AUX, 4, NV), BF16)


def corners(places, y_one, y_two, one_in, two_in, one, two):
    for side, before, out in zip(side_of(places[0]), (one_in, two_in), (one, two)):
        face, _ = faces_of(side)
        out[:FACE] = before[:FACE]
        out[WIDE : WIDE + AUX] = before[WIDE : WIDE + AUX]
        for n, message in enumerate((y_one, y_two)):
            at = FACE + n * DEPTH
            out[at : at + DEPTH] = message[pl.ds(face * DEPTH, DEPTH)]
            at = WIDE + (n + 1) * AUX
            out[at : at + AUX] = message[FACE:]


def y_faces(periods, places, message, y_one, y_two, acc_in, acc):
    acc[...] = acc_in[...]
    rows = aux_of(message, FACE)
    own_first, own_key = list_of(rows[POS_ROWS : POS_ROWS + LIST_ROWS])
    pos_t = turned(points_of(rows)[:, :ATOMS])
    k = iota((FACE, 1), 0)
    line = (k >> 3) * (SIDE * DEPTH) + (k & (DEPTH - 1))
    zi = (k & (DEPTH - 1)).astype(F32)
    zj = (iota((1, FACE), 1) & (DEPTH - 1)).astype(F32)
    for side, other in zip(side_of(places[1]), (y_one, y_two)):
        mine, theirs = faces_of(side)
        rows = aux_of(other, FACE)
        first, key = list_of(rows[POS_ROWS : POS_ROWS + LIST_ROWS])
        my_atom = line + mine * DEPTH
        their_atom = line + theirs * DEPTH
        left = [
            onehot(own_first, my_atom.astype(F32)),
            onehot(key, (my_atom + (4 - side) * ATOMS).astype(F32)),
        ]
        right = [
            onehot(own_key, (their_atom + (4 + side) * ATOMS).astype(F32)),
            onehot(first, their_atom.astype(F32)),
        ]
        count = dot_nt(jnp.concatenate(left, axis=1), jnp.concatenate(right, axis=1))
        lane = iota((ATOMS, FACE), 1)
        lane = (lane >> 3) * (SIDE * DEPTH) + (lane & (DEPTH - 1)) + theirs * DEPTH
        pick = jnp.where(iota((ATOMS, FACE), 0) == lane, 1.0, 0.0).astype(BF16)
        points = points_of(dot(rows[:, :ATOMS].astype(BF16), pick))
        pick = jnp.where(iota((FACE, ATOMS), 1) == my_atom, 1.0, 0.0).astype(BF16)
        mine_t = picked_rows(pick, pos_t)
        dx = points[0:1] - mine_t[:, 0:1]
        dy = (points[1:2] + wrap(places[1], places[3], side, periods[1])) - mine_t[:, 1:2]
        dz = (points[2:3] + z_shift(zi, zj)) - mine_t[:, 2:3]
        matrix = interleave(hopping(dx, dy, dz, count), FACE, FACE)
        part = dot(matrix, joined(other[:FACE]).astype(BF16))
        for x in range(SIDE):
            at = pl.ds(pl.multiple_of((x * SIDE + mine) * DEPTH * 4, DEPTH * 4), 4 * DEPTH)
            acc[at] += part[x * 4 * DEPTH : (x + 1) * 4 * DEPTH]


def x_faces(periods, places, message, x_one, x_two, acc, out, total):
    total[...] = acc[...]
    rows = aux_of(message, FACE)
    own_first, own_key = list_of(rows[POS_ROWS : POS_ROWS + LIST_ROWS])
    pos_t = turned(points_of(rows)[:, :ATOMS])
    k = iota((FACE, 1), 0)
    zi = (k & (DEPTH - 1)).astype(F32)
    y_sides = side_of(places[1])
    for side, other in zip(side_of(places[0]), (x_one, x_two)):
        mine, theirs = faces_of(side)
        my_atom = k + mine * FACE

        def ghost(shape, axis):
            at = iota(shape, axis)
            part = jnp.where(at < FACE, 0, jnp.where(at < FACE + DEPTH, 1, 2))
            step = jnp.where(part == 0, 0, jnp.where(part == 1, y_sides[0], y_sides[1]))
            row = jnp.where(step > 0, 0, (SIDE - 1) * DEPTH)
            atom = theirs * FACE + jnp.where(part == 0, at, row + (at & (DEPTH - 1)))
            return atom, step, part

        their_atom, step, part = ghost((WIDE, 1), 0)
        target = their_atom + ((side + 1) * 3 + step + 1) * ATOMS
        left = [onehot(own_first, my_atom.astype(F32))]
        right = [onehot(own_key, target.astype(F32))]
        points = None
        lane_atom, _, lane_part = ghost((ATOMS, WIDE), 1)
        for n, y in enumerate((0, *y_sides)):
            rows = aux_of(other, WIDE + n * AUX)
            first, key = list_of(rows[POS_ROWS : POS_ROWS + LIST_ROWS])
            wanted = my_atom + ((1 - side) * 3 + 1 - y) * ATOMS
            left.append(onehot(key, wanted.astype(F32)))
            right.append(onehot(first, jnp.where(part == n, their_atom, -2).astype(F32)))
            pick = jnp.where(
                (iota((ATOMS, WIDE), 0) == lane_atom) & (lane_part == n), 1.0, 0.0
            ).astype(BF16)
            placed = dot(rows[:, :ATOMS].astype(BF16), pick)
            points = placed if points is None else points + placed
        count = dot_nt(jnp.concatenate(left, axis=1), jnp.concatenate(right, axis=1))
        points = points_of(points)
        lane = iota((1, WIDE), 1)
        zj = (lane & (DEPTH - 1)).astype(F32)
        shifts = [wrap(places[1], places[3], y, periods[1]) for y in y_sides]
        shift_y = jnp.where(lane < FACE, 0.0, jnp.where(lane < FACE + DEPTH, *shifts))
        mine_t = picked_rows(
            jnp.where(iota((FACE, ATOMS), 1) == my_atom, 1.0, 0.0).astype(BF16), pos_t
        )
        dx = (points[0:1] + wrap(places[0], places[2], side, periods[0])) - mine_t[:, 0:1]
        dy = (points[1:2] + shift_y) - mine_t[:, 1:2]
        dz = (points[2:3] + z_shift(zi, zj)) - mine_t[:, 2:3]
        matrix = interleave(hopping(dx, dy, dz, count), FACE, WIDE)
        added = dot(matrix, joined(other[:WIDE]).astype(BF16))
        at = pl.ds(pl.multiple_of(mine * 4 * FACE, 4 * FACE), 4 * FACE)
        total[at] += added
    wide = total[...].reshape(ATOMS // 2, 8, NV)
    out[...] = jnp.stack([wide[:, :4], wide[:, 4:]], axis=1).reshape(ATOMS, 4, NV)


def swap(count, begin):
    pairs = []
    for i in range(begin, count + begin, 2):
        a, b = i % count, (i + 1) % count
        pairs += [(a, b), (b, a)]
    return pairs


def exchange(one, two, axis):
    count = lax.axis_size(axis)
    one = lax.ppermute(one, axis, swap(count, 0))
    two = lax.ppermute(two, axis, swap(count, 1))
    return one, two


def call(kernel, inputs, outputs, specs, **options):
    vmem = pl.BlockSpec(memory_space=pltpu.VMEM)
    return pl.pallas_call(
        kernel,
        out_shape=outputs,
        in_specs=specs + [vmem] * (len(inputs) - len(specs)),
        out_specs=[vmem] * len(outputs),
        compiler_params=pltpu.CompilerParams(vmem_limit_bytes=16 * 1024 * 1024),
        **options,
    )(*inputs)


def shards(trial, positions, pair_atoms, pair_owner, pair_image, pair_count):
    across_x = lax.axis_size("gx")
    across_y = lax.axis_size("gy")
    periods = (LATTICE_STEP * (SIDE * across_x), LATTICE_STEP * (SIDE * across_y))
    smem = pl.BlockSpec(memory_space=pltpu.SMEM)
    mine = trial.reshape(ATOMS, 4, NV)
    places = jnp.stack(
        [lax.axis_index("gx"), lax.axis_index("gy"), jnp.int32(across_x), jnp.int32(across_y)]
    ).astype(jnp.int32)

    def message(sites):
        return jax.ShapeDtypeStruct((sites, 4, NV), BF16)

    y_out = call(
        pack_y,
        (
            places,
            pair_count,
            mine,
            positions.reshape(3 * SIDE * SIDE, DEPTH),
            pair_atoms.reshape(2, -1),
            pair_owner.reshape(1, -1),
        ),
        [message(Y_SITES)] * 2,
        [smem] * 2,
        scratch_shapes=[pltpu.VMEM((4 * AUX, NV), F32)],
    )
    y_in = exchange(*y_out, "gy")
    rows = jax.ShapeDtypeStruct((4 * ATOMS, NV), F32)
    acc, *x_out = call(own, (places, mine, y_out[0]), [rows] + [message(X_SITES)] * 2, [smem])
    x_out = call(
        corners,
        (places, *y_in, *x_out),
        [message(X_SITES)] * 2,
        [smem],
        input_output_aliases={3: 0, 4: 1},
    )
    x_in = exchange(*x_out, "gx")
    (acc,) = call(
        lambda *refs: y_faces(periods, *refs),
        (places, y_out[0], *y_in, acc),
        [rows],
        [smem],
        input_output_aliases={4: 0},
    )
    (product,) = call(
        lambda *refs: x_faces(periods, *refs),
        (places, y_out[0], *x_in, acc),
        [jax.ShapeDtypeStruct((ATOMS, 4, NV), F32)],
        [smem],
        scratch_shapes=[pltpu.VMEM((4 * ATOMS, NV), F32)],
    )
    return product.reshape(trial.shape)


def solution(mesh):
    in_specs = (
        P("gx", "gy", None, None, None),
        P(None, "gx", "gy", None),
        P("gx", "gy", None, None),
        P("gx", "gy", None),
        P("gx", "gy", None, None),
        P("gx", "gy"),
    )
    out_specs = P("gx", "gy", None, None, None)
    return jax.shard_map(shards, mesh=mesh, in_specs=in_specs, out_specs=out_specs, check_vma=False)
```

time: 51.2 us -> 43.4 us (0.85)
  the two profiles are of different devices: /device:TPU:31 before, /device:TPU:63 now
where the time goes in v2:
time: 43.4 us; the launch traced here: 43 us
  starting transfers between devices  25.2 us (58%)
  Pallas kernels  9.02 us (21%)
  waiting for transfers between devices  5.67 us (13%)
  local copies, waits for them, and re-layouts  2.32 us (5%)
  between operations  0.75 us (2%)
    ppermute x2, starting transfers between devices, exchange(): two = lax.ppermute(two, axis, swap(count, 1))  18 us
    pallas_call x5, Pallas kernels, call(): pl.pallas_call(kernel, out_shape=outputs, in_specs=specs + [vmem] * (len(...  9.02 us
    ppermute x2, starting transfers between devices, exchange(): one = lax.ppermute(one, axis, swap(count, 0))  7.15 us
    ppermute x2, waiting for transfers between devices, exchange(): two = lax.ppermute(two, axis, swap(count, 1))  5.66 us
    unnamed x8, local copies, waits for them, and re-layouts  2.32 us
  transfers between devices with their start and end apart: 4, of which 1 were waited for; matrix products, arithmetic and copies ran while one was open for 0% of the time, Pallas kernels for 11%

profile of v2, /device:TPU:63, one launch (start us, length us, event | category | flops | bytes accessed | tf_op | source)
XLA Modules:
  0.0 43.0 jit_solution(6922763497250430092)
XLA Ops:
  0.0 0.0 copy-start.1
  0.7 0.1 pad_add_fusion.places.refs_0_
  0.7 0.0 copy-start.3
  0.7 0.0 copy-done.1
  0.8 0.7 %copy-done.3 = s32[1,1,512]{2,1,0:T(1,128)S(1)} copy-done((s32[1,1,512]{2,1,0:T(1,128)S(1)}, s32[1,1,512]{2,1,0:T(1,128)}, u32[]{:S(2)}) %copy-start.3) | copy-done | bytes 2072
  1.4 0.0 copy-start
  1.4 0.9 %copy-done = bf16[4,4,8,4,256]{4,3,2,1,0:T(4,128)(2,1)S(1)} copy-done((bf16[4,4,8,4,256]{4,3,2,1,0:T(4,128)(2,1)S(1)}, bf16[4,4,8,4,256]{4,3,2,1,0:T(4,128)(2,1)}, u32[]{:S(2)}) %copy-start) | copy-done | bytes 262168
  2.4 0.0 copy-start.2
  2.4 0.7 %copy-done.2 = s32[1,1,2,512]{3,2,1,0:T(2,128)S(1)} copy-done((s32[1,1,2,512]{3,2,1,0:T(2,128)S(1)}, s32[1,1,2,512]{3,2,1,0:T(2,128)}, u32[]{:S(2)}) %copy-start.2) | copy-done | bytes 4120
  3.1 0.8 %shard_map.55 = (bf16[36,4,256]{2,1,0:T(4,128)(2,1)S(1)}, bf16[36,4,256]{2,1,0:T(4,128)(2,1)S(1)}) custom-call(s32[4]{0:T(128)S(1)} %pad_add_fusion.places.refs_0_, s32[1,1]{1,0:T(1,128)S(6)} %copy.12.count, bf16[128,4,256]{2,1,0:T(4,128)(2,1)S(1)} %bitcast.7, f32[48,8]{1,0:T(8,128)S(1)} %bitcast.9, s32[2,512]{1,0:T(2,128)S(1)} %bitcast.10, ...), custom_call_target="tpu_custom_call" | custom-call | tf_op jit(solution)/shard_map/pallas_call | solution.py:340
  3.9 4.0 %collective-permute-start = (bf16[36,4,256]{2,1,0:T(4,128)(2,1)S(1)}, bf16[36,4,256]{2,1,0:T(4,128)(2,1)S(1)}, u32[]{:S(2)}, u32[]{:S(2)}) collective-permute-start(bf16[36,4,256]{2,1,0:T(4,128)(2,1)S(1)} %get-tuple-element.12.message.refs_1_), channel_id=1, source_target_pairs={{0,1},{1,0},{2,3},{3,2},{4,5},{5,4},{6,7},{7,6},{8,9},{9,8},{10,11... | collective-permute-start | bytes 221192 | tf_op jit(solution)/shard_map/ppermute | solution.py:333
  7.9 16.1 %collective-permute-start.1 = (bf16[36,4,256]{2,1,0:T(4,128)(2,1)S(1)}, bf16[36,4,256]{2,1,0:T(4,128)(2,1)S(1)}, u32[]{:S(2)}, u32[]{:S(2)}) collective-permute-start(bf16[36,4,256]{2,1,0:T(4,128)(2,1)S(1)} %get-tuple-element.13), channel_id=1, source_target_pairs={{1,2},{2,1},{3,4},{4,3},{5,6},{6,5},{7,8},{8,7},{9,10},{10,9},{11,... | collective-permute-start | bytes 221192 | tf_op jit(solution)/shard_map/ppermute | solution.py:334
  24.0 2.8 %shard_map.56 = (f32[512,256]{1,0:T(8,128)S(1)}, bf16[60,4,256]{2,1,0:T(4,128)(2,1)S(1)}, bf16[60,4,256]{2,1,0:T(4,128)(2,1)S(1)}) custom-call(s32[4]{0:T(128)S(1)} %pad_add_fusion.places.refs_0_, bf16[128,4,256]{2,1,0:T(4,128)(2,1)S(1)} %bitcast.8, bf16[36,4,256]{2,1,0:T(4,128)(2,1)S(1)} %get-tuple-element.12.message.refs_1_), custom_call_target="tpu_custom_call" | custom-call | tf_op jit(solution)/shard_map/pallas_call | solution.py:340
  26.8 0.0 collective-permute-done.y_one.refs_2_
  26.8 0.0 collective-permute-done.1.y_two.refs_3_
  26.8 0.6 %shard_map.57 = (bf16[60,4,256]{2,1,0:T(4,128)(2,1)S(1)}, bf16[60,4,256]{2,1,0:T(4,128)(2,1)S(1)}) custom-call(s32[4]{0:T(128)S(1)} %pad_add_fusion.places.refs_0_, bf16[36,4,256]{2,1,0:T(4,128)(2,1)S(1)} %collective-permute-done.y_one.refs_2_, ...), custom_call_target="tpu_custom_call", output_to_operand_aliasing={{0}: (3, {}), {1}: (4, {})} | custom-call | tf_op jit(solution)/shard_map/pallas_call | solution.py:340
  27.4 3.1 %collective-permute-start.2 = (bf16[60,4,256]{2,1,0:T(4,128)(2,1)S(1)}, bf16[60,4,256]{2,1,0:T(4,128)(2,1)S(1)}, u32[]{:S(2)}, u32[]{:S(2)}) collective-permute-start(bf16[60,4,256]{2,1,0:T(4,128)(2,1)S(1)} %get-tuple-element.16), channel_id=1, source_target_pairs={{0,16},{16,0},{32,48},{48,32},{64,80},{80,64},{96,112},{112,96},{1... | collective-permute-start | bytes 368648 | tf_op jit(solution)/shard_map/ppermute | solution.py:333
  30.6 1.9 %collective-permute-start.3 = (bf16[60,4,256]{2,1,0:T(4,128)(2,1)S(1)}, bf16[60,4,256]{2,1,0:T(4,128)(2,1)S(1)}, u32[]{:S(2)}, u32[]{:S(2)}) collective-permute-start(bf16[60,4,256]{2,1,0:T(4,128)(2,1)S(1)} %get-tuple-element.17), channel_id=1, source_target_pairs={{16,32},{32,16},{48,64},{64,48},{80,96},{96,80},{112,128},{128,112... | collective-permute-start | bytes 368648 | tf_op jit(solution)/shard_map/ppermute | solution.py:334
  32.5 1.9 %shard_map.58.refs_4_ = f32[512,256]{1,0:T(8,128)S(1)} custom-call(s32[4]{0:T(128)S(1)} %pad_add_fusion.places.refs_0_, bf16[36,4,256]{2,1,0:T(4,128)(2,1)S(1)} %get-tuple-element.12.message.refs_1_, bf16[36,4,256]{2,1,0:T(4,128)(2,1)S(1)} %collective-permute-done.y_one.refs_2_, ...), custom_call_target="tpu_custom_call", output_to_operand_aliasing={{}: (4, {})} | custom-call | tf_op jit(solution)/shard_map/pallas_call | solution.py:340
  34.4 0.0 collective-permute-done.2.refs_2_
  34.4 5.7 %collective-permute-done.3.refs_3_ = bf16[60,4,256]{2,1,0:T(4,128)(2,1)S(1)} collective-permute-done((bf16[60,4,256]{2,1,0:T(4,128)(2,1)S(1)}, bf16[60,4,256]{2,1,0:T(4,128)(2,1)S(1)}, u32[]{:S(2)}, u32[]{:S(2)}) %collective-permute-start.3) | collective-permute-done | bytes 122912 | tf_op jit(solution)/shard_map/ppermute | solution.py:334
  40.1 2.9 %shard_map.59 = f32[128,4,256]{2,1,0:T(4,128)} custom-call(s32[4]{0:T(128)S(1)} %pad_add_fusion.places.refs_0_, bf16[36,4,256]{2,1,0:T(4,128)(2,1)S(1)} %get-tuple-element.12.message.refs_1_, bf16[60,4,256]{2,1,0:T(4,128)(2,1)S(1)} %collective-permute-done.2.refs_2_, bf16[60,4,256]{2,1,0:T(4,128)(2,1)S(1)} %collective-permute-done.3.refs_3_, ...), custom_call_target="tpu_custom_call" | custom-call | tf_op jit(solution)/shard_map/pallas_call | solution.py:340
Async XLA Ops:
  0.0 0.8 %copy-start.1 = (f32[3,4,4,8]{3,2,1,0:T(4,128)S(1)}, f32[3,4,4,8]{3,2,1,0:T(4,128)}, u32[]{:S(2)}) copy-start(f32[3,4,4,8]{3,2,1,0:T(4,128)} %param.7) | copy-start | bytes 4612
  0.7 0.7 %copy-start.3 = (s32[1,1,512]{2,1,0:T(1,128)S(1)}, s32[1,1,512]{2,1,0:T(1,128)}, u32[]{:S(2)}) copy-start(s32[1,1,512]{2,1,0:T(1,128)} %param.9) | copy-start | bytes 6148
  1.4 0.9 %copy-start = (bf16[4,4,8,4,256]{4,3,2,1,0:T(4,128)(2,1)S(1)}, bf16[4,4,8,4,256]{4,3,2,1,0:T(4,128)(2,1)}, u32[]{:S(2)}) copy-start(bf16[4,4,8,4,256]{4,3,2,1,0:T(4,128)(2,1)} %param.6) | copy-start | bytes 786436
  2.4 0.7 %copy-start.2 = (s32[1,1,2,512]{3,2,1,0:T(2,128)S(1)}, s32[1,1,2,512]{3,2,1,0:T(2,128)}, u32[]{:S(2)}) copy-start(s32[1,1,2,512]{3,2,1,0:T(2,128)} %param.8) | copy-start | bytes 12292
  3.9 22.9 %collective-permute-start = (bf16[36,4,256]{2,1,0:T(4,128)(2,1)S(1)}, bf16[36,4,256]{2,1,0:T(4,128)(2,1)S(1)}, u32[]{:S(2)}, u32[]{:S(2)}) collective-permute-start(bf16[36,4,256]{2,1,0:T(4,128)(2,1)S(1)} %get-tuple-element.12.message.refs_1_), channel_id=1, source_target_pairs={{0,1},{1,0},{2,3},{3,2},{4,5},{5,4},{6,7},{7,6},{8,9},{9,8},{10,11... | collective-permute-start | bytes 221192 | tf_op jit(solution)/shard_map/ppermute | solution.py:333
  7.9 18.9 %collective-permute-start.1 = (bf16[36,4,256]{2,1,0:T(4,128)(2,1)S(1)}, bf16[36,4,256]{2,1,0:T(4,128)(2,1)S(1)}, u32[]{:S(2)}, u32[]{:S(2)}) collective-permute-start(bf16[36,4,256]{2,1,0:T(4,128)(2,1)S(1)} %get-tuple-element.13), channel_id=1, source_target_pairs={{1,2},{2,1},{3,4},{4,3},{5,6},{6,5},{7,8},{8,7},{9,10},{10,9},{11,... | collective-permute-start | bytes 221192 | tf_op jit(solution)/shard_map/ppermute | solution.py:334
  27.4 7.0 %collective-permute-start.2 = (bf16[60,4,256]{2,1,0:T(4,128)(2,1)S(1)}, bf16[60,4,256]{2,1,0:T(4,128)(2,1)S(1)}, u32[]{:S(2)}, u32[]{:S(2)}) collective-permute-start(bf16[60,4,256]{2,1,0:T(4,128)(2,1)S(1)} %get-tuple-element.16), channel_id=1, source_target_pairs={{0,16},{16,0},{32,48},{48,32},{64,80},{80,64},{96,112},{112,96},{1... | collective-permute-start | bytes 368648 | tf_op jit(solution)/shard_map/ppermute | solution.py:333
  30.6 9.5 %collective-permute-start.3 = (bf16[60,4,256]{2,1,0:T(4,128)(2,1)S(1)}, bf16[60,4,256]{2,1,0:T(4,128)(2,1)S(1)}, u32[]{:S(2)}, u32[]{:S(2)}) collective-permute-start(bf16[60,4,256]{2,1,0:T(4,128)(2,1)S(1)} %get-tuple-element.17), channel_id=1, source_target_pairs={{16,32},{32,16},{48,64},{64,48},{80,96},{96,80},{112,128},{128,112... | collective-permute-start | bytes 368648 | tf_op jit(solution)/shard_map/ppermute | solution.py:334

commit v3 on v2

v3 whole, which is shorter than its diff:
```python
import functools

import jax
import jax.numpy as jnp
from jax import lax
from jax.experimental import pallas as pl
from jax.experimental.pallas import tpu as pltpu
from jax.sharding import PartitionSpec as P

ONSITE_S = -0.22
ONSITE_P = 0.27
HOP_SS = -0.37
HOP_SP = 0.35
HOP_PPS = 0.4
HOP_PPP = -0.114
BOND_LENGTH = 1.536
LATTICE_STEP = 1.6

SIDE = 4
DEPTH = 8
ATOMS = SIDE * SIDE * DEPTH
FACE = SIDE * DEPTH
WIDE = FACE + 2 * DEPTH
NV = 256
LANES = NV // 2
POS_ROWS = 9
LIST_ROWS = 6
AUX = 4
Y_PLACE = (DEPTH, 0, 3 * DEPTH + AUX, 2 * DEPTH + AUX)
Y_AUX = 2 * DEPTH
Y_SITES = FACE + AUX
X_BLOCK = (FACE + AUX, FACE + AUX + DEPTH + AUX)
X_SITES = WIDE + 3 * AUX
STEPS = [(x, y) for x in (-1, 0, 1) for y in (-1, 0, 1)]
F32 = jnp.float32
BF16 = jnp.bfloat16


def iota(shape, axis):
    return lax.broadcasted_iota(jnp.int32, shape, axis)


def onehot(values, expected):
    wide = [jnp.where(row == expected, 1.0, 0.0).astype(BF16) for row in values]
    return wide[0] if len(wide) == 1 else jnp.concatenate(wide, axis=1)


def dot_nt(a, b):
    return lax.dot_general(a, b, (((1,), (1,)), ((), ())), preferred_element_type=F32)


def dot(a, b):
    return jnp.dot(a, b, preferred_element_type=F32)


def list_of(rows):
    first = [rows[k : k + 1] for k in range(2)]
    key = [rows[4 + k : 5 + k] * float(ATOMS) + rows[2 + k : 3 + k] for k in range(2)]
    return first, key


def code(step_x, step_y):
    return (step_x + 1) * 3 + step_y + 1


def hopping(dx, dy, dz, count):
    square = jnp.maximum(dx * dx + dy * dy + dz * dz, 0.5)
    inverse = lax.rsqrt(square)
    cosines = [d * inverse for d in (dx, dy, dz)]
    ratio = BOND_LENGTH * inverse
    radial = ratio * ratio * jnp.exp(1.0 - square * inverse * (1.0 / BOND_LENGTH))

    def final(value):
        return (value.astype(BF16).astype(F32) * count).astype(BF16)

    grid = [[None] * 4 for _ in range(4)]
    grid[0][0] = final(HOP_SS * radial)
    for a in range(3):
        across = final(HOP_SP * radial * cosines[a])
        grid[0][1 + a] = across
        grid[1 + a][0] = -across
        for b in range(a, 3):
            entry = (HOP_PPS - HOP_PPP) * cosines[a] * cosines[b]
            if a == b:
                entry = entry + HOP_PPP
            grid[1 + a][1 + b] = grid[1 + b][1 + a] = final(entry * radial)
    return grid


def planes_of(wave, block):
    n = block.shape[0]
    wide = block.astype(F32).reshape(n // 2, 2, 4, NV)
    wide = jnp.concatenate([wide[:, 0], wide[:, 1]], axis=1).reshape(4 * n, NV)
    for h in range(2):
        wave[h, : 4 * n] = wide[:, h * LANES : (h + 1) * LANES]
    halves = [[wave[h, pl.ds(b, n, stride=4), :] for h in range(2)] for b in range(4)]
    return [jnp.concatenate(pair, axis=1) for pair in halves]


def applied(grid, planes):
    total = None
    for b in range(4):
        stacked = jnp.concatenate([grid[a][b] for a in range(4)], axis=0)
        part = dot(stacked, planes[b].astype(BF16))
        total = part if total is None else total + part
    return total


def atoms_of(planes, wave):
    n = planes[0].shape[0]
    for a in range(4):
        for h in range(2):
            wave[h, pl.ds(a, n, stride=4), :] = planes[a][:, h * LANES : (h + 1) * LANES]
    wide = jnp.concatenate([wave[h, : 4 * n] for h in range(2)], axis=1)
    wide = wide.reshape(n // 2, 8, NV)
    return jnp.stack([wide[:, :4], wide[:, 4:]], axis=1).reshape(n, 4, NV)


def turned(points):
    n = points.shape[1]
    return jnp.concatenate([points, jnp.zeros((5, n), F32)], axis=0).T


def picked_rows(pick, points):
    total = None
    for _ in range(3):
        piece = points.astype(BF16)
        part = dot(pick, piece)
        total = part if total is None else total + part
        points = points - piece.astype(F32)
    return total


def z_shift(zi, zj):
    step = zj - zi
    period = LATTICE_STEP * DEPTH
    return jnp.where(step > 1.5, -period, jnp.where(step < -1.5, period, 0.0))


def wrap(place, across, side, period):
    high = jnp.where((side > 0) & (place == across - 1), period, 0.0)
    return jnp.where((side < 0) & (place == 0), -period, high)


def place_of(sizes):
    return lax.axis_index("gx"), lax.axis_index("gy"), *sizes


def side_of(place):
    first = 1 - 2 * (place & 1)
    return first, -first


def faces_of(side):
    mine = jnp.where(side > 0, SIDE - 1, 0)
    return mine, SIDE - 1 - mine


def aux_of(message, first):
    return jnp.concatenate([message[first + k].astype(F32) for k in range(AUX)], axis=0)


def points_of(rows):
    return rows[0:3] + rows[3:6] + rows[6:9]


def pack_y(sizes, trial, positions, atoms, owner, count, one, two, aux, pos, pairs, owners, total, sem):
    at_x, at_y, across_x, across_y = place_of(sizes)
    copies = [
        pltpu.make_async_copy(a, b, sem.at[k])
        for k, (a, b) in enumerate(
            ((positions, pos), (atoms, pairs), (owner, owners), (count, total))
        )
    ]
    for side, out in zip(side_of(at_y), (one, two)):
        face, _ = faces_of(side)
        for x in range(SIDE):
            begin = (x * SIDE + face) * DEPTH
            part = out.at[pl.ds(Y_PLACE[x], DEPTH)]
            copies.append(
                pltpu.make_async_copy(trial.at[pl.ds(begin, DEPTH)], part, sem.at[len(copies)])
            )
    for copy in copies:
        copy.start()
    rows = 3 * SIDE * SIDE
    tile = (iota((DEPTH, ATOMS), 1) & (DEPTH - 1)) == iota((DEPTH, ATOMS), 0)
    tile = jnp.where(tile, 1.0, 0.0).astype(BF16)
    row = iota((3 * rows, ATOMS), 0)
    keep = (row & (SIDE * SIDE - 1)) == (iota((3 * rows, ATOMS), 1) >> 3)
    gather = (iota((16, 3 * rows), 1) >> 4) == iota((16, 3 * rows), 0)
    gather = jnp.where(gather, 1.0, 0.0).astype(BF16)
    aux[:, ATOMS:] = jnp.zeros((4 * AUX, NV - ATOMS), F32)
    for copy in copies[:4]:
        copy.wait()
    rest = pos[...]
    parts = []
    for _ in range(3):
        piece = rest.astype(BF16)
        parts.append(piece)
        rest = rest - piece.astype(F32)
    spread = dot(jnp.concatenate(parts, axis=0), tile)
    aux[:, :ATOMS] = dot(gather, jnp.where(keep, spread, 0.0).astype(BF16))
    whose = owners[...]
    step = jnp.zeros(whose.shape, F32)
    for x, y in STEPS:
        name = lax.rem(at_x + x + across_x, across_x) * across_y
        name = name + lax.rem(at_y + y + across_y, across_y)
        step = jnp.where(whose == name, float(code(x, y)), step)
    live = iota(whose.shape, 1) < total[0, 0]
    first = jnp.where(live, pairs[0:1], -1).astype(F32)
    second = pairs[1:2].astype(F32)
    for k, values in enumerate((first, second, step)):
        for h in range(2):
            at = POS_ROWS + 2 * k + h
            aux[at : at + 1] = values[:, h * NV : (h + 1) * NV]
    for k in range(AUX):
        site = aux[4 * k : 4 * k + 4].astype(BF16)
        one[Y_AUX + k] = site
        two[Y_AUX + k] = site
    for copy in copies[4:]:
        copy.wait()


def own(sizes, trial, message, acc, one, two, wave):
    for side, out in zip(side_of(place_of(sizes)[0]), (one, two)):
        face, _ = faces_of(side)
        out[:FACE] = trial[pl.ds(face * FACE, FACE)]
        out[FACE : FACE + AUX] = message[Y_AUX : Y_AUX + AUX]
    rows = aux_of(message, Y_AUX)
    first, key = list_of(rows[POS_ROWS : POS_ROWS + LIST_ROWS])
    atom = iota((ATOMS, 1), 0)
    is_first = onehot(first, atom.astype(F32))
    is_second = onehot(key, (atom + code(0, 0) * ATOMS).astype(F32))
    count = dot_nt(is_first, is_second) + dot_nt(is_second, is_first)
    pos = points_of(rows)[:, :ATOMS]
    pos_t = turned(pos)
    zi = (atom & (DEPTH - 1)).astype(F32)
    zj = (iota((1, ATOMS), 1) & (DEPTH - 1)).astype(F32)
    dx, dy = (pos[a : a + 1] - pos_t[:, a : a + 1] for a in range(2))
    dz = (pos[2:3] + z_shift(zi, zj)) - pos_t[:, 2:3]
    grid = hopping(dx, dy, dz, count)
    planes = planes_of(wave, trial[...])
    matrix = jnp.concatenate([jnp.concatenate(line, axis=1) for line in grid], axis=0)
    part = dot(matrix, jnp.concatenate(planes, axis=0).astype(BF16))
    for a in range(4):
        onsite = ONSITE_P if a else ONSITE_S
        rows = slice(a * ATOMS, (a + 1) * ATOMS)
        acc[rows] = onsite * planes[a] + part[rows]


def corners(sizes, y_one, y_two, one_in, two_in, one, two, sem):
    del one_in, two_in
    copies = []
    for side, out in zip(side_of(place_of(sizes)[0]), (one, two)):
        face, _ = faces_of(side)
        begin = jnp.where(face == 0, Y_PLACE[0], Y_AUX)
        for n, message in enumerate((y_one, y_two)):
            part = out.at[pl.ds(X_BLOCK[n], DEPTH + AUX)]
            copy = pltpu.make_async_copy(
                message.at[pl.ds(begin, DEPTH + AUX)], part, sem.at[len(copies)]
            )
            copy.start()
            copies.append(copy)
    for copy in copies:
        copy.wait()


def y_faces(periods, sizes, message, y_one, y_two, acc_in, acc, middle, wave):
    acc[...] = acc_in[...]
    at_x, at_y, _, across_y = place_of(sizes)
    rows = aux_of(message, Y_AUX)
    own_first, own_key = list_of(rows[POS_ROWS : POS_ROWS + LIST_ROWS])
    pos_t = turned(points_of(rows)[:, :ATOMS])
    k = iota((FACE, 1), 0)
    line = (k >> 3) * (SIDE * DEPTH) + (k & (DEPTH - 1))
    crossed = ((k >> 3) ^ 1) * (SIDE * DEPTH) + (k & (DEPTH - 1))
    zi = (k & (DEPTH - 1)).astype(F32)
    zj = (iota((1, FACE), 1) & (DEPTH - 1)).astype(F32)
    half = 2 * DEPTH
    for side, other in zip(side_of(at_y), (y_one, y_two)):
        mine, theirs = faces_of(side)
        rows = aux_of(other, Y_AUX)
        first, key = list_of(rows[POS_ROWS : POS_ROWS + LIST_ROWS])
        my_atom = line + mine * DEPTH
        their_atom = crossed + theirs * DEPTH
        left = [
            onehot(own_first, my_atom.astype(F32)),
            onehot(key, (my_atom + (4 - side) * ATOMS).astype(F32)),
        ]
        right = [
            onehot(own_key, (their_atom + (4 + side) * ATOMS).astype(F32)),
            onehot(first, their_atom.astype(F32)),
        ]
        count = dot_nt(jnp.concatenate(left, axis=1), jnp.concatenate(right, axis=1))
        lane = iota((ATOMS, FACE), 1)
        lane = ((lane >> 3) ^ 1) * (SIDE * DEPTH) + (lane & (DEPTH - 1)) + theirs * DEPTH
        pick = jnp.where(iota((ATOMS, FACE), 0) == lane, 1.0, 0.0).astype(BF16)
        points = points_of(dot(rows[:, :ATOMS].astype(BF16), pick))
        pick = jnp.where(iota((FACE, ATOMS), 1) == my_atom, 1.0, 0.0).astype(BF16)
        mine_t = picked_rows(pick, pos_t)
        dx = points[0:1] - mine_t[:, 0:1]
        dy = (points[1:2] + wrap(at_y, across_y, side, periods[1])) - mine_t[:, 1:2]
        dz = (points[2:3] + z_shift(zi, zj)) - mine_t[:, 2:3]
        grid = hopping(dx, dy, dz, count)
        block = jnp.concatenate([other[:half], other[half + AUX :]], axis=0)
        part = applied(grid, planes_of(wave, block))
        for a in range(4):
            for x in range(SIDE):
                at = pl.multiple_of(a * ATOMS + (x * SIDE + mine) * DEPTH, DEPTH)
                begin = a * FACE + x * DEPTH
                acc[pl.ds(at, DEPTH)] += part[begin : begin + DEPTH]
    planes = [acc[a * ATOMS + FACE : a * ATOMS + 3 * FACE] for a in range(4)]
    middle[...] = atoms_of(planes, wave)


def x_faces(periods, sizes, message, x_two, x_one, acc, middle, out, wave, other_wave, faces, sem):
    copies = [pltpu.make_async_copy(middle, out.at[pl.ds(FACE, 2 * FACE)], sem.at[2])]
    copies[0].start()
    at_x, at_y, across_x, across_y = place_of(sizes)
    rows = aux_of(message, Y_AUX)
    own_first, own_key = list_of(rows[POS_ROWS : POS_ROWS + LIST_ROWS])
    pos_t = turned(points_of(rows)[:, :ATOMS])
    k = iota((FACE, 1), 0)
    zi = (k & (DEPTH - 1)).astype(F32)
    lane = iota((1, WIDE), 1)
    zj = (lane & (DEPTH - 1)).astype(F32)
    y_sides = side_of(at_y)
    shifts = [wrap(at_y, across_y, y, periods[1]) for y in y_sides]
    shift_y = jnp.where(lane < FACE, 0.0, jnp.where(lane < FACE + DEPTH, *shifts))
    parts = []
    for n, (side, other) in enumerate(zip(side_of(at_x), (x_one, x_two))):
        mine, theirs = faces_of(side)
        corner_at = jnp.where(theirs == 0, 0, AUX)
        aux_at = jnp.where(theirs == 0, DEPTH, 0)
        my_atom = k + mine * FACE

        def ghost(shape, axis):
            at = iota(shape, axis)
            part = jnp.where(at < FACE, 0, jnp.where(at < FACE + DEPTH, 1, 2))
            step = jnp.where(part == 0, 0, jnp.where(part == 1, y_sides[0], y_sides[1]))
            row = jnp.where(step > 0, 0, (SIDE - 1) * DEPTH)
            atom = theirs * FACE + jnp.where(part == 0, at, row + (at & (DEPTH - 1)))
            return atom, step, part

        their_atom, step, part = ghost((WIDE, 1), 0)
        target = their_atom + ((side + 1) * 3 + step + 1) * ATOMS
        left = [onehot(own_first, my_atom.astype(F32))]
        right = [onehot(own_key, target.astype(F32))]
        points = None
        lane_atom, _, lane_part = ghost((ATOMS, WIDE), 1)
        for m, y in enumerate((0, *y_sides)):
            rows = aux_of(other, X_BLOCK[m - 1] + aux_at if m else FACE)
            first, key = list_of(rows[POS_ROWS : POS_ROWS + LIST_ROWS])
            wanted = my_atom + ((1 - side) * 3 + 1 - y) * ATOMS
            left.append(onehot(key, wanted.astype(F32)))
            right.append(onehot(first, jnp.where(part == m, their_atom, -2).astype(F32)))
            pick = (iota((ATOMS, WIDE), 0) == lane_atom) & (lane_part == m)
            placed = dot(rows[:, :ATOMS].astype(BF16), jnp.where(pick, 1.0, 0.0).astype(BF16))
            points = placed if points is None else points + placed
        count = dot_nt(jnp.concatenate(left, axis=1), jnp.concatenate(right, axis=1))
        points = points_of(points)
        mine_t = picked_rows(
            jnp.where(iota((FACE, ATOMS), 1) == my_atom, 1.0, 0.0).astype(BF16), pos_t
        )
        dx = (points[0:1] + wrap(at_x, across_x, side, periods[0])) - mine_t[:, 0:1]
        dy = (points[1:2] + shift_y) - mine_t[:, 1:2]
        dz = (points[2:3] + z_shift(zi, zj)) - mine_t[:, 2:3]
        grid = hopping(dx, dy, dz, count)
        block = [other[:FACE]] + [other[pl.ds(X_BLOCK[m] + corner_at, DEPTH)] for m in range(2)]
        planes = planes_of((wave, other_wave)[n], jnp.concatenate(block, axis=0))
        part = applied(grid, planes)
        before = [acc[pl.ds(pl.multiple_of(a * ATOMS + mine * FACE, FACE), FACE)] for a in range(4)]
        parts.append([before[a] + part[a * FACE : (a + 1) * FACE] for a in range(4)])
    for n, side in enumerate(side_of(at_x)):
        mine, _ = faces_of(side)
        faces[n] = atoms_of(parts[n], (wave, other_wave)[n])
        copy = pltpu.make_async_copy(faces.at[n], out.at[pl.ds(mine * FACE, FACE)], sem.at[n])
        copy.start()
        copies.append(copy)
    for copy in copies:
        copy.wait()


def swap(count, begin):
    pairs = []
    for i in range(begin, count + begin, 2):
        a, b = i % count, (i + 1) % count
        pairs += [(a, b), (b, a)]
    return pairs


def exchange(one, two, axis):
    count = lax.axis_size(axis)
    two = lax.ppermute(two, axis, swap(count, 1))
    one = lax.ppermute(one, axis, swap(count, 0))
    return one, two


VMEM = pl.BlockSpec(memory_space=pltpu.VMEM)
HBM = pl.BlockSpec(memory_space=pltpu.HBM)
ANY = pl.BlockSpec(memory_space=pl.ANY)


def call(kernel, inputs, outputs, in_space=VMEM, out_space=VMEM, limit=16, **options):
    limit = limit and limit * 1024 * 1024
    return pl.pallas_call(
        kernel,
        out_shape=outputs,
        in_specs=[in_space] * len(inputs),
        out_specs=[out_space] * len(outputs),
        compiler_params=pltpu.CompilerParams(vmem_limit_bytes=limit),
        **options,
    )(*inputs)


def shards(trial, positions, pair_atoms, pair_owner, pair_image, pair_count):
    sizes = lax.axis_size("gx"), lax.axis_size("gy")
    periods = tuple(LATTICE_STEP * (SIDE * count) for count in sizes)
    mine = trial.reshape(ATOMS, 4, NV)
    slots = pair_owner.shape[2]

    def message(sites):
        return jax.ShapeDtypeStruct((sites, 4, NV), BF16)

    def wave(rows):
        return pltpu.VMEM((2, rows, LANES), F32)

    y_out = call(
        functools.partial(pack_y, sizes),
        (
            mine,
            positions.reshape(3 * SIDE * SIDE, DEPTH),
            pair_atoms.reshape(2, slots),
            pair_owner.reshape(1, slots),
            pair_count,
        ),
        [message(Y_SITES)] * 2,
        in_space=HBM,
        limit=None,
        scratch_shapes=[
            pltpu.VMEM((4 * AUX, NV), F32),
            pltpu.VMEM((3 * SIDE * SIDE, DEPTH), F32),
            pltpu.VMEM((2, slots), jnp.int32),
            pltpu.VMEM((1, slots), jnp.int32),
            pltpu.SMEM((1, 1), jnp.int32),
            pltpu.SemaphoreType.DMA((4 + 2 * SIDE,)),
        ],
    )
    y_one, y_two = exchange(*y_out, "gy")
    rows = jax.ShapeDtypeStruct((4 * ATOMS, NV), F32)
    acc, *x_out = call(
        functools.partial(own, sizes),
        (mine, y_out[0]),
        [rows] + [message(X_SITES)] * 2,
        scratch_shapes=[wave(4 * ATOMS)],
    )
    x_out = call(
        functools.partial(corners, sizes),
        (y_one, y_two, *x_out),
        [message(X_SITES)] * 2,
        in_space=ANY,
        out_space=ANY,
        input_output_aliases={2: 0, 3: 1},
        scratch_shapes=[pltpu.SemaphoreType.DMA((4,))],
    )
    x_one, x_two = exchange(*x_out, "gx")
    acc, middle = call(
        functools.partial(y_faces, periods, sizes),
        (y_out[0], y_one, y_two, acc),
        [rows, jax.ShapeDtypeStruct((ATOMS // 2, 4, NV), F32)],
        scratch_shapes=[wave(2 * ATOMS)],
    )
    (product,) = call(
        functools.partial(x_faces, periods, sizes),
        (y_out[0], x_two, x_one, acc, middle),
        [jax.ShapeDtypeStruct((ATOMS, 4, NV), F32)],
        out_space=HBM,
        scratch_shapes=[
            wave(4 * WIDE),
            wave(4 * WIDE),
            pltpu.VMEM((2, FACE, 4, NV), F32),
            pltpu.SemaphoreType.DMA((3,)),
        ],
    )
    return product.reshape(trial.shape)


def solution(mesh):
    in_specs = (
        P("gx", "gy", None, None, None),
        P(None, "gx", "gy", None),
        P("gx", "gy", None, None),
        P("gx", "gy", None),
        P("gx", "gy", None, None),
        P("gx", "gy"),
    )
    out_specs = P("gx", "gy", None, None, None)
    return jax.shard_map(shards, mesh=mesh, in_specs=in_specs, out_specs=out_specs, check_vma=False)
```

time: 43.4 us -> 39.4 us (0.908)
  the two profiles are of different devices: /device:TPU:63 before, /device:TPU:1 now
where the time goes in v3:
time: 39.4 us; the launch traced here: 39 us
  starting transfers between devices  30.3 us (77%)
  Pallas kernels  5.09 us (13%)
  waiting for transfers between devices  1.95 us (5%)
  local copies, waits for them, and re-layouts  0.89 us (2%)
  between operations  0.8 us (2%)
    ppermute x2, starting transfers between devices, exchange(): two = lax.ppermute(two, axis, swap(count, 1))  23.9 us
    ppermute x2, starting transfers between devices, exchange(): one = lax.ppermute(one, axis, swap(count, 0))  6.4 us
    pallas_call x5, Pallas kernels, call(): pl.pallas_call(kernel, out_shape=outputs, in_specs=[in_space] * len(input...  5.09 us
    ppermute x2, waiting for transfers between devices, exchange(): one = lax.ppermute(one, axis, swap(count, 0))  1.95 us
    unnamed x6, local copies, waits for them, and re-layouts  0.89 us
  transfers between devices with their start and end apart: 4, of which 2 were waited for; matrix products, arithmetic and copies ran while one was open for 0% of the time, Pallas kernels for 4%

profile of v3, /device:TPU:1, one launch (start us, length us, event | category | flops | bytes accessed | tf_op | source)
XLA Modules:
  0.0 39.0 jit_solution(3740227974118031423)
XLA Ops:
  0.0 0.0 copy-start
  0.7 1.8 %shard_map.55 = (bf16[36,4,256]{2,1,0:T(4,128)(2,1)}, bf16[36,4,256]{2,1,0:T(4,128)(2,1)}) custom-call(bf16[128,4,256]{2,1,0:T(4,128)(2,1)} %bitcast.5, f32[48,8]{1,0:T(8,128)} %bitcast.7, s32[2,512]{1,0:T(2,128)} %bitcast.8, s32[1,512]{1,0:T(1,128)} %bitcast.9, s32[1,1]{1,0:T(1,128)S(6)} %copy.10.count), custom_call_target="tpu_custom_call" | custom-call | tf_op jit(solution)/shard_map/pallas_call | solution.py:406
  2.5 18.8 %collective-permute-start.1 = (bf16[36,4,256]{2,1,0:T(4,128)(2,1)}, bf16[36,4,256]{2,1,0:T(4,128)(2,1)S(1)}, u32[]{:S(2)}, u32[]{:S(2)}) collective-permute-start(bf16[36,4,256]{2,1,0:T(4,128)(2,1)} %get-tuple-element.15), channel_id=1, source_target_pairs={{1,2},{2,1},{3,4},{4,3},{5,6},{6,5},{7,8},{8,7},{9,10},{10,9},{11,... | collective-permute-start | bytes 221192 | tf_op jit(solution)/shard_map/ppermute | solution.py:394
  21.3 1.9 %collective-permute-start = (bf16[36,4,256]{2,1,0:T(4,128)(2,1)}, bf16[36,4,256]{2,1,0:T(4,128)(2,1)S(1)}, u32[]{:S(2)}, u32[]{:S(2)}) collective-permute-start(bf16[36,4,256]{2,1,0:T(4,128)(2,1)} %get-tuple-element.14.message), channel_id=1, source_target_pairs={{0,1},{1,0},{2,3},{3,2},{4,5},{5,4},{6,7},{7,6},{8,9},{9,8},{10,11... | collective-permute-start | bytes 221192 | tf_op jit(solution)/shard_map/ppermute | solution.py:395
  23.2 0.0 copy-done
  23.2 0.0 copy-start.1
  23.2 0.9 %copy-done.1 = bf16[36,4,256]{2,1,0:T(4,128)(2,1)S(1)} copy-done((bf16[36,4,256]{2,1,0:T(4,128)(2,1)S(1)}, bf16[36,4,256]{2,1,0:T(4,128)(2,1)}, u32[]{:S(2)}) %copy-start.1) | copy-done | bytes 73752
  24.1 0.7 %shard_map.56 = (f32[512,256]{1,0:T(8,128)S(1)}, bf16[60,4,256]{2,1,0:T(4,128)(2,1)S(1)}, bf16[60,4,256]{2,1,0:T(4,128)(2,1)S(1)}) custom-call(bf16[128,4,256]{2,1,0:T(4,128)(2,1)S(1)} %bitcast.6, bf16[36,4,256]{2,1,0:T(4,128)(2,1)S(1)} %copy-done.1), custom_call_target="tpu_custom_call" | custom-call | tf_op jit(solution)/shard_map/pallas_call | solution.py:406
  24.8 0.0 collective-permute-done.1.y_two
  24.8 1.8 %collective-permute-done.y_one = bf16[36,4,256]{2,1,0:T(4,128)(2,1)S(1)} collective-permute-done((bf16[36,4,256]{2,1,0:T(4,128)(2,1)}, bf16[36,4,256]{2,1,0:T(4,128)(2,1)S(1)}, u32[]{:S(2)}, u32[]{:S(2)}) %collective-permute-start) | collective-permute-done | bytes 73760 | tf_op jit(solution)/shard_map/ppermute | solution.py:395
  26.6 0.0 copy-start.2
  26.6 0.2 shard_map.57
  26.8 5.1 %collective-permute-start.2 = (bf16[60,4,256]{2,1,0:T(4,128)(2,1)S(1)}, bf16[60,4,256]{2,1,0:T(4,128)(2,1)S(1)}, u32[]{:S(2)}, u32[]{:S(2)}) collective-permute-start(bf16[60,4,256]{2,1,0:T(4,128)(2,1)S(1)} %get-tuple-element.18), channel_id=1, source_target_pairs={{16,32},{32,16},{48,64},{64,48},{80,96},{96,80},{112,128},{128,112... | collective-permute-start | bytes 368648 | tf_op jit(solution)/shard_map/ppermute | solution.py:394
  31.9 4.5 %collective-permute-start.3 = (bf16[60,4,256]{2,1,0:T(4,128)(2,1)S(1)}, bf16[60,4,256]{2,1,0:T(4,128)(2,1)S(1)}, u32[]{:S(2)}, u32[]{:S(2)}) collective-permute-start(bf16[60,4,256]{2,1,0:T(4,128)(2,1)S(1)} %get-tuple-element.19), channel_id=1, source_target_pairs={{0,16},{16,0},{32,48},{48,32},{64,80},{80,64},{96,112},{112,96},{1... | collective-permute-start | bytes 368648 | tf_op jit(solution)/shard_map/ppermute | solution.py:395
  36.4 0.0 copy-done.2
  36.4 0.8 %shard_map.58 = (f32[512,256]{1,0:T(8,128)S(1)}, f32[64,4,256]{2,1,0:T(4,128)S(1)}) custom-call(bf16[36,4,256]{2,1,0:T(4,128)(2,1)S(1)} %copy-done.2, bf16[36,4,256]{2,1,0:T(4,128)(2,1)S(1)} %collective-permute-done.y_one, bf16[36,4,256]{2,1,0:T(4,128)(2,1)S(1)} %collective-permute-done.1.y_two, f32[512,256]{1,0:T(8,128)S(1)} %get-tuple-element.20.acc_in), custom_call_target="tpu_custom_call" | custom-call | tf_op jit(solution)/shard_map/pallas_call | solution.py:406
  37.1 0.0 collective-permute-done.2.x_two
  37.2 0.2 collective-permute-done.3.x_one
  37.3 1.7 %shard_map.59 = f32[128,4,256]{2,1,0:T(4,128)} custom-call(bf16[36,4,256]{2,1,0:T(4,128)(2,1)S(1)} %copy-done.2, bf16[60,4,256]{2,1,0:T(4,128)(2,1)S(1)} %collective-permute-done.2.x_two, bf16[60,4,256]{2,1,0:T(4,128)(2,1)S(1)} %collective-permute-done.3.x_one, f32[512,256]{1,0:T(8,128)S(1)} %get-tuple-element.21.acc, f32[64,4,256]{2,1,0:T(4,128)S(1)} %get-tuple-element.22.middle), custom_call_target="tpu_custom_call" | custom-call | tf_op jit(solution)/shard_map/pallas_call | solution.py:406
Async XLA Ops:
  0.0 23.2 %copy-start = (bf16[4,4,8,4,256]{4,3,2,1,0:T(4,128)(2,1)S(1)}, bf16[4,4,8,4,256]{4,3,2,1,0:T(4,128)(2,1)}, u32[]{:S(2)}) copy-start(bf16[4,4,8,4,256]{4,3,2,1,0:T(4,128)(2,1)} %param.6) | copy-start | bytes 786436
  2.5 22.3 %collective-permute-start.1 = (bf16[36,4,256]{2,1,0:T(4,128)(2,1)}, bf16[36,4,256]{2,1,0:T(4,128)(2,1)S(1)}, u32[]{:S(2)}, u32[]{:S(2)}) collective-permute-start(bf16[36,4,256]{2,1,0:T(4,128)(2,1)} %get-tuple-element.15), channel_id=1, source_target_pairs={{1,2},{2,1},{3,4},{4,3},{5,6},{6,5},{7,8},{8,7},{9,10},{10,9},{11,... | collective-permute-start | bytes 221192 | tf_op jit(solution)/shard_map/ppermute | solution.py:394
  21.3 5.3 %collective-permute-start = (bf16[36,4,256]{2,1,0:T(4,128)(2,1)}, bf16[36,4,256]{2,1,0:T(4,128)(2,1)S(1)}, u32[]{:S(2)}, u32[]{:S(2)}) collective-permute-start(bf16[36,4,256]{2,1,0:T(4,128)(2,1)} %get-tuple-element.14.message), channel_id=1, source_target_pairs={{0,1},{1,0},{2,3},{3,2},{4,5},{5,4},{6,7},{7,6},{8,9},{9,8},{10,11... | collective-permute-start | bytes 221192 | tf_op jit(solution)/shard_map/ppermute | solution.py:395
  23.2 0.9 %copy-start.1 = (bf16[36,4,256]{2,1,0:T(4,128)(2,1)S(1)}, bf16[36,4,256]{2,1,0:T(4,128)(2,1)}, u32[]{:S(2)}) copy-start(bf16[36,4,256]{2,1,0:T(4,128)(2,1)} %get-tuple-element.14.message) | copy-start | bytes 221188
  26.6 9.8 %copy-start.2 = (bf16[36,4,256]{2,1,0:T(4,128)(2,1)S(1)}, bf16[36,4,256]{2,1,0:T(4,128)(2,1)}, u32[]{:S(2)}) copy-start(bf16[36,4,256]{2,1,0:T(4,128)(2,1)} %get-tuple-element.14.message) | copy-start | bytes 221188
  26.8 10.4 %collective-permute-start.2 = (bf16[60,4,256]{2,1,0:T(4,128)(2,1)S(1)}, bf16[60,4,256]{2,1,0:T(4,128)(2,1)S(1)}, u32[]{:S(2)}, u32[]{:S(2)}) collective-permute-start(bf16[60,4,256]{2,1,0:T(4,128)(2,1)S(1)} %get-tuple-element.18), channel_id=1, source_target_pairs={{16,32},{32,16},{48,64},{64,48},{80,96},{96,80},{112,128},{128,112... | collective-permute-start | bytes 368648 | tf_op jit(solution)/shard_map/ppermute | solution.py:394
  31.9 5.4 %collective-permute-start.3 = (bf16[60,4,256]{2,1,0:T(4,128)(2,1)S(1)}, bf16[60,4,256]{2,1,0:T(4,128)(2,1)S(1)}, u32[]{:S(2)}, u32[]{:S(2)}) collective-permute-start(bf16[60,4,256]{2,1,0:T(4,128)(2,1)S(1)} %get-tuple-element.19), channel_id=1, source_target_pairs={{0,16},{16,0},{32,48},{48,32},{64,80},{80,64},{96,112},{112,96},{1... | collective-permute-start | bytes 368648 | tf_op jit(solution)/shard_map/ppermute | solution.py:395

commit v4 on v3

--- a/solution.py
+++ b/solution.py
@@ -160,19 +160,22 @@
     return jnp.concatenate([message[first + k].astype(F32) for k in range(AUX)], axis=0)
 
 
+def either(lower, low, top):
+    return lambda at: jnp.where(lower, low[at].astype(F32), top[at].astype(F32))
+
+
 def points_of(rows):
     return rows[0:3] + rows[3:6] + rows[6:9]
 
 
-def pack_y(sizes, trial, positions, atoms, owner, count, one, two, aux, pos, pairs, owners, total, sem):
+def pack_y(sizes, trial, positions, atoms, owner, count, low, two, top, aux, pos, pairs, owners, sem):
     at_x, at_y, across_x, across_y = place_of(sizes)
     copies = [
         pltpu.make_async_copy(a, b, sem.at[k])
-        for k, (a, b) in enumerate(
-            ((positions, pos), (atoms, pairs), (owner, owners), (count, total))
-        )
+        for k, (a, b) in enumerate(((positions, pos), (atoms, pairs), (owner, owners)))
     ]
-    for side, out in zip(side_of(at_y), (one, two)):
+    first, second = side_of(at_y)
+    for side, out in ((first, low), (second, two), (first, top)):
         face, _ = faces_of(side)
         for x in range(SIDE):
             begin = (x * SIDE + face) * DEPTH
@@ -190,7 +193,7 @@
     gather = (iota((16, 3 * rows), 1) >> 4) == iota((16, 3 * rows), 0)
     gather = jnp.where(gather, 1.0, 0.0).astype(BF16)
     aux[:, ATOMS:] = jnp.zeros((4 * AUX, NV - ATOMS), F32)
-    for copy in copies[:4]:
+    for copy in copies[:3]:
         copy.wait()
     rest = pos[...]
     parts = []
@@ -206,7 +209,7 @@
         name = lax.rem(at_x + x + across_x, across_x) * across_y
         name = name + lax.rem(at_y + y + across_y, across_y)
         step = jnp.where(whose == name, float(code(x, y)), step)
-    live = iota(whose.shape, 1) < total[0, 0]
+    live = iota(whose.shape, 1) < count[0, 0]
     first = jnp.where(live, pairs[0:1], -1).astype(F32)
     second = pairs[1:2].astype(F32)
     for k, values in enumerate((first, second, step)):
@@ -215,18 +218,19 @@
             aux[at : at + 1] = values[:, h * NV : (h + 1) * NV]
     for k in range(AUX):
         site = aux[4 * k : 4 * k + 4].astype(BF16)
-        one[Y_AUX + k] = site
-        two[Y_AUX + k] = site
-    for copy in copies[4:]:
+        for out in (low, two, top):
+            out[Y_AUX + k] = site
+    for copy in copies[3:]:
         copy.wait()
 
 
-def own(sizes, trial, message, acc, one, two, wave):
+def own(sizes, trial, aux, acc, one, two, wave):
     for side, out in zip(side_of(place_of(sizes)[0]), (one, two)):
         face, _ = faces_of(side)
         out[:FACE] = trial[pl.ds(face * FACE, FACE)]
-        out[FACE : FACE + AUX] = message[Y_AUX : Y_AUX + AUX]
-    rows = aux_of(message, Y_AUX)
+        for k in range(AUX):
+            out[FACE + k] = aux[4 * k : 4 * k + 4].astype(BF16)
+    rows = aux[...]
     first, key = list_of(rows[POS_ROWS : POS_ROWS + LIST_ROWS])
     atom = iota((ATOMS, 1), 0)
     is_first = onehot(first, atom.astype(F32))
@@ -248,27 +252,44 @@
         acc[rows] = onsite * planes[a] + part[rows]
 
 
-def corners(sizes, y_one, y_two, one_in, two_in, one, two, sem):
+def in_lower(sizes):
+    _, at_y, _, across_y = place_of(sizes)
+    return at_y < across_y // 4 * 2
+
+
+def corners(sizes, y_low, y_two, y_top, one_in, two_in, one, two, sem):
     del one_in, two_in
+    lower = in_lower(sizes)
     copies = []
     for side, out in zip(side_of(place_of(sizes)[0]), (one, two)):
         face, _ = faces_of(side)
         begin = jnp.where(face == 0, Y_PLACE[0], Y_AUX)
-        for n, message in enumerate((y_one, y_two)):
+
+        def copy_of(message, n):
             part = out.at[pl.ds(X_BLOCK[n], DEPTH + AUX)]
-            copy = pltpu.make_async_copy(
+            return pltpu.make_async_copy(
                 message.at[pl.ds(begin, DEPTH + AUX)], part, sem.at[len(copies)]
             )
-            copy.start()
-            copies.append(copy)
+
+        @pl.when(lower)
+        def _():
+            copy_of(y_low, 0).start()
+
+        @pl.when(jnp.logical_not(lower))
+        def _():
+            copy_of(y_top, 0).start()
+
+        copies.append(copy_of(y_low, 0))
+        copies.append(copy_of(y_two, 1))
+        copies[-1].start()
     for copy in copies:
         copy.wait()
 
 
-def y_faces(periods, sizes, message, y_one, y_two, acc_in, acc, middle, wave):
+def y_faces(periods, sizes, aux, y_low, y_two, y_top, acc_in, acc, middle, wave):
     acc[...] = acc_in[...]
     at_x, at_y, _, across_y = place_of(sizes)
-    rows = aux_of(message, Y_AUX)
+    rows = aux[...]
     own_first, own_key = list_of(rows[POS_ROWS : POS_ROWS + LIST_ROWS])
     pos_t = turned(points_of(rows)[:, :ATOMS])
     k = iota((FACE, 1), 0)
@@ -277,9 +298,10 @@
     zi = (k & (DEPTH - 1)).astype(F32)
     zj = (iota((1, FACE), 1) & (DEPTH - 1)).astype(F32)
     half = 2 * DEPTH
-    for side, other in zip(side_of(at_y), (y_one, y_two)):
+    readers = either(in_lower(sizes), y_low, y_top), lambda at: y_two[at].astype(F32)
+    for side, read in zip(side_of(at_y), readers):
         mine, theirs = faces_of(side)
-        rows = aux_of(other, Y_AUX)
+        rows = jnp.concatenate([read(Y_AUX + k) for k in range(AUX)], axis=0)
         first, key = list_of(rows[POS_ROWS : POS_ROWS + LIST_ROWS])
         my_atom = line + mine * DEPTH
         their_atom = crossed + theirs * DEPTH
@@ -302,7 +324,7 @@
         dy = (points[1:2] + wrap(at_y, across_y, side, periods[1])) - mine_t[:, 1:2]
         dz = (points[2:3] + z_shift(zi, zj)) - mine_t[:, 2:3]
         grid = hopping(dx, dy, dz, count)
-        block = jnp.concatenate([other[:half], other[half + AUX :]], axis=0)
+        block = jnp.concatenate([read(slice(0, half)), read(slice(half + AUX, Y_SITES))], axis=0)
         part = applied(grid, planes_of(wave, block))
         for a in range(4):
             for x in range(SIDE):
@@ -313,11 +335,11 @@
     middle[...] = atoms_of(planes, wave)
 
 
-def x_faces(periods, sizes, message, x_two, x_one, acc, middle, out, wave, other_wave, faces, sem):
+def x_faces(periods, sizes, aux, x_two, x_one, acc, middle, out, wave, other_wave, faces, sem):
     copies = [pltpu.make_async_copy(middle, out.at[pl.ds(FACE, 2 * FACE)], sem.at[2])]
     copies[0].start()
     at_x, at_y, across_x, across_y = place_of(sizes)
-    rows = aux_of(message, Y_AUX)
+    rows = aux[...]
     own_first, own_key = list_of(rows[POS_ROWS : POS_ROWS + LIST_ROWS])
     pos_t = turned(points_of(rows)[:, :ATOMS])
     k = iota((FACE, 1), 0)
@@ -396,9 +418,20 @@
     return one, two
 
 
+def exchange_y(low, two, top):
+    count = lax.axis_size("gy")
+    pairs = swap(count, 0)
+    begin = count // 4 * 2
+    low = lax.ppermute(low, "gy", pairs[:begin])
+    two = lax.ppermute(two, "gy", swap(count, 1))
+    top = lax.ppermute(top, "gy", pairs[begin:])
+    return low, two, top
+
+
 VMEM = pl.BlockSpec(memory_space=pltpu.VMEM)
 HBM = pl.BlockSpec(memory_space=pltpu.HBM)
 ANY = pl.BlockSpec(memory_space=pl.ANY)
+SMEM = pl.BlockSpec(memory_space=pltpu.SMEM)
 
 
 def call(kernel, inputs, outputs, in_space=VMEM, out_space=VMEM, limit=16, **options):
@@ -406,7 +439,7 @@
     return pl.pallas_call(
         kernel,
         out_shape=outputs,
-        in_specs=[in_space] * len(inputs),
+        in_specs=in_space if isinstance(in_space, list) else [in_space] * len(inputs),
         out_specs=[out_space] * len(outputs),
         compiler_params=pltpu.CompilerParams(vmem_limit_bytes=limit),
         **options,
@@ -425,54 +458,54 @@
     def wave(rows):
         return pltpu.VMEM((2, rows, LANES), F32)
 
-    y_out = call(
+    *y_out, aux = call(
         functools.partial(pack_y, sizes),
-        (
-            mine,
-            positions.reshape(3 * SIDE * SIDE, DEPTH),
-            pair_atoms.reshape(2, slots),
-            pair_owner.reshape(1, slots),
-            pair_count,
-        ),
-        [message(Y_SITES)] * 2,
-        in_space=HBM,
-        limit=None,
+        tuple(
+            pltpu.with_memory_space_constraint(array, pltpu.HBM)
+            for array in (
+                mine,
+                positions.reshape(3 * SIDE * SIDE, DEPTH),
+                pair_atoms.reshape(2, slots),
+                pair_owner.reshape(1, slots),
+            )
+        )
+        + (pair_count,),
+        [message(Y_SITES)] * 3 + [jax.ShapeDtypeStruct((4 * AUX, NV), F32)],
+        in_space=[HBM] * 4 + [SMEM],
         scratch_shapes=[
-            pltpu.VMEM((4 * AUX, NV), F32),
             pltpu.VMEM((3 * SIDE * SIDE, DEPTH), F32),
             pltpu.VMEM((2, slots), jnp.int32),
             pltpu.VMEM((1, slots), jnp.int32),
-            pltpu.SMEM((1, 1), jnp.int32),
-            pltpu.SemaphoreType.DMA((4 + 2 * SIDE,)),
+            pltpu.SemaphoreType.DMA((3 + 3 * SIDE,)),
         ],
     )
-    y_one, y_two = exchange(*y_out, "gy")
+    y_low, y_two, y_top = exchange_y(*y_out)
     rows = jax.ShapeDtypeStruct((4 * ATOMS, NV), F32)
     acc, *x_out = call(
         functools.partial(own, sizes),
-        (mine, y_out[0]),
+        (mine, aux),
         [rows] + [message(X_SITES)] * 2,
         scratch_shapes=[wave(4 * ATOMS)],
     )
     x_out = call(
         functools.partial(corners, sizes),
-        (y_one, y_two, *x_out),
+        (y_low, y_two, y_top, *x_out),
         [message(X_SITES)] * 2,
         in_space=ANY,
         out_space=ANY,
-        input_output_aliases={2: 0, 3: 1},
+        input_output_aliases={3: 0, 4: 1},
         scratch_shapes=[pltpu.SemaphoreType.DMA((4,))],
     )
     x_one, x_two = exchange(*x_out, "gx")
     acc, middle = call(
         functools.partial(y_faces, periods, sizes),
-        (y_out[0], y_one, y_two, acc),
+        (aux, y_low, y_two, y_top, acc),
         [rows, jax.ShapeDtypeStruct((ATOMS // 2, 4, NV), F32)],
         scratch_shapes=[wave(2 * ATOMS)],
     )
     (product,) = call(
         functools.partial(x_faces, periods, sizes),
-        (y_out[0], x_two, x_one, acc, middle),
+        (aux, x_two, x_one, acc, middle),
         [jax.ShapeDtypeStruct((ATOMS, 4, NV), F32)],
         out_space=HBM,
         scratch_shapes=[

time: 39.4 us -> 35.8 us (0.909)
  waiting for transfers between devices: 1.95 us -> 0.53 us
  local copies, waits for them, and re-layouts: 0.89 us -> 0.01 us
  Pallas kernels: 5.09 us -> 4.48 us
  starting transfers between devices: 30.3 us -> 29.7 us
    ppermute x0 -> x3, starting transfers between devices: none -> 20.1 us  [the longest x1 14.6 us: exchange_y(): two = lax.ppermute(two, 'gy', swap(count, 1))]
    ppermute x2 -> x1, starting transfers between devices: 23.9 us -> 4.55 us  [exchange(): two = lax.ppermute(two, axis, swap(count, 1))]
    ppermute x2 -> x1, waiting for transfers between devices: 1.95 us -> 0.17 us  [exchange(): one = lax.ppermute(one, axis, swap(count, 0))]
    ppermute x2 -> x1, starting transfers between devices: 6.4 us -> 5.05 us  [exchange(): one = lax.ppermute(one, axis, swap(count, 0))]
    unnamed x6 -> x2, local copies, waits for them, and re-layouts: 0.89 us -> 0.01 us
    pallas_call x5, Pallas kernels: 5.09 us -> 4.48 us  [call(): pl.pallas_call(kernel, out_shape=outputs, in_specs=in_space if isinstance...]
  transfers between devices with their start and end apart: 4 -> 5, of which waited for: 2 -> 2; matrix products, arithmetic and copies ran while one was open for 0% -> 0% of each run, Pallas kernels for 4% -> 4%
where the time goes in v4:
time: 35.8 us; the launch traced here: 35.5 us
  starting transfers between devices  29.7 us (83%)
  Pallas kernels  4.48 us (13%)
  between operations  0.79 us (2%)
  waiting for transfers between devices  0.53 us (1%)
    ppermute x1, starting transfers between devices, exchange_y(): two = lax.ppermute(two, 'gy', swap(count, 1))  14.6 us
    ppermute x1, starting transfers between devices, exchange(): one = lax.ppermute(one, axis, swap(count, 0))  5.05 us
    ppermute x1, starting transfers between devices, exchange_y(): low = lax.ppermute(low, 'gy', pairs[:begin])  4.83 us
    ppermute x1, starting transfers between devices, exchange(): two = lax.ppermute(two, axis, swap(count, 1))  4.55 us
    pallas_call x5, Pallas kernels, call(): pl.pallas_call(kernel, out_shape=outputs, in_specs=in_space if isinstance...  4.48 us
  transfers between devices with their start and end apart: 5, of which 2 were waited for; matrix products, arithmetic and copies ran while one was open for 0% of the time, Pallas kernels for 4%

profile of v4, /device:TPU:1, one launch (start us, length us, event | category | flops | bytes accessed | tf_op | source)
XLA Modules:
  0.0 35.5 jit_solution(8562915539910418799)
XLA Ops:
  0.0 0.0 copy-start
  0.7 1.2 %shard_map.55 = (bf16[36,4,256]{2,1,0:T(4,128)(2,1)S(1)}, bf16[36,4,256]{2,1,0:T(4,128)(2,1)S(1)}, bf16[36,4,256]{2,1,0:T(4,128)(2,1)S(1)}, f32[16,256]{1,0:T(8,128)S(1)}) custom-call(bf16[128,4,256]{2,1,0:T(4,128)(2,1)} %bitcast.5, f32[48,8]{1,0:T(8,128)} %bitcast.7, s32[2,512]{1,0:T(2,128)} %bitcast.8, s32[1,512]{1,0:T(1,128)} %bitcast.9, ...), custom_call_target="tpu_custom_call" | custom-call | tf_op jit(solution)/shard_map/pallas_call | solution.py:439
  1.9 4.8 %collective-permute-start = (bf16[36,4,256]{2,1,0:T(4,128)(2,1)S(1)}, bf16[36,4,256]{2,1,0:T(4,128)(2,1)S(1)}, u32[]{:S(2)}, u32[]{:S(2)}) collective-permute-start(bf16[36,4,256]{2,1,0:T(4,128)(2,1)S(1)} %get-tuple-element.17), channel_id=1, source_target_pairs={{0,1},{1,0},{2,3},{3,2},{4,5},{5,4},{6,7},{7,6},{16,17},{17,16},{1... | collective-permute-start | bytes 221192 | tf_op jit(solution)/shard_map/ppermute | solution.py:425
  6.7 14.6 %collective-permute-start.1 = (bf16[36,4,256]{2,1,0:T(4,128)(2,1)S(1)}, bf16[36,4,256]{2,1,0:T(4,128)(2,1)S(1)}, u32[]{:S(2)}, u32[]{:S(2)}) collective-permute-start(bf16[36,4,256]{2,1,0:T(4,128)(2,1)S(1)} %get-tuple-element.18), channel_id=1, source_target_pairs={{1,2},{2,1},{3,4},{4,3},{5,6},{6,5},{7,8},{8,7},{9,10},{10,9},{11,... | collective-permute-start | bytes 221192 | tf_op jit(solution)/shard_map/ppermute | solution.py:426
  21.3 0.7 %collective-permute-start.2 = (bf16[36,4,256]{2,1,0:T(4,128)(2,1)S(1)}, bf16[36,4,256]{2,1,0:T(4,128)(2,1)S(1)}, u32[]{:S(2)}, u32[]{:S(2)}) collective-permute-start(bf16[36,4,256]{2,1,0:T(4,128)(2,1)S(1)} %get-tuple-element.19), channel_id=1, source_target_pairs={{8,9},{9,8},{10,11},{11,10},{12,13},{13,12},{14,15},{15,14},{24,25... | collective-permute-start | bytes 221192 | tf_op jit(solution)/shard_map/ppermute | solution.py:427
  22.0 0.0 copy-done
  22.0 0.7 %shard_map.56 = (f32[512,256]{1,0:T(8,128)S(1)}, bf16[60,4,256]{2,1,0:T(4,128)(2,1)S(1)}, bf16[60,4,256]{2,1,0:T(4,128)(2,1)S(1)}) custom-call(bf16[128,4,256]{2,1,0:T(4,128)(2,1)S(1)} %bitcast.6, f32[16,256]{1,0:T(8,128)S(1)} %get-tuple-element.16.aux), custom_call_target="tpu_custom_call" | custom-call | tf_op jit(solution)/shard_map/pallas_call | solution.py:439
  22.7 0.0 collective-permute-done.y_low
  22.7 0.4 collective-permute-done.1.y_two
  23.1 0.0 collective-permute-done.2.y_top
  23.1 0.2 shard_map.57
  23.2 4.6 %collective-permute-start.3 = (bf16[60,4,256]{2,1,0:T(4,128)(2,1)S(1)}, bf16[60,4,256]{2,1,0:T(4,128)(2,1)S(1)}, u32[]{:S(2)}, u32[]{:S(2)}) collective-permute-start(bf16[60,4,256]{2,1,0:T(4,128)(2,1)S(1)} %get-tuple-element.22), channel_id=1, source_target_pairs={{16,32},{32,16},{48,64},{64,48},{80,96},{96,80},{112,128},{128,112... | collective-permute-start | bytes 368648 | tf_op jit(solution)/shard_map/ppermute | solution.py:416
  27.8 5.0 %collective-permute-start.4 = (bf16[60,4,256]{2,1,0:T(4,128)(2,1)S(1)}, bf16[60,4,256]{2,1,0:T(4,128)(2,1)S(1)}, u32[]{:S(2)}, u32[]{:S(2)}) collective-permute-start(bf16[60,4,256]{2,1,0:T(4,128)(2,1)S(1)} %get-tuple-element.23), channel_id=1, source_target_pairs={{0,16},{16,0},{32,48},{48,32},{64,80},{80,64},{96,112},{112,96},{1... | collective-permute-start | bytes 368648 | tf_op jit(solution)/shard_map/ppermute | solution.py:417
  32.9 0.8 %shard_map.58 = (f32[512,256]{1,0:T(8,128)S(1)}, f32[64,4,256]{2,1,0:T(4,128)S(1)}) custom-call(f32[16,256]{1,0:T(8,128)S(1)} %get-tuple-element.16.aux, bf16[36,4,256]{2,1,0:T(4,128)(2,1)S(1)} %collective-permute-done.y_low, bf16[36,4,256]{2,1,0:T(4,128)(2,1)S(1)} %collective-permute-done.1.y_two, bf16[36,4,256]{2,1,0:T(4,128)(2,1)S(1)} %collective-permute-done.2.y_top, ...), custom_call_target="tpu_custom_call" | custom-call | tf_op jit(solution)/shard_map/pallas_call | solution.py:439
  33.6 0.0 collective-permute-done.3.x_two
  33.6 0.2 collective-permute-done.4.x_one
  33.8 1.7 %shard_map.59 = f32[128,4,256]{2,1,0:T(4,128)} custom-call(f32[16,256]{1,0:T(8,128)S(1)} %get-tuple-element.16.aux, bf16[60,4,256]{2,1,0:T(4,128)(2,1)S(1)} %collective-permute-done.3.x_two, bf16[60,4,256]{2,1,0:T(4,128)(2,1)S(1)} %collective-permute-done.4.x_one, f32[512,256]{1,0:T(8,128)S(1)} %get-tuple-element.25.acc, ...), custom_call_target="tpu_custom_call" | custom-call | tf_op jit(solution)/shard_map/pallas_call | solution.py:439
Async XLA Ops:
  0.0 22.0 %copy-start = (bf16[4,4,8,4,256]{4,3,2,1,0:T(4,128)(2,1)S(1)}, bf16[4,4,8,4,256]{4,3,2,1,0:T(4,128)(2,1)}, u32[]{:S(2)}) copy-start(bf16[4,4,8,4,256]{4,3,2,1,0:T(4,128)(2,1)} %param.6) | copy-start | bytes 786436
  1.9 20.8 %collective-permute-start = (bf16[36,4,256]{2,1,0:T(4,128)(2,1)S(1)}, bf16[36,4,256]{2,1,0:T(4,128)(2,1)S(1)}, u32[]{:S(2)}, u32[]{:S(2)}) collective-permute-start(bf16[36,4,256]{2,1,0:T(4,128)(2,1)S(1)} %get-tuple-element.17), channel_id=1, source_target_pairs={{0,1},{1,0},{2,3},{3,2},{4,5},{5,4},{6,7},{7,6},{16,17},{17,16},{1... | collective-permute-start | bytes 221192 | tf_op jit(solution)/shard_map/ppermute | solution.py:425
  6.7 16.3 %collective-permute-start.1 = (bf16[36,4,256]{2,1,0:T(4,128)(2,1)S(1)}, bf16[36,4,256]{2,1,0:T(4,128)(2,1)S(1)}, u32[]{:S(2)}, u32[]{:S(2)}) collective-permute-start(bf16[36,4,256]{2,1,0:T(4,128)(2,1)S(1)} %get-tuple-element.18), channel_id=1, source_target_pairs={{1,2},{2,1},{3,4},{4,3},{5,6},{6,5},{7,8},{8,7},{9,10},{10,9},{11,... | collective-permute-start | bytes 221192 | tf_op jit(solution)/shard_map/ppermute | solution.py:426
  21.3 1.7 %collective-permute-start.2 = (bf16[36,4,256]{2,1,0:T(4,128)(2,1)S(1)}, bf16[36,4,256]{2,1,0:T(4,128)(2,1)S(1)}, u32[]{:S(2)}, u32[]{:S(2)}) collective-permute-start(bf16[36,4,256]{2,1,0:T(4,128)(2,1)S(1)} %get-tuple-element.19), channel_id=1, source_target_pairs={{8,9},{9,8},{10,11},{11,10},{12,13},{13,12},{14,15},{15,14},{24,25... | collective-permute-start | bytes 221192 | tf_op jit(solution)/shard_map/ppermute | solution.py:427
  23.2 10.4 %collective-permute-start.3 = (bf16[60,4,256]{2,1,0:T(4,128)(2,1)S(1)}, bf16[60,4,256]{2,1,0:T(4,128)(2,1)S(1)}, u32[]{:S(2)}, u32[]{:S(2)}) collective-permute-start(bf16[60,4,256]{2,1,0:T(4,128)(2,1)S(1)} %get-tuple-element.22), channel_id=1, source_target_pairs={{16,32},{32,16},{48,64},{64,48},{80,96},{96,80},{112,128},{128,112... | collective-permute-start | bytes 368648 | tf_op jit(solution)/shard_map/ppermute | solution.py:416
  27.8 6.0 %collective-permute-start.4 = (bf16[60,4,256]{2,1,0:T(4,128)(2,1)S(1)}, bf16[60,4,256]{2,1,0:T(4,128)(2,1)S(1)}, u32[]{:S(2)}, u32[]{:S(2)}) collective-permute-start(bf16[60,4,256]{2,1,0:T(4,128)(2,1)S(1)} %get-tuple-element.23), channel_id=1, source_target_pairs={{0,16},{16,0},{32,48},{48,32},{64,80},{80,64},{96,112},{112,96},{1... | collective-permute-start | bytes 368648 | tf_op jit(solution)/shard_map/ppermute | solution.py:417

commit v5 on v4

v5 whole, which is shorter than its diff:
```python
import functools

import jax
import jax.numpy as jnp
from jax import lax
from jax.experimental import pallas as pl
from jax.experimental.pallas import tpu as pltpu
from jax.sharding import PartitionSpec as P

ONSITE_S = -0.22
ONSITE_P = 0.27
HOP_SS = -0.37
HOP_SP = 0.35
HOP_PPS = 0.4
HOP_PPP = -0.114
BOND_LENGTH = 1.536
LATTICE_STEP = 1.6

SIDE = 4
DEPTH = 8
ATOMS = SIDE * SIDE * DEPTH
FACE = SIDE * DEPTH
WIDE = FACE + 2 * DEPTH
NV = 256
LANES = NV // 2
POS_ROWS = 9
LIST_ROWS = 6
AUX = 4
Y_PLACE = (DEPTH, 0, 3 * DEPTH + AUX, 2 * DEPTH + AUX)
Y_AUX = 2 * DEPTH
Y_SITES = FACE + AUX
BLOCK = DEPTH + AUX
X_BLOCK = (FACE + AUX, FACE + AUX + BLOCK)
X_SITES = WIDE + 3 * AUX
STEPS = [(x, y) for x in (-1, 0, 1) for y in (-1, 0, 1)]
F32 = jnp.float32
BF16 = jnp.bfloat16


def iota(shape, axis):
    return lax.broadcasted_iota(jnp.int32, shape, axis)


def onehot(values, expected):
    wide = [jnp.where(row == expected, 1.0, 0.0).astype(BF16) for row in values]
    return wide[0] if len(wide) == 1 else jnp.concatenate(wide, axis=1)


def dot_nt(a, b):
    return lax.dot_general(a, b, (((1,), (1,)), ((), ())), preferred_element_type=F32)


def dot(a, b):
    return jnp.dot(a, b, preferred_element_type=F32)


def list_of(rows):
    first = [rows[k : k + 1] for k in range(2)]
    key = [rows[4 + k : 5 + k] * float(ATOMS) + rows[2 + k : 3 + k] for k in range(2)]
    return first, key


def code(step_x, step_y):
    return (step_x + 1) * 3 + step_y + 1


def hopping(dx, dy, dz, count):
    square = jnp.maximum(dx * dx + dy * dy + dz * dz, 0.5)
    inverse = lax.rsqrt(square)
    cosines = [d * inverse for d in (dx, dy, dz)]
    ratio = BOND_LENGTH * inverse
    radial = ratio * ratio * jnp.exp(1.0 - square * inverse * (1.0 / BOND_LENGTH))

    def final(value):
        return (value.astype(BF16).astype(F32) * count).astype(BF16)

    grid = [[None] * 4 for _ in range(4)]
    grid[0][0] = final(HOP_SS * radial)
    for a in range(3):
        across = final(HOP_SP * radial * cosines[a])
        grid[0][1 + a] = across
        grid[1 + a][0] = -across
        for b in range(a, 3):
            entry = (HOP_PPS - HOP_PPP) * cosines[a] * cosines[b]
            if a == b:
                entry = entry + HOP_PPP
            grid[1 + a][1 + b] = grid[1 + b][1 + a] = final(entry * radial)
    return grid


def planes_of(wave, block):
    n = block.shape[0]
    wide = block.astype(F32).reshape(n // 2, 2, 4, NV)
    wide = jnp.concatenate([wide[:, 0], wide[:, 1]], axis=1).reshape(4 * n, NV)
    for h in range(2):
        wave[h, : 4 * n] = wide[:, h * LANES : (h + 1) * LANES]
    halves = [[wave[h, pl.ds(b, n, stride=4), :] for h in range(2)] for b in range(4)]
    return [jnp.concatenate(pair, axis=1) for pair in halves]


def applied(grid, planes):
    total = None
    for b in range(4):
        stacked = jnp.concatenate([grid[a][b] for a in range(4)], axis=0)
        part = dot(stacked, planes[b].astype(BF16))
        total = part if total is None else total + part
    return total


def atoms_of(planes, wave):
    n = planes[0].shape[0]
    for a in range(4):
        for h in range(2):
            wave[h, pl.ds(a, n, stride=4), :] = planes[a][:, h * LANES : (h + 1) * LANES]
    wide = jnp.concatenate([wave[h, : 4 * n] for h in range(2)], axis=1)
    wide = wide.reshape(n // 2, 8, NV)
    return jnp.stack([wide[:, :4], wide[:, 4:]], axis=1).reshape(n, 4, NV)


def turned(points):
    n = points.shape[1]
    return jnp.concatenate([points, jnp.zeros((5, n), F32)], axis=0).T


def picked_rows(pick, points):
    total = None
    for _ in range(3):
        piece = points.astype(BF16)
        part = dot(pick, piece)
        total = part if total is None else total + part
        points = points - piece.astype(F32)
    return total


def z_shift(zi, zj):
    step = zj - zi
    period = LATTICE_STEP * DEPTH
    return jnp.where(step > 1.5, -period, jnp.where(step < -1.5, period, 0.0))


def wrap(place, across, side, period):
    high = jnp.where((side > 0) & (place == across - 1), period, 0.0)
    return jnp.where((side < 0) & (place == 0), -period, high)


def place_of(sizes):
    return lax.axis_index("gx"), lax.axis_index("gy"), *sizes


def side_of(place):
    first = 1 - 2 * (place & 1)
    return first, -first


def faces_of(side):
    mine = jnp.where(side > 0, SIDE - 1, 0)
    return mine, SIDE - 1 - mine


def sum_of(*readers):
    def read(at):
        total = None
        for reader in readers:
            value = reader(at)
            total = value if total is None else total + value
        return total

    return read


def reader_of(message, first=0):
    return lambda at: message[pl.ds(first + at[0], at[1])].astype(F32)


def aux_of(read, first):
    sites = read((first, AUX))
    return jnp.concatenate([sites[k] for k in range(AUX)], axis=0)


def points_of(rows):
    return rows[0:3] + rows[3:6] + rows[6:9]


def pack_y(sizes, trial, positions, atoms, owner, count, *refs):
    low, two, top, over, over_up, over_down, aux, pos, pairs, owners, sem = refs
    at_x, at_y, across_x, across_y = place_of(sizes)
    copies = [
        pltpu.make_async_copy(a, b, sem.at[k])
        for k, (a, b) in enumerate(((positions, pos), (atoms, pairs), (owner, owners)))
    ]
    faces = [faces_of(side)[0] for side in side_of(at_y)]
    moves = [
        (x, faces[n], out.at[pl.ds(begin + Y_PLACE[x], DEPTH)])
        for n, out, begin in (
            (0, low, 0),
            (1, low, Y_SITES),
            (1, two, 0),
            (0, top, 0),
            (1, over, 0),
        )
        for x in range(SIDE)
    ]
    moves.append((SIDE - 1, faces[1], over_up.at[pl.ds(AUX, DEPTH)]))
    moves.append((0, faces[1], over_down.at[pl.ds(0, DEPTH)]))
    for x, face, out in moves:
        begin = (x * SIDE + face) * DEPTH
        copies.append(
            pltpu.make_async_copy(trial.at[pl.ds(begin, DEPTH)], out, sem.at[len(copies)])
        )
    for copy in copies:
        copy.start()
    rows = 3 * SIDE * SIDE
    tile = (iota((DEPTH, ATOMS), 1) & (DEPTH - 1)) == iota((DEPTH, ATOMS), 0)
    tile = jnp.where(tile, 1.0, 0.0).astype(BF16)
    row = iota((3 * rows, ATOMS), 0)
    keep = (row & (SIDE * SIDE - 1)) == (iota((3 * rows, ATOMS), 1) >> 3)
    gather = (iota((16, 3 * rows), 1) >> 4) == iota((16, 3 * rows), 0)
    gather = jnp.where(gather, 1.0, 0.0).astype(BF16)
    aux[:, ATOMS:] = jnp.zeros((4 * AUX, NV - ATOMS), F32)
    for copy in copies[:3]:
        copy.wait()
    rest = pos[...]
    parts = []
    for _ in range(3):
        piece = rest.astype(BF16)
        parts.append(piece)
        rest = rest - piece.astype(F32)
    spread = dot(jnp.concatenate(parts, axis=0), tile)
    aux[:, :ATOMS] = dot(gather, jnp.where(keep, spread, 0.0).astype(BF16))
    whose = owners[...]
    step = jnp.zeros(whose.shape, F32)
    for x, y in STEPS:
        name = lax.rem(at_x + x + across_x, across_x) * across_y
        name = name + lax.rem(at_y + y + across_y, across_y)
        step = jnp.where(whose == name, float(code(x, y)), step)
    live = iota(whose.shape, 1) < count[0, 0]
    first = jnp.where(live, pairs[0:1], -1).astype(F32)
    second = pairs[1:2].astype(F32)
    for k, values in enumerate((first, second, step)):
        for h in range(2):
            at = POS_ROWS + 2 * k + h
            aux[at : at + 1] = values[:, h * NV : (h + 1) * NV]
    places = [(out, Y_AUX) for out in (low, two, top, over)]
    places += [(low, Y_SITES + Y_AUX), (over_up, 0), (over_down, DEPTH)]
    for k in range(AUX):
        site = aux[4 * k : 4 * k + 4].astype(BF16)
        for out, at in places:
            out[at + k] = site
    for copy in copies[3:]:
        copy.wait()


def own(trial, aux, acc, wave):
    rows = aux[...]
    first, key = list_of(rows[POS_ROWS : POS_ROWS + LIST_ROWS])
    atom = iota((ATOMS, 1), 0)
    is_first = onehot(first, atom.astype(F32))
    is_second = onehot(key, (atom + code(0, 0) * ATOMS).astype(F32))
    count = dot_nt(is_first, is_second) + dot_nt(is_second, is_first)
    pos = points_of(rows)[:, :ATOMS]
    pos_t = turned(pos)
    zi = (atom & (DEPTH - 1)).astype(F32)
    zj = (iota((1, ATOMS), 1) & (DEPTH - 1)).astype(F32)
    dx, dy = (pos[a : a + 1] - pos_t[:, a : a + 1] for a in range(2))
    dz = (pos[2:3] + z_shift(zi, zj)) - pos_t[:, 2:3]
    grid = hopping(dx, dy, dz, count)
    planes = planes_of(wave, trial[...])
    matrix = jnp.concatenate([jnp.concatenate(line, axis=1) for line in grid], axis=0)
    part = dot(matrix, jnp.concatenate(planes, axis=0).astype(BF16))
    for a in range(4):
        onsite = ONSITE_P if a else ONSITE_S
        rows = slice(a * ATOMS, (a + 1) * ATOMS)
        acc[rows] = onsite * planes[a] + part[rows]


def corners(sizes, late, *refs):
    *inputs, one, two, sem = refs
    if late:
        _, relayed, *inputs = inputs
    trial, message, y_one, y_two = inputs
    at_x, at_y, _, across_y = place_of(sizes)
    copies = []

    def copy_of(source, begin, count, out, at):
        return pltpu.make_async_copy(
            source.at[pl.ds(begin, count)], out.at[pl.ds(at, count)], sem.at[len(copies)]
        )

    for side, out in zip(side_of(at_x), (one, two)):
        face, _ = faces_of(side)
        begin = jnp.where(face == 0, Y_PLACE[0], Y_AUX)
        for given in (
            (trial, face * FACE, FACE, out, 0),
            (message, Y_AUX, AUX, out, FACE),
            (y_one, begin, BLOCK, out, X_BLOCK[0]),
        ):
            copies.append(copy_of(*given))
            copies[-1].start()
        plain = copy_of(y_two, begin, BLOCK, out, X_BLOCK[1])
        if late:
            other = copy_of(relayed, begin, BLOCK, out, X_BLOCK[1])

            @pl.when(at_y == across_y - 1)
            def _():
                other.start()

            @pl.when(at_y != across_y - 1)
            def _():
                plain.start()
        else:
            plain.start()
        copies.append(plain)
    for copy in copies:
        copy.wait()


def crossed(sizes, over, up, down, one, two, sem):
    del over
    copies = []
    for n, (side, out) in enumerate(zip(side_of(place_of(sizes)[0]), (one, two))):
        low, high = (pltpu.make_async_copy(source.at[pl.ds(0, BLOCK)], out, sem.at[n]) for source in (up, down))

        @pl.when(side < 0)
        def _():
            low.start()

        @pl.when(side > 0)
        def _():
            high.start()

        copies.append(low)
    for copy in copies:
        copy.wait()


def hand_on(after, y_low, top, relay, out, sem):
    del after
    copies = [
        pltpu.make_async_copy(y_low.at[pl.ds(Y_SITES, Y_SITES)], relay, sem.at[0]),
        pltpu.make_async_copy(top, out, sem.at[1]),
    ]
    for copy in copies:
        copy.start()
    for copy in copies:
        copy.wait()


def own_of(aux):
    rows = aux[...]
    return *list_of(rows[POS_ROWS : POS_ROWS + LIST_ROWS]), turned(points_of(rows)[:, :ATOMS])


def y_atoms(side):
    mine, theirs = faces_of(side)
    k = iota((FACE, 1), 0)
    z = k & (DEPTH - 1)
    line = (k >> 3) * (SIDE * DEPTH) + z
    crossed = ((k >> 3) ^ 1) * (SIDE * DEPTH) + z
    return line + mine * DEPTH, crossed + theirs * DEPTH


def y_ahead(side, own_first, own_key, pos_t):
    my_atom, their_atom = y_atoms(side)
    left = onehot(own_first, my_atom.astype(F32))
    right = onehot(own_key, (their_atom + (4 + side) * ATOMS).astype(F32))
    pick = jnp.where(iota((FACE, ATOMS), 1) == my_atom, 1.0, 0.0).astype(BF16)
    return dot_nt(left, right), picked_rows(pick, pos_t)


def y_part(period, sizes, side, read, forward, mine_t, wave):
    _, at_y, _, across_y = place_of(sizes)
    _, theirs = faces_of(side)
    my_atom, their_atom = y_atoms(side)
    rows = aux_of(read, Y_AUX)
    first, key = list_of(rows[POS_ROWS : POS_ROWS + LIST_ROWS])
    left = onehot(key, (my_atom + (4 - side) * ATOMS).astype(F32))
    count = forward + dot_nt(left, onehot(first, their_atom.astype(F32)))
    lane = iota((ATOMS, FACE), 1)
    lane = ((lane >> 3) ^ 1) * (SIDE * DEPTH) + (lane & (DEPTH - 1)) + theirs * DEPTH
    pick = jnp.where(iota((ATOMS, FACE), 0) == lane, 1.0, 0.0).astype(BF16)
    points = points_of(dot(rows[:, :ATOMS].astype(BF16), pick))
    zi = (iota((FACE, 1), 0) & (DEPTH - 1)).astype(F32)
    zj = (iota((1, FACE), 1) & (DEPTH - 1)).astype(F32)
    dx = points[0:1] - mine_t[:, 0:1]
    dy = (points[1:2] + wrap(at_y, across_y, side, period)) - mine_t[:, 1:2]
    dz = (points[2:3] + z_shift(zi, zj)) - mine_t[:, 2:3]
    grid = hopping(dx, dy, dz, count)
    half = 2 * DEPTH
    block = jnp.concatenate([read((0, half)), read((half + AUX, half))], axis=0)
    return applied(grid, planes_of(wave, block))


def y_add(acc, side, part):
    mine, _ = faces_of(side)
    for a in range(4):
        for x in range(SIDE):
            at = pl.multiple_of(a * ATOMS + (x * SIDE + mine) * DEPTH, DEPTH)
            begin = a * FACE + x * DEPTH
            acc[pl.ds(at, DEPTH)] += part[begin : begin + DEPTH]


def ghost(theirs, y_sides, shape, axis):
    at = iota(shape, axis)
    part = jnp.where(at < FACE, 0, jnp.where(at < FACE + DEPTH, 1, 2))
    step = jnp.where(part == 0, 0, jnp.where(part == 1, y_sides[0], y_sides[1]))
    row = jnp.where(step > 0, 0, (SIDE - 1) * DEPTH)
    atom = theirs * FACE + jnp.where(part == 0, at, row + (at & (DEPTH - 1)))
    return atom, step, part


def first_half(periods, sizes, aux, y_low, y_top, acc_in, *refs):
    acc, forward_y, mine_y, forward_x, mine_x, wave = refs
    acc[...] = acc_in[...]
    at_x, at_y, _, _ = place_of(sizes)
    own_first, own_key, pos_t = own_of(aux)
    y_sides = side_of(at_y)
    forward_y[...], mine_y[...] = y_ahead(y_sides[1], own_first, own_key, pos_t)
    for n, side in enumerate(side_of(at_x)):
        mine, theirs = faces_of(side)
        my_atom = iota((FACE, 1), 0) + mine * FACE
        their_atom, step, _ = ghost(theirs, y_sides, (WIDE, 1), 0)
        target = their_atom + ((side + 1) * 3 + step + 1) * ATOMS
        left = onehot(own_first, my_atom.astype(F32))
        forward_x[n] = dot_nt(left, onehot(own_key, target.astype(F32)))
        pick = jnp.where(iota((FACE, ATOMS), 1) == my_atom, 1.0, 0.0).astype(BF16)
        mine_x[n] = picked_rows(pick, pos_t)
    forward, mine_t = y_ahead(y_sides[0], own_first, own_key, pos_t)
    read = sum_of(reader_of(y_low), reader_of(y_top))
    y_add(acc, y_sides[0], y_part(periods[1], sizes, y_sides[0], read, forward, mine_t, wave))


def second_half(periods, sizes, *refs):
    forward_y, mine_y, forward_x, mine_x, acc_in = refs[:5]
    y_two, over, relayed, *beside = refs[5:10]
    x_messages = refs[10:12]
    out, acc, wave, one_wave, two_wave, result, sem = refs[12:]
    at_x, at_y, across_x, across_y = place_of(sizes)
    acc[...] = acc_in[...]
    y_sides = side_of(at_y)
    x_sides = side_of(at_x)
    read = sum_of(reader_of(y_two), reader_of(over), reader_of(relayed))
    added = y_part(periods[1], sizes, y_sides[1], read, forward_y[...], mine_y[...], wave)
    k = iota((FACE, 1), 0)
    zi = (k & (DEPTH - 1)).astype(F32)
    lane = iota((1, WIDE), 1)
    zj = (lane & (DEPTH - 1)).astype(F32)
    shifts = [wrap(at_y, across_y, y, periods[1]) for y in y_sides]
    shift_y = jnp.where(lane < FACE, 0.0, jnp.where(lane < FACE + DEPTH, *shifts))
    parts = []
    for n, side in enumerate(x_sides):
        mine, theirs = faces_of(side)
        corner_at = jnp.where(theirs == 0, 0, AUX)
        aux_at = jnp.where(theirs == 0, DEPTH, 0)
        plain = reader_of(x_messages[n])

        def second(at, plain=plain, other=reader_of(beside[n])):
            return plain((X_BLOCK[1] + at[0], at[1])) + other(at)

        def first(at, plain=plain):
            return plain((X_BLOCK[0] + at[0], at[1]))

        my_atom = k + mine * FACE
        their_atom, _, part = ghost(theirs, y_sides, (WIDE, 1), 0)
        lane_atom, _, lane_part = ghost(theirs, y_sides, (ATOMS, WIDE), 1)
        left, right, picks, placed = [], [], [], []
        for m, y in enumerate((0, *y_sides)):
            rows = aux_of((plain, first, second)[m], aux_at if m else FACE)
            listed, key = list_of(rows[POS_ROWS : POS_ROWS + LIST_ROWS])
            wanted = my_atom + ((1 - side) * 3 + 1 - y) * ATOMS
            left.append(onehot(key, wanted.astype(F32)))
            right.append(onehot(listed, jnp.where(part == m, their_atom, -2).astype(F32)))
            pick = (iota((ATOMS, WIDE), 0) == lane_atom) & (lane_part == m)
            picks.append(jnp.where(pick, 1.0, 0.0).astype(BF16))
            placed.append(rows[:, :ATOMS].astype(BF16))
        count = forward_x[n] + dot_nt(
            jnp.concatenate(left, axis=1), jnp.concatenate(right, axis=1)
        )
        points = dot(jnp.concatenate(placed, axis=1), jnp.concatenate(picks, axis=0))
        points = points_of(points)
        mine_t = mine_x[n]
        dx = (points[0:1] + wrap(at_x, across_x, side, periods[0])) - mine_t[:, 0:1]
        dy = (points[1:2] + shift_y) - mine_t[:, 1:2]
        dz = (points[2:3] + z_shift(zi, zj)) - mine_t[:, 2:3]
        grid = hopping(dx, dy, dz, count)
        block = [plain((0, FACE)), first((corner_at, DEPTH)), second((corner_at, DEPTH))]
        planes = planes_of((one_wave, two_wave)[n], jnp.concatenate(block, axis=0))
        parts.append(applied(grid, planes))
    y_add(acc, y_sides[1], added)
    planes = [acc[a * ATOMS + FACE : a * ATOMS + 3 * FACE] for a in range(4)]
    result[FACE : 3 * FACE] = atoms_of(planes, wave)
    middle = pl.ds(FACE, 2 * FACE)
    copies = [pltpu.make_async_copy(result.at[middle], out.at[middle], sem.at[2])]
    copies[0].start()
    for n, side in enumerate(x_sides):
        mine, _ = faces_of(side)
        planes = []
        for a in range(4):
            at = pl.multiple_of(a * ATOMS + mine * FACE, FACE)
            planes.append(acc[pl.ds(at, FACE)] + parts[n][a * FACE : (a + 1) * FACE])
        face = pl.ds(mine * FACE, FACE)
        result[face] = atoms_of(planes, (one_wave, two_wave)[n])
        copies.append(pltpu.make_async_copy(result.at[face], out.at[face], sem.at[n]))
        copies[-1].start()
    for copy in copies:
        copy.wait()


def swap(count, begin):
    pairs = []
    for i in range(begin, count + begin, 2):
        a, b = i % count, (i + 1) % count
        pairs += [(a, b), (b, a)]
    return pairs


def exchange_x(one, two, rows):
    count, across_y = lax.axis_size("gx"), lax.axis_size("gy")

    def pairs(begin):
        return [
            (a * across_y + y, b * across_y + y) for y in rows for a, b in swap(count, begin)
        ]

    two = lax.ppermute(two, ("gx", "gy"), pairs(1))
    one = lax.ppermute(one, ("gx", "gy"), pairs(0))
    return one, two


def over_wrap(message, step):
    count, across_y = lax.axis_size("gx"), lax.axis_size("gy")
    pairs = [
        (x * across_y + across_y - 1, (x + step) % count * across_y) for x in range(count)
    ]
    return lax.ppermute(message, ("gx", "gy"), pairs)


VMEM = pl.BlockSpec(memory_space=pltpu.VMEM)
SMEM = pl.BlockSpec(memory_space=pltpu.SMEM)
HBM = pl.BlockSpec(memory_space=pltpu.HBM)
ANY = pl.BlockSpec(memory_space=pl.ANY)


def call(kernel, inputs, outputs, in_space=VMEM, out_space=VMEM, **options):
    return pl.pallas_call(
        kernel,
        out_shape=outputs,
        in_specs=in_space if isinstance(in_space, list) else [in_space] * len(inputs),
        out_specs=[out_space] * len(outputs),
        compiler_params=pltpu.CompilerParams(vmem_limit_bytes=16 * 1024 * 1024),
        **options,
    )(*inputs)


def shards(trial, positions, pair_atoms, pair_owner, pair_image, pair_count):
    sizes = across_x, across_y = lax.axis_size("gx"), lax.axis_size("gy")
    periods = tuple(LATTICE_STEP * (SIDE * count) for count in sizes)
    mine = trial.reshape(ATOMS, 4, NV)
    slots = pair_owner.shape[2]

    def message(sites):
        return jax.ShapeDtypeStruct((sites, 4, NV), BF16)

    def floats(*shape):
        return jax.ShapeDtypeStruct(shape, F32)

    def wave(rows):
        return pltpu.VMEM((2, rows, LANES), F32)

    low, two, top, over, over_up, over_down, aux = call(
        functools.partial(pack_y, sizes),
        tuple(
            pltpu.with_memory_space_constraint(array, pltpu.HBM)
            for array in (
                mine,
                positions.reshape(3 * SIDE * SIDE, DEPTH),
                pair_atoms.reshape(2, slots),
                pair_owner.reshape(1, slots),
            )
        )
        + (pair_count,),
        [message(2 * Y_SITES)]
        + [message(Y_SITES)] * 3
        + [message(Y_SITES)] * 2
        + [floats(4 * AUX, NV)],
        in_space=[HBM] * 4 + [SMEM],
        scratch_shapes=[
            pltpu.VMEM((3 * SIDE * SIDE, DEPTH), F32),
            pltpu.VMEM((2, slots), jnp.int32),
            pltpu.VMEM((1, slots), jnp.int32),
            pltpu.SemaphoreType.DMA((3 + 5 * SIDE + 2,)),
        ],
    )
    half = across_y // 4 * 2
    pairs = swap(across_y, 0)
    early = lax.axis_index("gy") < half
    y_low = lax.ppermute(low, "gy", pairs[:half])
    y_two = lax.ppermute(two, "gy", swap(across_y, 1)[:-2])
    over = over_wrap(over, 0)
    over_up = over_wrap(over_up, 1)
    over_down = over_wrap(over_down, -1)
    (acc,) = call(own, (mine, aux), [floats(4 * ATOMS, NV)], scratch_shapes=[wave(4 * ATOMS)])

    def x_messages(late, *given):
        return call(
            functools.partial(corners, sizes, late),
            given,
            [message(X_SITES)] * 2,
            in_space=ANY,
            out_space=ANY,
            scratch_shapes=[pltpu.SemaphoreType.DMA((8,))],
        )

    x_in = lax.cond(
        early,
        lambda: exchange_x(*x_messages(False, mine, two, y_low, y_two), range(half)),
        lambda: (jnp.zeros((X_SITES, 4, NV), BF16),) * 2,
    )
    relay, top = call(
        hand_on,
        (x_in[0], y_low, top),
        [message(Y_SITES)] * 2,
        in_space=ANY,
        out_space=ANY,
        scratch_shapes=[pltpu.SemaphoreType.DMA((2,))],
    )
    relayed = lax.ppermute(relay, "gy", [(1, across_y - 1)])
    y_top = lax.ppermute(top, "gy", pairs[half:])
    beside = call(
        functools.partial(crossed, sizes),
        (over, over_up, over_down),
        [message(BLOCK)] * 2,
        in_space=ANY,
        out_space=ANY,
        scratch_shapes=[pltpu.SemaphoreType.DMA((2,))],
    )
    x_late = x_messages(True, beside[0], relayed, mine, two, y_top, y_two)
    x_in = lax.cond(
        early,
        lambda: tuple(x_in),
        lambda: exchange_x(*x_late, range(half, across_y)),
    )
    acc, *ahead = call(
        functools.partial(first_half, periods, sizes),
        (aux, y_low, y_top, acc),
        [
            floats(4 * ATOMS, NV),
            floats(FACE, FACE),
            floats(FACE, 8),
            floats(2, FACE, WIDE),
            floats(2, FACE, 8),
        ],
        scratch_shapes=[wave(4 * FACE)],
    )
    (product,) = call(
        functools.partial(second_half, periods, sizes),
        (*ahead, acc, y_two, over, relayed, *beside, *x_in),
        [floats(ATOMS, 4, NV)],
        out_space=HBM,
        scratch_shapes=[
            pltpu.VMEM((4 * ATOMS, NV), F32),
            wave(2 * ATOMS),
            wave(4 * WIDE),
            wave(4 * WIDE),
            pltpu.VMEM((ATOMS, 4, NV), F32),
            pltpu.SemaphoreType.DMA((3,)),
        ],
    )
    return product.reshape(trial.shape)


def solution(mesh):
    in_specs = (
        P("gx", "gy", None, None, None),
        P(None, "gx", "gy", None),
        P("gx", "gy", None, None),
        P("gx", "gy", None),
        P("gx", "gy", None, None),
        P("gx", "gy"),
    )
    out_specs = P("gx", "gy", None, None, None)
    return jax.shard_map(shards, mesh=mesh, in_specs=in_specs, out_specs=out_specs, check_vma=False)
```

time: 35.8 us -> 43.4 us (1.21)
  the two profiles are of different devices: /device:TPU:1 before, /device:TPU:64 now
where the time goes in v5:
time: 43.4 us; the launch traced here: 43 us
  starting transfers between devices  23.9 us (55%)
  waiting for transfers between devices  11.1 us (26%)
  Pallas kernels  5.28 us (12%)
  local copies, waits for them, and re-layouts  1.81 us (4%)
  between operations  0.84 us (2%)
    ppermute x1, starting transfers between devices, shards(): y_low = lax.ppermute(low, 'gy', pairs[:half])  14.2 us
    ppermute x1, waiting for transfers between devices, exchange_x(): two = lax.ppermute(two, ('gx', 'gy'), pairs(1))  7.69 us
    pallas_call x8, Pallas kernels, call(): pl.pallas_call(kernel, out_shape=outputs, in_specs=in_space if isinstance...  5.28 us
    ppermute x1, waiting for transfers between devices, shards(): y_two = lax.ppermute(two, 'gy', swap(across_y, 1)[:-2])  2.29 us
    ppermute x3, starting transfers between devices, over_wrap(): return lax.ppermute(message, ('gx', 'gy'), pairs)  2 us
    ppermute x1, starting transfers between devices, exchange_x(): one = lax.ppermute(one, ('gx', 'gy'), pairs(0))  1.92 us
    ppermute x1, starting transfers between devices, exchange_x(): two = lax.ppermute(two, ('gx', 'gy'), pairs(1))  1.92 us
    ppermute x1, starting transfers between devices, shards(): y_two = lax.ppermute(two, 'gy', swap(across_y, 1)[:-2])  1.92 us
  transfers between devices with their start and end apart: 9, of which 3 were waited for; matrix products, arithmetic and copies ran while one was open for 0% of the time, Pallas kernels for 3%

profile of v5, /device:TPU:64, one launch (start us, length us, event | category | flops | bytes accessed | tf_op | source)
XLA Modules:
  0.0 43.0 jit_solution(7654396909898275023)
XLA Ops:
  0.7 1.3 %shard_map.55 = (bf16[72,4,256]{2,1,0:T(4,128)(2,1)S(1)}, bf16[36,4,256]{2,1,0:T(4,128)(2,1)S(1)}, bf16[36,4,256]{2,1,0:T(4,128)(2,1)S(1)}, bf16[36,4,256]{2,1,0...) custom-call(bf16[128,4,256]{2,1,0:T(4,128)(2,1)} %bitcast.5, ...), custom_call_target="tpu_custom_call" | custom-call | tf_op jit(solution)/shard_map/pallas_call | solution.py:544
  2.0 14.2 %collective-permute-start.4 = (bf16[72,4,256]{2,1,0:T(4,128)(2,1)S(1)}, bf16[72,4,256]{2,1,0:T(4,128)(2,1)S(1)}, u32[]{:S(2)}, u32[]{:S(2)}) collective-permute-start(bf16[72,4,256]{2,1,0:T(4,128)(2,1)S(1)} %get-tuple-element.49), channel_id=1, source_target_pairs={{0,1},{1,0},{2,3},{3,2},{4,5},{5,4},{6,7},{7,6},{16,17},{17,16},{1... | collective-permute-start | bytes 442376 | tf_op jit(solution)/shard_map/ppermute | solution.py:596
  16.2 1.9 %collective-permute-start.5 = (bf16[36,4,256]{2,1,0:T(4,128)(2,1)S(1)}, bf16[36,4,256]{2,1,0:T(4,128)(2,1)S(1)}, u32[]{:S(2)}, u32[]{:S(2)}) collective-permute-start(bf16[36,4,256]{2,1,0:T(4,128)(2,1)S(1)} %get-tuple-element.50.refs_3_), channel_id=1, source_target_pairs={{1,2},{2,1},{3,4},{4,3},{5,6},{6,5},{7,8},{8,7},{9,10},{10,9},{11,... | collective-permute-start | bytes 221192 | tf_op jit(solution)/shard_map/ppermute | solution.py:597
  18.1 0.7 %collective-permute-start.7 = (bf16[36,4,256]{2,1,0:T(4,128)(2,1)S(1)}, bf16[36,4,256]{2,1,0:T(4,128)(2,1)S(1)}, u32[]{:S(2)}, u32[]{:S(2)}) collective-permute-start(bf16[36,4,256]{2,1,0:T(4,128)(2,1)S(1)} %get-tuple-element.59), channel_id=1, source_target_pairs={{15,0},{31,16},{47,32},{63,48},{79,64},{95,80},{111,96},{127,112},... | collective-permute-start | bytes 221192 | tf_op jit(solution)/shard_map/ppermute | solution.py:534
  18.8 0.7 %collective-permute-start.9 = (bf16[36,4,256]{2,1,0:T(4,128)(2,1)S(1)}, bf16[36,4,256]{2,1,0:T(4,128)(2,1)S(1)}, u32[]{:S(2)}, u32[]{:S(2)}) collective-permute-start(bf16[36,4,256]{2,1,0:T(4,128)(2,1)S(1)} %get-tuple-element.61), channel_id=1, source_target_pairs={{15,16},{31,32},{47,48},{63,64},{79,80},{95,96},{111,112},{127,128... | collective-permute-start | bytes 221192 | tf_op jit(solution)/shard_map/ppermute | solution.py:534
  19.5 0.7 %collective-permute-start.10 = (bf16[36,4,256]{2,1,0:T(4,128)(2,1)S(1)}, bf16[36,4,256]{2,1,0:T(4,128)(2,1)S(1)}, u32[]{:S(2)}, u32[]{:S(2)}) collective-permute-start(bf16[36,4,256]{2,1,0:T(4,128)(2,1)S(1)} %get-tuple-element.62), channel_id=1, source_target_pairs={{15,1008},{31,0},{47,16},{63,32},{79,48},{95,64},{111,80},{127,96}... | collective-permute-start | bytes 221192 | tf_op jit(solution)/shard_map/ppermute | solution.py:534
  20.2 2.3 %collective-permute-done.5.refs_5_ = bf16[36,4,256]{2,1,0:T(4,128)(2,1)S(1)} collective-permute-done((bf16[36,4,256]{2,1,0:T(4,128)(2,1)S(1)}, bf16[36,4,256]{2,1,0:T(4,128)(2,1)S(1)}, u32[]{:S(2)}, u32[]{:S(2)}) %collective-permute-start.5) | collective-permute-done | bytes 73760 | tf_op jit(solution)/shard_map/ppermute | solution.py:597
  22.5 12.0 %conditional.2 = (bf16[60,4,256]{2,1,0:T(4,128)(2,1)}, bf16[60,4,256]{2,1,0:T(4,128)(2,1)}) conditional(s32[]{:T(128)} %convert_element_type.4, () %tuple.18, (bf16[128,4,256]{2,1,0:T(4,128)(2,1)S(1)}, bf16[36,4,256]{2,1,0:T(4,128)(2,1)S(1)}, bf16[72,4,256]{2,1,0:T(4,128)(2,1)S(1)}, bf16[36,4,256]{2,1,0:T(4,128)(2,1)S(1)}) %tuple.24), branch_computations={%region_0.0_spmd, %region_1.0_spmd} | conditional | bytes 983136 | solution.py:613
  22.5 0.4 branch_1_fun.1
  22.9 1.9 %collective-permute-start = (bf16[60,4,256]{2,1,0:T(4,128)(2,1)S(1)}, bf16[60,4,256]{2,1,0:T(4,128)(2,1)}, u32[]{:S(2)}, u32[]{:S(2)}) collective-permute-start(bf16[60,4,256]{2,1,0:T(4,128)(2,1)S(1)} %get-tuple-element.25), channel_id=1, source_target_pairs={{0,16},{16,0},{32,48},{48,32},{64,80},{80,64},{96,112},{112,96},{1... | collective-permute-start | bytes 368648 | tf_op jit(solution)/shard_map/cond/branch_1_fun/ppermute | solution.py:525
  24.8 1.9 %collective-permute-start.1 = (bf16[60,4,256]{2,1,0:T(4,128)(2,1)S(1)}, bf16[60,4,256]{2,1,0:T(4,128)(2,1)}, u32[]{:S(2)}, u32[]{:S(2)}) collective-permute-start(bf16[60,4,256]{2,1,0:T(4,128)(2,1)S(1)} %get-tuple-element.26), channel_id=1, source_target_pairs={{16,32},{32,16},{48,64},{64,48},{80,96},{96,80},{112,128},{128,112... | collective-permute-start | bytes 368648 | tf_op jit(solution)/shard_map/cond/branch_1_fun/ppermute | solution.py:524
  26.7 7.7 %collective-permute-done.1 = bf16[60,4,256]{2,1,0:T(4,128)(2,1)} collective-permute-done((bf16[60,4,256]{2,1,0:T(4,128)(2,1)S(1)}, bf16[60,4,256]{2,1,0:T(4,128)(2,1)}, u32[]{:S(2)}, u32[]{:S(2)}) %collective-permute-start.1) | collective-permute-done | bytes 122912 | tf_op jit(solution)/shard_map/cond/branch_1_fun/ppermute | solution.py:524
  34.4 0.2 shard_map.56
  34.6 0.7 %collective-permute-start.6 = (bf16[36,4,256]{2,1,0:T(4,128)(2,1)S(1)}, bf16[36,4,256]{2,1,0:T(4,128)(2,1)S(1)}, u32[]{:S(2)}, u32[]{:S(2)}) collective-permute-start(bf16[36,4,256]{2,1,0:T(4,128)(2,1)S(1)} %get-tuple-element.53), channel_id=1, source_target_pairs={{8,9},{9,8},{10,11},{11,10},{12,13},{13,12},{14,15},{15,14},{24,25... | collective-permute-start | bytes 221192 | tf_op jit(solution)/shard_map/ppermute | solution.py:627
  35.3 1.3 %collective-permute-start.8 = (bf16[36,4,256]{2,1,0:T(4,128)(2,1)S(1)}, bf16[36,4,256]{2,1,0:T(4,128)(2,1)S(1)}, u32[]{:S(2)}, u32[]{:S(2)}) collective-permute-start(bf16[36,4,256]{2,1,0:T(4,128)(2,1)S(1)} %get-tuple-element.60), channel_id=1, source_target_pairs={{1,15},{17,31},{33,47},{49,63},{65,79},{81,95},{97,111},{113,127},... | collective-permute-start | bytes 221192 | tf_op jit(solution)/shard_map/ppermute | solution.py:626
  36.6 0.7 %shard_map.57.acc_in = f32[512,256]{1,0:T(8,128)S(1)} custom-call(bf16[128,4,256]{2,1,0:T(4,128)(2,1)S(1)} %bitcast.7, f32[16,256]{1,0:T(8,128)S(1)} %get-tuple-element.48.aux), custom_call_target="tpu_custom_call" | custom-call | tf_op jit(solution)/shard_map/pallas_call | solution.py:544
  37.3 0.1 shard_map.59
  37.4 1.1 %collective-permute-done.8.refs_1_.refs_7_ = bf16[36,4,256]{2,1,0:T(4,128)(2,1)S(1)} collective-permute-done((bf16[36,4,256]{2,1,0:T(4,128)(2,1)S(1)}, bf16[36,4,256]{2,1,0:T(4,128)(2,1)S(1)}, u32[]{:S(2)}, u32[]{:S(2)}) %collective-permute-start.8) | collective-permute-done | bytes 73760 | tf_op jit(solution)/shard_map/ppermute | solution.py:626
  38.6 0.4 shard_map.60
  38.9 1.8 %conditional.3 = (bf16[60,4,256]{2,1,0:T(4,128)(2,1)S(1)}, bf16[60,4,256]{2,1,0:T(4,128)(2,1)S(1)}) conditional(s32[]{:T(128)} %convert_element_type.4, (bf16[60,4,256]{2,1,0:T(4,128)(2,1)S(1)}, bf16[60,4,256]{2,1,0:T(4,128)(2,1)S(1)}) %shard_map.60, (bf16[60,4,256]{2,1,0:T(4,128)(2,1)}, bf16[60,4,256]{2,1,0:T(4,128)(2,1)}) %conditional.2), branch_computations={%region_2.0_spmd, %region_3.0_spmd} | conditional | bytes 983136 | solution.py:637
  39.0 0.9 %copy.12 = bf16[60,4,256]{2,1,0:T(4,128)(2,1)S(1)} copy(bf16[60,4,256]{2,1,0:T(4,128)(2,1)} %get-tuple-element.73) | data formatting | bytes 245760 | tf_op jit(solution)/shard_map/cond
  39.9 0.9 %copy.13 = bf16[60,4,256]{2,1,0:T(4,128)(2,1)S(1)} copy(bf16[60,4,256]{2,1,0:T(4,128)(2,1)} %get-tuple-element.74) | data formatting | bytes 245760 | tf_op jit(solution)/shard_map/cond
  40.8 0.6 %shard_map.58 = (f32[512,256]{1,0:T(8,128)S(1)}, f32[32,32]{1,0:T(8,128)S(1)}, f32[32,8]{1,0:T(8,128)S(1)}, f32[2,32,48]{2,1,0:T(8,128)S(1)}, f32[2,32,8]{2,1,0:T(8,128)S(1)}) custom-call(f32[16,256]{1,0:T(8,128)S(1)} %get-tuple-element.48.aux, bf16[72,4,256]{2,1,0:T(4,128)(2,1)S(1)} %collective-permute-done.4.y_low, ...), custom_call_target="tpu_custom_call" | custom-call | tf_op jit(solution)/shard_map/pallas_call | solution.py:544
  41.4 1.6 %shard_map.61 = f32[128,4,256]{2,1,0:T(4,128)} custom-call(f32[32,32]{1,0:T(8,128)S(1)} %get-tuple-element.54.refs_0_, f32[32,8]{1,0:T(8,128)S(1)} %get-tuple-element.55.refs_1_, f32[2,32,48]{2,1,0:T(8,128)S(1)} %get-tuple-element.56.refs_2_, f32[2,32,8]{2,1,0:T(8,128)S(1)} %get-tuple-element.57.refs_3_, f32[512,256]{1,0:T(8,128)S(1)} %get-tuple-element.58.refs_4_, ...), custom_call_target="tpu_custom_call" | custom-call | tf_op jit(solution)/shard_map/pallas_call | solution.py:544
  (8 shorter events, 0.0 us)
Async XLA Ops:
  0.0 22.5 %copy-start = (bf16[4,4,8,4,256]{4,3,2,1,0:T(4,128)(2,1)S(1)}, bf16[4,4,8,4,256]{4,3,2,1,0:T(4,128)(2,1)}, u32[]{:S(2)}) copy-start(bf16[4,4,8,4,256]{4,3,2,1,0:T(4,128)(2,1)} %param.10) | copy-start | bytes 786436
  2.0 20.5 %collective-permute-start.4 = (bf16[72,4,256]{2,1,0:T(4,128)(2,1)S(1)}, bf16[72,4,256]{2,1,0:T(4,128)(2,1)S(1)}, u32[]{:S(2)}, u32[]{:S(2)}) collective-permute-start(bf16[72,4,256]{2,1,0:T(4,128)(2,1)S(1)} %get-tuple-element.49), channel_id=1, source_target_pairs={{0,1},{1,0},{2,3},{3,2},{4,5},{5,4},{6,7},{7,6},{16,17},{17,16},{1... | collective-permute-start | bytes 442376 | tf_op jit(solution)/shard_map/ppermute | solution.py:596
  16.2 6.2 %collective-permute-start.5 = (bf16[36,4,256]{2,1,0:T(4,128)(2,1)S(1)}, bf16[36,4,256]{2,1,0:T(4,128)(2,1)S(1)}, u32[]{:S(2)}, u32[]{:S(2)}) collective-permute-start(bf16[36,4,256]{2,1,0:T(4,128)(2,1)S(1)} %get-tuple-element.50.refs_3_), channel_id=1, source_target_pairs={{1,2},{2,1},{3,4},{4,3},{5,6},{6,5},{7,8},{8,7},{9,10},{10,9},{11,... | collective-permute-start | bytes 221192 | tf_op jit(solution)/shard_map/ppermute | solution.py:597
  18.1 19.1 %collective-permute-start.7 = (bf16[36,4,256]{2,1,0:T(4,128)(2,1)S(1)}, bf16[36,4,256]{2,1,0:T(4,128)(2,1)S(1)}, u32[]{:S(2)}, u32[]{:S(2)}) collective-permute-start(bf16[36,4,256]{2,1,0:T(4,128)(2,1)S(1)} %get-tuple-element.59), channel_id=1, source_target_pairs={{15,0},{31,16},{47,32},{63,48},{79,64},{95,80},{111,96},{127,112},... | collective-permute-start | bytes 221192 | tf_op jit(solution)/shard_map/ppermute | solution.py:534
  18.8 18.5 %collective-permute-start.9 = (bf16[36,4,256]{2,1,0:T(4,128)(2,1)S(1)}, bf16[36,4,256]{2,1,0:T(4,128)(2,1)S(1)}, u32[]{:S(2)}, u32[]{:S(2)}) collective-permute-start(bf16[36,4,256]{2,1,0:T(4,128)(2,1)S(1)} %get-tuple-element.61), channel_id=1, source_target_pairs={{15,16},{31,32},{47,48},{63,64},{79,80},{95,96},{111,112},{127,128... | collective-permute-start | bytes 221192 | tf_op jit(solution)/shard_map/ppermute | solution.py:534
  19.5 17.8 %collective-permute-start.10 = (bf16[36,4,256]{2,1,0:T(4,128)(2,1)S(1)}, bf16[36,4,256]{2,1,0:T(4,128)(2,1)S(1)}, u32[]{:S(2)}, u32[]{:S(2)}) collective-permute-start(bf16[36,4,256]{2,1,0:T(4,128)(2,1)S(1)} %get-tuple-element.62), channel_id=1, source_target_pairs={{15,1008},{31,0},{47,16},{63,32},{79,48},{95,64},{111,80},{127,96}... | collective-permute-start | bytes 221192 | tf_op jit(solution)/shard_map/ppermute | solution.py:534
  22.9 3.9 %collective-permute-start = (bf16[60,4,256]{2,1,0:T(4,128)(2,1)S(1)}, bf16[60,4,256]{2,1,0:T(4,128)(2,1)}, u32[]{:S(2)}, u32[]{:S(2)}) collective-permute-start(bf16[60,4,256]{2,1,0:T(4,128)(2,1)S(1)} %get-tuple-element.25), channel_id=1, source_target_pairs={{0,16},{16,0},{32,48},{48,32},{64,80},{80,64},{96,112},{112,96},{1... | collective-permute-start | bytes 368648 | tf_op jit(solution)/shard_map/cond/branch_1_fun/ppermute | solution.py:525
  24.8 9.6 %collective-permute-start.1 = (bf16[60,4,256]{2,1,0:T(4,128)(2,1)S(1)}, bf16[60,4,256]{2,1,0:T(4,128)(2,1)}, u32[]{:S(2)}, u32[]{:S(2)}) collective-permute-start(bf16[60,4,256]{2,1,0:T(4,128)(2,1)S(1)} %get-tuple-element.26), channel_id=1, source_target_pairs={{16,32},{32,16},{48,64},{64,48},{80,96},{96,80},{112,128},{128,112... | collective-permute-start | bytes 368648 | tf_op jit(solution)/shard_map/cond/branch_1_fun/ppermute | solution.py:524
  34.6 2.8 %collective-permute-start.6 = (bf16[36,4,256]{2,1,0:T(4,128)(2,1)S(1)}, bf16[36,4,256]{2,1,0:T(4,128)(2,1)S(1)}, u32[]{:S(2)}, u32[]{:S(2)}) collective-permute-start(bf16[36,4,256]{2,1,0:T(4,128)(2,1)S(1)} %get-tuple-element.53), channel_id=1, source_target_pairs={{8,9},{9,8},{10,11},{11,10},{12,13},{13,12},{14,15},{15,14},{24,25... | collective-permute-start | bytes 221192 | tf_op jit(solution)/shard_map/ppermute | solution.py:627
  35.3 3.3 %collective-permute-start.8 = (bf16[36,4,256]{2,1,0:T(4,128)(2,1)S(1)}, bf16[36,4,256]{2,1,0:T(4,128)(2,1)S(1)}, u32[]{:S(2)}, u32[]{:S(2)}) collective-permute-start(bf16[36,4,256]{2,1,0:T(4,128)(2,1)S(1)} %get-tuple-element.60), channel_id=1, source_target_pairs={{1,15},{17,31},{33,47},{49,63},{65,79},{81,95},{97,111},{113,127},... | collective-permute-start | bytes 221192 | tf_op jit(solution)/shard_map/ppermute | solution.py:626

commit v6 on v4

v6 whole, which is shorter than its diff:
```python
import functools

import jax
import jax.numpy as jnp
from jax import lax
from jax.experimental import pallas as pl
from jax.experimental.pallas import tpu as pltpu
from jax.sharding import PartitionSpec as P

ONSITE_S = -0.22
ONSITE_P = 0.27
HOP_SS = -0.37
HOP_SP = 0.35
HOP_PPS = 0.4
HOP_PPP = -0.114
BOND_LENGTH = 1.536
LATTICE_STEP = 1.6

SIDE = 4
DEPTH = 8
ATOMS = SIDE * SIDE * DEPTH
FACE = SIDE * DEPTH
WIDE = FACE + 2 * DEPTH
NV = 256
LANES = NV // 2
POS_ROWS = 9
LIST_ROWS = 6
AUX = 4
BLOCK = DEPTH + AUX
PLACE = (DEPTH, 0, 3 * DEPTH + AUX, 2 * DEPTH + AUX)
X_AUX = 2 * DEPTH
X_SITES = FACE + AUX
Y_BLOCK = (FACE + AUX, FACE + AUX + BLOCK)
Y_SITES = WIDE + 3 * AUX
STEPS = [(x, y) for x in (-1, 0, 1) for y in (-1, 0, 1)]
F32 = jnp.float32
BF16 = jnp.bfloat16


def iota(shape, axis):
    return lax.broadcasted_iota(jnp.int32, shape, axis)


def onehot(values, expected):
    wide = [jnp.where(row == expected, 1.0, 0.0).astype(BF16) for row in values]
    return wide[0] if len(wide) == 1 else jnp.concatenate(wide, axis=1)


def dot_nt(a, b):
    return lax.dot_general(a, b, (((1,), (1,)), ((), ())), preferred_element_type=F32)


def dot(a, b):
    return jnp.dot(a, b, preferred_element_type=F32)


def list_of(rows):
    first = [rows[k : k + 1] for k in range(2)]
    key = [rows[4 + k : 5 + k] * float(ATOMS) + rows[2 + k : 3 + k] for k in range(2)]
    return first, key


def code(step_x, step_y):
    return (step_x + 1) * 3 + step_y + 1


def hopping(dx, dy, dz, count):
    square = jnp.maximum(dx * dx + dy * dy + dz * dz, 0.5)
    inverse = lax.rsqrt(square)
    cosines = [d * inverse for d in (dx, dy, dz)]
    ratio = BOND_LENGTH * inverse
    radial = ratio * ratio * jnp.exp(1.0 - square * inverse * (1.0 / BOND_LENGTH))

    def final(value):
        return (value.astype(BF16).astype(F32) * count).astype(BF16)

    grid = [[None] * 4 for _ in range(4)]
    grid[0][0] = final(HOP_SS * radial)
    for a in range(3):
        across = final(HOP_SP * radial * cosines[a])
        grid[0][1 + a] = across
        grid[1 + a][0] = -across
        for b in range(a, 3):
            entry = (HOP_PPS - HOP_PPP) * cosines[a] * cosines[b]
            if a == b:
                entry = entry + HOP_PPP
            grid[1 + a][1 + b] = grid[1 + b][1 + a] = final(entry * radial)
    return grid


def planes_of(wave, block):
    n = block.shape[0]
    wide = block.astype(F32).reshape(n // 2, 2, 4, NV)
    wide = jnp.concatenate([wide[:, 0], wide[:, 1]], axis=1).reshape(4 * n, NV)
    for h in range(2):
        wave[h, : 4 * n] = wide[:, h * LANES : (h + 1) * LANES]
    halves = [[wave[h, pl.ds(b, n, stride=4), :] for h in range(2)] for b in range(4)]
    return [jnp.concatenate(pair, axis=1) for pair in halves]


def applied(grid, planes):
    total = None
    for b in range(4):
        stacked = jnp.concatenate([grid[a][b] for a in range(4)], axis=0)
        part = dot(stacked, planes[b].astype(BF16))
        total = part if total is None else total + part
    return total


def atoms_of(planes, wave):
    n = planes[0].shape[0]
    for a in range(4):
        for h in range(2):
            wave[h, pl.ds(a, n, stride=4), :] = planes[a][:, h * LANES : (h + 1) * LANES]
    wide = jnp.concatenate([wave[h, : 4 * n] for h in range(2)], axis=1)
    wide = wide.reshape(n // 2, 8, NV)
    return jnp.stack([wide[:, :4], wide[:, 4:]], axis=1).reshape(n, 4, NV)


def turned(points):
    n = points.shape[1]
    return jnp.concatenate([points, jnp.zeros((5, n), F32)], axis=0).T


def picked_rows(pick, points):
    total = None
    for _ in range(3):
        piece = points.astype(BF16)
        part = dot(pick, piece)
        total = part if total is None else total + part
        points = points - piece.astype(F32)
    return total


def z_shift(zi, zj):
    step = zj - zi
    period = LATTICE_STEP * DEPTH
    return jnp.where(step > 1.5, -period, jnp.where(step < -1.5, period, 0.0))


def wrap(place, across, side, period):
    high = jnp.where((side > 0) & (place == across - 1), period, 0.0)
    return jnp.where((side < 0) & (place == 0), -period, high)


def place_of(sizes):
    return lax.axis_index("gx"), lax.axis_index("gy"), *sizes


def side_of(place):
    first = 1 - 2 * (place & 1)
    return first, -first


def faces_of(side):
    mine = jnp.where(side > 0, SIDE - 1, 0)
    return mine, SIDE - 1 - mine


def sum_of(*readers):
    def read(at):
        total = None
        for reader in readers:
            value = reader(at)
            total = value if total is None else total + value
        return total

    return read


def reader_of(message, first=0):
    return lambda at: message[pl.ds(first + at[0], at[1])].astype(F32)


def aux_of(read, first):
    sites = read((first, AUX))
    return jnp.concatenate([sites[k] for k in range(AUX)], axis=0)


def points_of(rows):
    return rows[0:3] + rows[3:6] + rows[6:9]


def pack_x(sizes, trial, positions, atoms, owner, count, one, two, aux, pos, pairs, owners, sem):
    at_x, at_y, across_x, across_y = place_of(sizes)
    copies = [
        pltpu.make_async_copy(a, b, sem.at[k])
        for k, (a, b) in enumerate(((positions, pos), (atoms, pairs), (owner, owners)))
    ]
    for side, out in zip(side_of(at_x), (one, two)):
        face, _ = faces_of(side)
        for y in range(SIDE):
            begin = (face * SIDE + y) * DEPTH
            part = out.at[pl.ds(PLACE[y], DEPTH)]
            copies.append(
                pltpu.make_async_copy(trial.at[pl.ds(begin, DEPTH)], part, sem.at[len(copies)])
            )
    for copy in copies:
        copy.start()
    rows = 3 * SIDE * SIDE
    tile = (iota((DEPTH, ATOMS), 1) & (DEPTH - 1)) == iota((DEPTH, ATOMS), 0)
    tile = jnp.where(tile, 1.0, 0.0).astype(BF16)
    row = iota((3 * rows, ATOMS), 0)
    keep = (row & (SIDE * SIDE - 1)) == (iota((3 * rows, ATOMS), 1) >> 3)
    gather = (iota((16, 3 * rows), 1) >> 4) == iota((16, 3 * rows), 0)
    gather = jnp.where(gather, 1.0, 0.0).astype(BF16)
    aux[:, ATOMS:] = jnp.zeros((4 * AUX, NV - ATOMS), F32)
    for copy in copies[:3]:
        copy.wait()
    rest = pos[...]
    parts = []
    for _ in range(3):
        piece = rest.astype(BF16)
        parts.append(piece)
        rest = rest - piece.astype(F32)
    spread = dot(jnp.concatenate(parts, axis=0), tile)
    aux[:, :ATOMS] = dot(gather, jnp.where(keep, spread, 0.0).astype(BF16))
    whose = owners[...]
    step = jnp.zeros(whose.shape, F32)
    for x, y in STEPS:
        name = lax.rem(at_x + x + across_x, across_x) * across_y
        name = name + lax.rem(at_y + y + across_y, across_y)
        step = jnp.where(whose == name, float(code(x, y)), step)
    live = iota(whose.shape, 1) < count[0, 0]
    first = jnp.where(live, pairs[0:1], -1).astype(F32)
    second = pairs[1:2].astype(F32)
    for k, values in enumerate((first, second, step)):
        for h in range(2):
            at = POS_ROWS + 2 * k + h
            aux[at : at + 1] = values[:, h * NV : (h + 1) * NV]
    for k in range(AUX):
        site = aux[4 * k : 4 * k + 4].astype(BF16)
        for out in (one, two):
            out[X_AUX + k] = site
    for copy in copies[3:]:
        copy.wait()


def own(sizes, trial, aux, acc, low, two, top, wave):
    first, second = side_of(place_of(sizes)[1])
    for side, outs in ((first, (low, top)), (second, (two,))):
        face, _ = faces_of(side)
        for out in outs:
            for x in range(SIDE):
                begin = (x * SIDE + face) * DEPTH
                out[x * DEPTH : (x + 1) * DEPTH] = trial[pl.ds(begin, DEPTH)]
            for k in range(AUX):
                out[FACE + k] = aux[4 * k : 4 * k + 4].astype(BF16)
    rows = aux[...]
    first, key = list_of(rows[POS_ROWS : POS_ROWS + LIST_ROWS])
    atom = iota((ATOMS, 1), 0)
    is_first = onehot(first, atom.astype(F32))
    is_second = onehot(key, (atom + code(0, 0) * ATOMS).astype(F32))
    count = dot_nt(is_first, is_second) + dot_nt(is_second, is_first)
    pos = points_of(rows)[:, :ATOMS]
    pos_t = turned(pos)
    zi = (atom & (DEPTH - 1)).astype(F32)
    zj = (iota((1, ATOMS), 1) & (DEPTH - 1)).astype(F32)
    dx, dy = (pos[a : a + 1] - pos_t[:, a : a + 1] for a in range(2))
    dz = (pos[2:3] + z_shift(zi, zj)) - pos_t[:, 2:3]
    grid = hopping(dx, dy, dz, count)
    planes = planes_of(wave, trial[...])
    matrix = jnp.concatenate([jnp.concatenate(line, axis=1) for line in grid], axis=0)
    part = dot(matrix, jnp.concatenate(planes, axis=0).astype(BF16))
    for a in range(4):
        onsite = ONSITE_P if a else ONSITE_S
        rows = slice(a * ATOMS, (a + 1) * ATOMS)
        acc[rows] = onsite * planes[a] + part[rows]


def corners(sizes, x_two, x_one, low_in, two_in, top_in, low, two, top, sem):
    del low_in, two_in, top_in
    first, second = side_of(place_of(sizes)[1])
    copies = []
    for side, out in ((first, low), (second, two), (first, top)):
        face, _ = faces_of(side)
        begin = jnp.where(face == 0, PLACE[0], X_AUX)
        for n, message in enumerate((x_one, x_two)):
            part = out.at[pl.ds(Y_BLOCK[n], BLOCK)]
            copies.append(
                pltpu.make_async_copy(message.at[pl.ds(begin, BLOCK)], part, sem.at[len(copies)])
            )
            copies[-1].start()
    for copy in copies:
        copy.wait()


def own_of(aux):
    rows = aux[...]
    return *list_of(rows[POS_ROWS : POS_ROWS + LIST_ROWS]), turned(points_of(rows)[:, :ATOMS])


def pick_rows(atom, pos_t):
    return picked_rows(jnp.where(iota((FACE, ATOMS), 1) == atom, 1.0, 0.0).astype(BF16), pos_t)


def x_part(period, sizes, side, read, own_first, own_key, pos_t, wave):
    at_x, _, across_x, _ = place_of(sizes)
    mine, theirs = faces_of(side)
    k = iota((FACE, 1), 0)
    my_atom = mine * FACE + k
    their_atom = theirs * FACE + (k ^ DEPTH)
    rows = aux_of(read, X_AUX)
    first, key = list_of(rows[POS_ROWS : POS_ROWS + LIST_ROWS])
    left = [
        onehot(own_first, my_atom.astype(F32)),
        onehot(key, (my_atom + ((1 - side) * 3 + 1) * ATOMS).astype(F32)),
    ]
    right = [
        onehot(own_key, (their_atom + ((side + 1) * 3 + 1) * ATOMS).astype(F32)),
        onehot(first, their_atom.astype(F32)),
    ]
    count = dot_nt(jnp.concatenate(left, axis=1), jnp.concatenate(right, axis=1))
    lane = theirs * FACE + (iota((ATOMS, FACE), 1) ^ DEPTH)
    pick = jnp.where(iota((ATOMS, FACE), 0) == lane, 1.0, 0.0).astype(BF16)
    points = points_of(dot(rows[:, :ATOMS].astype(BF16), pick))
    mine_t = pick_rows(my_atom, pos_t)
    zi = (k & (DEPTH - 1)).astype(F32)
    zj = (iota((1, FACE), 1) & (DEPTH - 1)).astype(F32)
    dx = (points[0:1] + wrap(at_x, across_x, side, period)) - mine_t[:, 0:1]
    dy = points[1:2] - mine_t[:, 1:2]
    dz = (points[2:3] + z_shift(zi, zj)) - mine_t[:, 2:3]
    grid = hopping(dx, dy, dz, count)
    half = 2 * DEPTH
    block = jnp.concatenate([read((0, half)), read((half + AUX, half))], axis=0)
    return applied(grid, planes_of(wave, block))


def ghost(theirs, x_sides, shape, axis):
    at = iota(shape, axis)
    part = jnp.where(at < FACE, 0, jnp.where(at < FACE + DEPTH, 1, 2))
    step = jnp.where(part == 0, 0, jnp.where(part == 1, x_sides[0], x_sides[1]))
    layer = jnp.where(part == 0, at >> 3, jnp.where(step > 0, 0, SIDE - 1))
    return layer * FACE + theirs * DEPTH + (at & (DEPTH - 1)), step, part


def y_atoms(side):
    mine, _ = faces_of(side)
    k = iota((FACE, 1), 0)
    return (k >> 3) * FACE + mine * DEPTH + (k & (DEPTH - 1))


def first_half(periods, sizes, aux, x_two, x_one, acc_in, acc, forward, mine_y, wave, other_wave):
    at_x, at_y, _, _ = place_of(sizes)
    own_first, own_key, pos_t = own_of(aux)
    x_sides = side_of(at_x)
    parts = [
        x_part(periods[0], sizes, side, reader_of(message), own_first, own_key, pos_t, scratch)
        for side, message, scratch in zip(x_sides, (x_one, x_two), (wave, other_wave))
    ]
    for n, side in enumerate(side_of(at_y)):
        _, theirs = faces_of(side)
        my_atom = y_atoms(side)
        their_atom, step, _ = ghost(theirs, x_sides, (WIDE, 1), 0)
        target = their_atom + ((step + 1) * 3 + side + 1) * ATOMS
        left = onehot(own_first, my_atom.astype(F32))
        forward[n] = dot_nt(left, onehot(own_key, target.astype(F32)))
        mine_y[n] = pick_rows(my_atom, pos_t)
    acc[...] = acc_in[...]
    for side, part in zip(x_sides, parts):
        mine, _ = faces_of(side)
        for a in range(4):
            at = pl.multiple_of(a * ATOMS + mine * FACE, FACE)
            acc[pl.ds(at, FACE)] += part[a * FACE : (a + 1) * FACE]


def y_part(periods, sizes, side, read, forward, mine_t, wave):
    at_x, at_y, across_x, across_y = place_of(sizes)
    _, theirs = faces_of(side)
    x_sides = side_of(at_x)
    corner_at = jnp.where(theirs == 0, 0, AUX)
    aux_at = jnp.where(theirs == 0, DEPTH, 0)
    my_atom = y_atoms(side)
    their_atom, _, part = ghost(theirs, x_sides, (WIDE, 1), 0)
    lane_atom, _, lane_part = ghost(theirs, x_sides, (ATOMS, WIDE), 1)
    left, right, picks, placed = [], [], [], []
    for m, x in enumerate((0, *x_sides)):
        rows = aux_of(read, Y_BLOCK[m - 1] + aux_at if m else FACE)
        listed, key = list_of(rows[POS_ROWS : POS_ROWS + LIST_ROWS])
        wanted = my_atom + ((1 - x) * 3 + 1 - side) * ATOMS
        left.append(onehot(key, wanted.astype(F32)))
        right.append(onehot(listed, jnp.where(part == m, their_atom, -2).astype(F32)))
        pick = (iota((ATOMS, WIDE), 0) == lane_atom) & (lane_part == m)
        picks.append(jnp.where(pick, 1.0, 0.0).astype(BF16))
        placed.append(rows[:, :ATOMS].astype(BF16))
    count = forward + dot_nt(jnp.concatenate(left, axis=1), jnp.concatenate(right, axis=1))
    points = points_of(dot(jnp.concatenate(placed, axis=1), jnp.concatenate(picks, axis=0)))
    lane = iota((1, WIDE), 1)
    zi = (iota((FACE, 1), 0) & (DEPTH - 1)).astype(F32)
    zj = (lane & (DEPTH - 1)).astype(F32)
    shifts = [wrap(at_x, across_x, x, periods[0]) for x in x_sides]
    shift_x = jnp.where(lane < FACE, 0.0, jnp.where(lane < FACE + DEPTH, *shifts))
    dx = (points[0:1] + shift_x) - mine_t[:, 0:1]
    dy = (points[1:2] + wrap(at_y, across_y, side, periods[1])) - mine_t[:, 1:2]
    dz = (points[2:3] + z_shift(zi, zj)) - mine_t[:, 2:3]
    grid = hopping(dx, dy, dz, count)
    block = [read((0, FACE))] + [read((Y_BLOCK[m] + corner_at, DEPTH)) for m in range(2)]
    return applied(grid, planes_of(wave, jnp.concatenate(block, axis=0)))


def y_rows(side):
    mine, _ = faces_of(side)
    return [(x * SIDE + mine) * DEPTH for x in range(SIDE)]


def second_half(periods, sizes, forward, mine_y, acc, low, faces, done, sums, wave, store):
    sides = side_of(place_of(sizes)[1])
    part = y_part(periods, sizes, sides[0], reader_of(low), forward[0], mine_y[0], wave)
    sums[...] = acc[...]
    for a in range(4):
        for x, row in enumerate(y_rows(sides[0])):
            at = pl.multiple_of(a * ATOMS + row, DEPTH)
            begin = a * FACE + x * DEPTH
            sums[pl.ds(at, DEPTH)] += part[begin : begin + DEPTH]
    done[...] = atoms_of([sums[a * ATOMS : (a + 1) * ATOMS] for a in range(4)], store)
    for n, side in enumerate(sides):
        for a in range(4):
            for x, row in enumerate(y_rows(side)):
                at = pl.multiple_of(a * ATOMS + row, DEPTH)
                begin = a * FACE + x * DEPTH
                faces[n, begin : begin + DEPTH] = sums[pl.ds(at, DEPTH)]


def last_face(periods, sizes, forward, mine_y, faces, done, two, top, out, results, wave, store, sem):
    _, at_y, _, across_y = place_of(sizes)
    lower = at_y < across_y // 4 * 2
    sides = side_of(at_y)
    copies = []

    def copy_of(source, begin, row, count):
        return pltpu.make_async_copy(
            source.at[pl.ds(begin, count)], out.at[pl.ds(row, count)], sem.at[len(copies)]
        )

    def total_of(n, message, scratch):
        read = reader_of(message)
        part = faces[n] + y_part(periods, sizes, sides[n], read, forward[n], mine_y[n], scratch)
        return atoms_of([part[a * FACE : (a + 1) * FACE] for a in range(4)], scratch)

    for x in range(SIDE):
        row = x * FACE + DEPTH
        copies.append(copy_of(done, row, row, FACE - 2 * DEPTH))
        copies[-1].start()
    for row in y_rows(sides[0]):
        copies.append(copy_of(done, row, row, DEPTH))
    firsts = copies[SIDE:]

    @pl.when(lower)
    def _():
        for copy in firsts:
            copy.start()

    results[1] = total_of(1, two, wave)
    for x, row in enumerate(y_rows(sides[1])):
        copies.append(copy_of(results.at[1], x * DEPTH, row, DEPTH))
        copies[-1].start()

    @pl.when(jnp.logical_not(lower))
    def _():
        results[0] = total_of(0, top, store)
        for x, row in enumerate(y_rows(sides[0])):
            pltpu.make_async_copy(
                results.at[0, pl.ds(x * DEPTH, DEPTH)],
                out.at[pl.ds(row, DEPTH)],
                sem.at[SIDE + x],
            ).start()

    for copy in copies:
        copy.wait()


def swap(count, begin):
    pairs = []
    for i in range(begin, count + begin, 2):
        a, b = i % count, (i + 1) % count
        pairs += [(a, b), (b, a)]
    return pairs


def exchange_x(one, two):
    count = lax.axis_size("gx")
    two = lax.ppermute(two, "gx", swap(count, 1))
    one = lax.ppermute(one, "gx", swap(count, 0))
    return one, two


def exchange_y(low, two, top):
    count = lax.axis_size("gy")
    pairs = swap(count, 0)
    begin = count // 4 * 2
    low = lax.ppermute(low, "gy", pairs[:begin])
    two = lax.ppermute(two, "gy", swap(count, 1))
    top = lax.ppermute(top, "gy", pairs[begin:])
    return low, two, top


VMEM = pl.BlockSpec(memory_space=pltpu.VMEM)
SMEM = pl.BlockSpec(memory_space=pltpu.SMEM)
HBM = pl.BlockSpec(memory_space=pltpu.HBM)
ANY = pl.BlockSpec(memory_space=pl.ANY)


def call(kernel, inputs, outputs, in_space=VMEM, out_space=VMEM, **options):
    return pl.pallas_call(
        kernel,
        out_shape=outputs,
        in_specs=in_space if isinstance(in_space, list) else [in_space] * len(inputs),
        out_specs=[out_space] * len(outputs),
        compiler_params=pltpu.CompilerParams(vmem_limit_bytes=16 * 1024 * 1024),
        **options,
    )(*inputs)


def shards(trial, positions, pair_atoms, pair_owner, pair_image, pair_count):
    sizes = across_x, across_y = lax.axis_size("gx"), lax.axis_size("gy")
    periods = tuple(LATTICE_STEP * (SIDE * count) for count in sizes)
    mine = trial.reshape(ATOMS, 4, NV)
    slots = pair_owner.shape[2]

    def message(sites):
        return jax.ShapeDtypeStruct((sites, 4, NV), BF16)

    def floats(*shape):
        return jax.ShapeDtypeStruct(shape, F32)

    def wave(rows):
        return pltpu.VMEM((2, rows, LANES), F32)

    *x_out, aux = call(
        functools.partial(pack_x, sizes),
        tuple(
            pltpu.with_memory_space_constraint(array, pltpu.HBM)
            for array in (
                mine,
                positions.reshape(3 * SIDE * SIDE, DEPTH),
                pair_atoms.reshape(2, slots),
                pair_owner.reshape(1, slots),
            )
        )
        + (pair_count,),
        [message(X_SITES)] * 2 + [floats(4 * AUX, NV)],
        in_space=[HBM] * 4 + [SMEM],
        scratch_shapes=[
            pltpu.VMEM((3 * SIDE * SIDE, DEPTH), F32),
            pltpu.VMEM((2, slots), jnp.int32),
            pltpu.VMEM((1, slots), jnp.int32),
            pltpu.SemaphoreType.DMA((3 + 2 * SIDE,)),
        ],
    )
    x_one, x_two = exchange_x(*x_out)
    acc, *y_out = call(
        functools.partial(own, sizes),
        (mine, aux),
        [floats(4 * ATOMS, NV)] + [message(Y_SITES)] * 3,
        scratch_shapes=[wave(4 * ATOMS)],
    )
    y_out = call(
        functools.partial(corners, sizes),
        (x_two, x_one, *y_out),
        [message(Y_SITES)] * 3,
        in_space=ANY,
        out_space=ANY,
        input_output_aliases={2: 0, 3: 1, 4: 2},
        scratch_shapes=[pltpu.SemaphoreType.DMA((6,))],
    )
    low, two, top = exchange_y(*y_out)
    acc, forward, mine_y = call(
        functools.partial(first_half, periods, sizes),
        (aux, x_two, x_one, acc),
        [floats(4 * ATOMS, NV), floats(2, FACE, WIDE), floats(2, FACE, 8)],
        scratch_shapes=[wave(4 * FACE)] * 2,
    )
    faces, done = call(
        functools.partial(second_half, periods, sizes),
        (forward, mine_y, acc, low),
        [floats(2, 4 * FACE, NV), floats(ATOMS, 4, NV)],
        scratch_shapes=[
            pltpu.VMEM((4 * ATOMS, NV), F32),
            wave(4 * WIDE),
            wave(4 * ATOMS),
        ],
    )
    (product,) = call(
        functools.partial(last_face, periods, sizes),
        (forward, mine_y, faces, done, two, top),
        [floats(ATOMS, 4, NV)],
        out_space=HBM,
        scratch_shapes=[
            pltpu.VMEM((2, FACE, 4, NV), F32),
            wave(4 * WIDE),
            wave(4 * WIDE),
            pltpu.SemaphoreType.DMA((3 * SIDE,)),
        ],
    )
    return product.reshape(trial.shape)


def solution(mesh):
    in_specs = (
        P("gx", "gy", None, None, None),
        P(None, "gx", "gy", None),
        P("gx", "gy", None, None),
        P("gx", "gy", None),
        P("gx", "gy", None, None),
        P("gx", "gy"),
    )
    out_specs = P("gx", "gy", None, None, None)
    return jax.shard_map(shards, mesh=mesh, in_specs=in_specs, out_specs=out_specs, check_vma=False)
```

time: 35.8 us -> 36.9 us (1.031)
  waiting for transfers between devices: 0.53 us -> 1.36 us
    ppermute x2, starting transfers between devices: 9.6 us -> 18 us  [the longest x1 13.5 us: exchange_x(): one = lax.ppermute(one, 'gx', swap(count, 0))]
    ppermute x1, starting transfers between devices: 14.6 us -> 9.14 us  [exchange_y(): two = lax.ppermute(two, 'gy', swap(count, 1))]
    ppermute x1, starting transfers between devices: 4.83 us -> 1.92 us  [exchange_y(): low = lax.ppermute(low, 'gy', pairs[:begin])]
    ppermute x1, waiting for transfers between devices: 0.35 us -> 1.16 us  [exchange_y(): two = lax.ppermute(two, 'gy', swap(count, 1))]
    pallas_call x5 -> x6, Pallas kernels: 4.48 us -> 4.77 us  [call(): pl.pallas_call(kernel, out_shape=outputs, in_specs=in_space if isinstance...]
  transfers between devices with their start and end apart: 5 -> 5, of which waited for: 2 -> 2; matrix products, arithmetic and copies ran while one was open for 0% -> 0% of each run, Pallas kernels for 4% -> 6%
where the time goes in v6:
time: 36.9 us; the launch traced here: 36.6 us
  starting transfers between devices  29.7 us (80%)
  Pallas kernels  4.77 us (13%)
  waiting for transfers between devices  1.36 us (4%)
  between operations  0.8 us (2%)
    ppermute x1, starting transfers between devices, exchange_x(): one = lax.ppermute(one, 'gx', swap(count, 0))  13.5 us
    ppermute x1, starting transfers between devices, exchange_y(): two = lax.ppermute(two, 'gy', swap(count, 1))  9.14 us
    pallas_call x6, Pallas kernels, call(): pl.pallas_call(kernel, out_shape=outputs, in_specs=in_space if isinstance...  4.77 us
    ppermute x1, starting transfers between devices, exchange_x(): two = lax.ppermute(two, 'gx', swap(count, 1))  4.51 us
    ppermute x1, starting transfers between devices, exchange_y(): low = lax.ppermute(low, 'gy', pairs[:begin])  1.92 us
    ppermute x1, waiting for transfers between devices, exchange_y(): two = lax.ppermute(two, 'gy', swap(count, 1))  1.16 us
  transfers between devices with their start and end apart: 5, of which 2 were waited for; matrix products, arithmetic and copies ran while one was open for 0% of the time, Pallas kernels for 6%

profile of v6, /device:TPU:1, one launch (start us, length us, event | category | flops | bytes accessed | tf_op | source)
XLA Modules:
  0.0 36.6 jit_solution(4183713500879565062)
XLA Ops:
  0.0 0.0 copy-start
  0.7 1.1 %shard_map.55 = (bf16[36,4,256]{2,1,0:T(4,128)(2,1)S(1)}, bf16[36,4,256]{2,1,0:T(4,128)(2,1)S(1)}, f32[16,256]{1,0:T(8,128)S(1)}) custom-call(bf16[128,4,256]{2,1,0:T(4,128)(2,1)} %bitcast.5, f32[48,8]{1,0:T(8,128)} %bitcast.7, s32[2,512]{1,0:T(2,128)} %bitcast.8, s32[1,512]{1,0:T(1,128)} %bitcast.9, s32[1,1]{1,0:T(1,128)S(6)} %copy.12.count), custom_call_target="tpu_custom_call" | custom-call | tf_op jit(solution)/shard_map/pallas_call | solution.py:504
  1.8 4.5 %collective-permute-start = (bf16[36,4,256]{2,1,0:T(4,128)(2,1)S(1)}, bf16[36,4,256]{2,1,0:T(4,128)(2,1)S(1)}, u32[]{:S(2)}, u32[]{:S(2)}) collective-permute-start(bf16[36,4,256]{2,1,0:T(4,128)(2,1)S(1)} %get-tuple-element.21), channel_id=1, source_target_pairs={{16,32},{32,16},{48,64},{64,48},{80,96},{96,80},{112,128},{128,112... | collective-permute-start | bytes 221192 | tf_op jit(solution)/shard_map/ppermute | solution.py:482
  6.4 13.5 %collective-permute-start.1 = (bf16[36,4,256]{2,1,0:T(4,128)(2,1)S(1)}, bf16[36,4,256]{2,1,0:T(4,128)(2,1)S(1)}, u32[]{:S(2)}, u32[]{:S(2)}) collective-permute-start(bf16[36,4,256]{2,1,0:T(4,128)(2,1)S(1)} %get-tuple-element.22), channel_id=1, source_target_pairs={{0,16},{16,0},{32,48},{48,32},{64,80},{80,64},{96,112},{112,96},{1... | collective-permute-start | bytes 221192 | tf_op jit(solution)/shard_map/ppermute | solution.py:483
  19.8 0.0 copy-done
  19.8 0.7 %shard_map.56 = (f32[512,256]{1,0:T(8,128)S(1)}, bf16[60,4,256]{2,1,0:T(4,128)(2,1)S(1)}, bf16[60,4,256]{2,1,0:T(4,128)(2,1)S(1)}, bf16[60,4,256]{2,1,0:T(4,128)(2,1)S(1)}) custom-call(bf16[128,4,256]{2,1,0:T(4,128)(2,1)S(1)} %bitcast.6, f32[16,256]{1,0:T(8,128)S(1)} %get-tuple-element.20.aux), custom_call_target="tpu_custom_call" | custom-call | tf_op jit(solution)/shard_map/pallas_call | solution.py:504
  20.5 0.0 collective-permute-done.x_two
  20.5 0.2 collective-permute-done.1.x_one
  20.7 0.2 shard_map.58
  21.0 1.9 %collective-permute-start.2 = (bf16[60,4,256]{2,1,0:T(4,128)(2,1)S(1)}, bf16[60,4,256]{2,1,0:T(4,128)(2,1)S(1)}, u32[]{:S(2)}, u32[]{:S(2)}) collective-permute-start(bf16[60,4,256]{2,1,0:T(4,128)(2,1)S(1)} %get-tuple-element.30), channel_id=1, source_target_pairs={{0,1},{1,0},{2,3},{3,2},{4,5},{5,4},{6,7},{7,6},{16,17},{17,16},{1... | collective-permute-start | bytes 368648 | tf_op jit(solution)/shard_map/ppermute | solution.py:491
  22.9 9.1 %collective-permute-start.3 = (bf16[60,4,256]{2,1,0:T(4,128)(2,1)S(1)}, bf16[60,4,256]{2,1,0:T(4,128)(2,1)S(1)}, u32[]{:S(2)}, u32[]{:S(2)}) collective-permute-start(bf16[60,4,256]{2,1,0:T(4,128)(2,1)S(1)} %get-tuple-element.33), channel_id=1, source_target_pairs={{1,2},{2,1},{3,4},{4,3},{5,6},{6,5},{7,8},{8,7},{9,10},{10,9},{11,... | collective-permute-start | bytes 368648 | tf_op jit(solution)/shard_map/ppermute | solution.py:492
  32.0 0.7 %collective-permute-start.4 = (bf16[60,4,256]{2,1,0:T(4,128)(2,1)S(1)}, bf16[60,4,256]{2,1,0:T(4,128)(2,1)S(1)}, u32[]{:S(2)}, u32[]{:S(2)}) collective-permute-start(bf16[60,4,256]{2,1,0:T(4,128)(2,1)S(1)} %get-tuple-element.34), channel_id=1, source_target_pairs={{8,9},{9,8},{10,11},{11,10},{12,13},{13,12},{14,15},{15,14},{24,25... | collective-permute-start | bytes 368648 | tf_op jit(solution)/shard_map/ppermute | solution.py:493
  32.7 1.0 %shard_map.57 = (f32[512,256]{1,0:T(8,128)S(1)}, f32[2,32,48]{2,1,0:T(8,128)S(1)}, f32[2,32,8]{2,1,0:T(8,128)S(1)}) custom-call(f32[16,256]{1,0:T(8,128)S(1)} %get-tuple-element.20.aux, bf16[36,4,256]{2,1,0:T(4,128)(2,1)S(1)} %collective-permute-done.x_two, bf16[36,4,256]{2,1,0:T(4,128)(2,1)S(1)} %collective-permute-done.1.x_one, ...), custom_call_target="tpu_custom_call" | custom-call | tf_op jit(solution)/shard_map/pallas_call | solution.py:504
  33.7 0.0 collective-permute-done.2.low
  33.7 0.6 %shard_map.59 = (f32[2,128,256]{2,1,0:T(8,128)S(1)}, f32[128,4,256]{2,1,0:T(4,128)S(1)}) custom-call(f32[2,32,48]{2,1,0:T(8,128)S(1)} %get-tuple-element.24.forward, f32[2,32,8]{2,1,0:T(8,128)S(1)} %get-tuple-element.25.mine_y, f32[512,256]{1,0:T(8,128)S(1)} %get-tuple-element.26.acc, bf16[60,4,256]{2,1,0:T(4,128)(2,1)S(1)} %collective-permute-done.2.low), custom_call_target="tpu_custom_call" | custom-call | tf_op jit(solution)/shard_map/pallas_call | solution.py:504
  34.3 1.2 %collective-permute-done.3.two = bf16[60,4,256]{2,1,0:T(4,128)(2,1)S(1)} collective-permute-done((bf16[60,4,256]{2,1,0:T(4,128)(2,1)S(1)}, bf16[60,4,256]{2,1,0:T(4,128)(2,1)S(1)}, u32[]{:S(2)}, u32[]{:S(2)}) %collective-permute-start.3) | collective-permute-done | bytes 122912 | tf_op jit(solution)/shard_map/ppermute | solution.py:492
  35.4 0.0 collective-permute-done.4.top
  35.4 1.2 %shard_map.60 = f32[128,4,256]{2,1,0:T(4,128)} custom-call(f32[2,32,48]{2,1,0:T(8,128)S(1)} %get-tuple-element.24.forward, f32[2,32,8]{2,1,0:T(8,128)S(1)} %get-tuple-element.25.mine_y, f32[2,128,256]{2,1,0:T(8,128)S(1)} %get-tuple-element.31.faces, f32[128,4,256]{2,1,0:T(4,128)S(1)} %get-tuple-element.32.done, ...), custom_call_target="tpu_custom_call" | custom-call | tf_op jit(solution)/shard_map/pallas_call | solution.py:504
Async XLA Ops:
  0.0 19.8 %copy-start = (bf16[4,4,8,4,256]{4,3,2,1,0:T(4,128)(2,1)S(1)}, bf16[4,4,8,4,256]{4,3,2,1,0:T(4,128)(2,1)}, u32[]{:S(2)}) copy-start(bf16[4,4,8,4,256]{4,3,2,1,0:T(4,128)(2,1)} %param.6) | copy-start | bytes 786436
  1.8 18.7 %collective-permute-start = (bf16[36,4,256]{2,1,0:T(4,128)(2,1)S(1)}, bf16[36,4,256]{2,1,0:T(4,128)(2,1)S(1)}, u32[]{:S(2)}, u32[]{:S(2)}) collective-permute-start(bf16[36,4,256]{2,1,0:T(4,128)(2,1)S(1)} %get-tuple-element.21), channel_id=1, source_target_pairs={{16,32},{32,16},{48,64},{64,48},{80,96},{96,80},{112,128},{128,112... | collective-permute-start | bytes 221192 | tf_op jit(solution)/shard_map/ppermute | solution.py:482
  6.4 14.4 %collective-permute-start.1 = (bf16[36,4,256]{2,1,0:T(4,128)(2,1)S(1)}, bf16[36,4,256]{2,1,0:T(4,128)(2,1)S(1)}, u32[]{:S(2)}, u32[]{:S(2)}) collective-permute-start(bf16[36,4,256]{2,1,0:T(4,128)(2,1)S(1)} %get-tuple-element.22), channel_id=1, source_target_pairs={{0,16},{16,0},{32,48},{48,32},{64,80},{80,64},{96,112},{112,96},{1... | collective-permute-start | bytes 221192 | tf_op jit(solution)/shard_map/ppermute | solution.py:483
  21.0 12.7 %collective-permute-start.2 = (bf16[60,4,256]{2,1,0:T(4,128)(2,1)S(1)}, bf16[60,4,256]{2,1,0:T(4,128)(2,1)S(1)}, u32[]{:S(2)}, u32[]{:S(2)}) collective-permute-start(bf16[60,4,256]{2,1,0:T(4,128)(2,1)S(1)} %get-tuple-element.30), channel_id=1, source_target_pairs={{0,1},{1,0},{2,3},{3,2},{4,5},{5,4},{6,7},{7,6},{16,17},{17,16},{1... | collective-permute-start | bytes 368648 | tf_op jit(solution)/shard_map/ppermute | solution.py:491
  22.9 12.5 %collective-permute-start.3 = (bf16[60,4,256]{2,1,0:T(4,128)(2,1)S(1)}, bf16[60,4,256]{2,1,0:T(4,128)(2,1)S(1)}, u32[]{:S(2)}, u32[]{:S(2)}) collective-permute-start(bf16[60,4,256]{2,1,0:T(4,128)(2,1)S(1)} %get-tuple-element.33), channel_id=1, source_target_pairs={{1,2},{2,1},{3,4},{4,3},{5,6},{6,5},{7,8},{8,7},{9,10},{10,9},{11,... | collective-permute-start | bytes 368648 | tf_op jit(solution)/shard_map/ppermute | solution.py:492
  32.0 3.4 %collective-permute-start.4 = (bf16[60,4,256]{2,1,0:T(4,128)(2,1)S(1)}, bf16[60,4,256]{2,1,0:T(4,128)(2,1)S(1)}, u32[]{:S(2)}, u32[]{:S(2)}) collective-permute-start(bf16[60,4,256]{2,1,0:T(4,128)(2,1)S(1)} %get-tuple-element.34), channel_id=1, source_target_pairs={{8,9},{9,8},{10,11},{11,10},{12,13},{13,12},{14,15},{15,14},{24,25... | collective-permute-start | bytes 368648 | tf_op jit(solution)/shard_map/ppermute | solution.py:493

commit v7 on v5

--- a/solution.py
+++ b/solution.py
@@ -193,7 +193,6 @@
         (x, faces[n], out.at[pl.ds(begin + Y_PLACE[x], DEPTH)])
         for n, out, begin in (
             (0, low, 0),
-            (1, low, Y_SITES),
             (1, two, 0),
             (0, top, 0),
             (1, over, 0),
@@ -241,7 +240,7 @@
             at = POS_ROWS + 2 * k + h
             aux[at : at + 1] = values[:, h * NV : (h + 1) * NV]
     places = [(out, Y_AUX) for out in (low, two, top, over)]
-    places += [(low, Y_SITES + Y_AUX), (over_up, 0), (over_down, DEPTH)]
+    places += [(over_up, 0), (over_down, DEPTH)]
     for k in range(AUX):
         site = aux[4 * k : 4 * k + 4].astype(BF16)
         for out, at in places:
@@ -274,10 +273,11 @@
 
 
 def corners(sizes, late, *refs):
-    *inputs, one, two, sem = refs
+    _, *inputs, one, two, sem = refs
     if late:
-        _, relayed, *inputs = inputs
-    trial, message, y_one, y_two = inputs
+        over, y_one, y_two, trial, message = inputs
+    else:
+        y_two, y_one, trial, message = inputs
     at_x, at_y, _, across_y = place_of(sizes)
     copies = []
 
@@ -298,7 +298,7 @@
             copies[-1].start()
         plain = copy_of(y_two, begin, BLOCK, out, X_BLOCK[1])
         if late:
-            other = copy_of(relayed, begin, BLOCK, out, X_BLOCK[1])
+            other = copy_of(over, begin, BLOCK, out, X_BLOCK[1])
 
             @pl.when(at_y == across_y - 1)
             def _():
@@ -333,16 +333,25 @@
         copy.wait()
 
 
-def hand_on(after, y_low, top, relay, out, sem):
+def hand_on(after, over, top, back, top_out, sem):
     del after
     copies = [
-        pltpu.make_async_copy(y_low.at[pl.ds(Y_SITES, Y_SITES)], relay, sem.at[0]),
-        pltpu.make_async_copy(top, out, sem.at[1]),
+        pltpu.make_async_copy(over, back, sem.at[0]),
+        pltpu.make_async_copy(top, top_out, sem.at[1]),
     ]
     for copy in copies:
         copy.start()
     for copy in copies:
         copy.wait()
+
+
+def settle(y_two, y_low, out):
+    del y_two, y_low
+    out[...] = jnp.zeros_like(out)
+
+
+def blank(*_):
+    pass
 
 
 def own_of(aux):
@@ -408,38 +417,48 @@
     return atom, step, part
 
 
-def first_half(periods, sizes, aux, y_low, y_top, acc_in, *refs):
-    acc, forward_y, mine_y, forward_x, mine_x, wave = refs
+def first_half(periods, sizes, aux, message, acc_in, acc, wave):
+    side = side_of(place_of(sizes)[1])[0]
+    forward, mine_t = y_ahead(side, *own_of(aux))
     acc[...] = acc_in[...]
-    at_x, at_y, _, _ = place_of(sizes)
+    y_add(acc, side, y_part(periods[1], sizes, side, reader_of(message), forward, mine_t, wave))
+
+
+def second_half(periods, sizes, late, *refs):
+    _, at_y, _, across_y = place_of(sizes)
+    mine = at_y < across_y // 4 * 2
+    if late:
+        _, *refs = refs
+        mine = jnp.logical_not(mine)
+
+    @pl.when(mine)
+    def _():
+        finish(periods, sizes, late, *refs)
+
+
+def finish(periods, sizes, late, aux, y_two, other, *refs):
+    beside, given, acc_in = refs[:2], refs[2:4], refs[4]
+    out, acc, wave, one_wave, two_wave, result, x_messages, sem, x_sem = refs[5:]
+    at_x, at_y, across_x, across_y = place_of(sizes)
+    arrivals = []
+    if late:
+        x_messages = given[1], given[0]
+    else:
+        x_messages = x_messages.at[0], x_messages.at[1]
+        arrivals = [
+            pltpu.make_async_copy(source, target, x_sem.at[n])
+            for n, (source, target) in enumerate(zip(given, x_messages[::-1]))
+        ]
+    for arrival in arrivals:
+        arrival.start()
+    acc[...] = acc_in[...]
     own_first, own_key, pos_t = own_of(aux)
     y_sides = side_of(at_y)
-    forward_y[...], mine_y[...] = y_ahead(y_sides[1], own_first, own_key, pos_t)
-    for n, side in enumerate(side_of(at_x)):
-        mine, theirs = faces_of(side)
-        my_atom = iota((FACE, 1), 0) + mine * FACE
-        their_atom, step, _ = ghost(theirs, y_sides, (WIDE, 1), 0)
-        target = their_atom + ((side + 1) * 3 + step + 1) * ATOMS
-        left = onehot(own_first, my_atom.astype(F32))
-        forward_x[n] = dot_nt(left, onehot(own_key, target.astype(F32)))
-        pick = jnp.where(iota((FACE, ATOMS), 1) == my_atom, 1.0, 0.0).astype(BF16)
-        mine_x[n] = picked_rows(pick, pos_t)
-    forward, mine_t = y_ahead(y_sides[0], own_first, own_key, pos_t)
-    read = sum_of(reader_of(y_low), reader_of(y_top))
-    y_add(acc, y_sides[0], y_part(periods[1], sizes, y_sides[0], read, forward, mine_t, wave))
-
-
-def second_half(periods, sizes, *refs):
-    forward_y, mine_y, forward_x, mine_x, acc_in = refs[:5]
-    y_two, over, relayed, *beside = refs[5:10]
-    x_messages = refs[10:12]
-    out, acc, wave, one_wave, two_wave, result, sem = refs[12:]
-    at_x, at_y, across_x, across_y = place_of(sizes)
-    acc[...] = acc_in[...]
-    y_sides = side_of(at_y)
     x_sides = side_of(at_x)
-    read = sum_of(reader_of(y_two), reader_of(over), reader_of(relayed))
-    added = y_part(periods[1], sizes, y_sides[1], read, forward_y[...], mine_y[...], wave)
+
+    read = sum_of(reader_of(y_two), reader_of(other))
+    forward_y, mine_y = y_ahead(y_sides[1], own_first, own_key, pos_t)
+    added = y_part(periods[1], sizes, y_sides[1], read, forward_y, mine_y, wave)
     k = iota((FACE, 1), 0)
     zi = (k & (DEPTH - 1)).astype(F32)
     lane = iota((1, WIDE), 1)
@@ -447,6 +466,8 @@
     shifts = [wrap(at_y, across_y, y, periods[1]) for y in y_sides]
     shift_y = jnp.where(lane < FACE, 0.0, jnp.where(lane < FACE + DEPTH, *shifts))
     parts = []
+    for arrival in arrivals:
+        arrival.wait()
     for n, side in enumerate(x_sides):
         mine, theirs = faces_of(side)
         corner_at = jnp.where(theirs == 0, 0, AUX)
@@ -460,9 +481,12 @@
             return plain((X_BLOCK[0] + at[0], at[1]))
 
         my_atom = k + mine * FACE
-        their_atom, _, part = ghost(theirs, y_sides, (WIDE, 1), 0)
+        their_atom, step, part = ghost(theirs, y_sides, (WIDE, 1), 0)
+        target = their_atom + ((side + 1) * 3 + step + 1) * ATOMS
         lane_atom, _, lane_part = ghost(theirs, y_sides, (ATOMS, WIDE), 1)
-        left, right, picks, placed = [], [], [], []
+        left = [onehot(own_first, my_atom.astype(F32))]
+        right = [onehot(own_key, target.astype(F32))]
+        picks, placed = [], []
         for m, y in enumerate((0, *y_sides)):
             rows = aux_of((plain, first, second)[m], aux_at if m else FACE)
             listed, key = list_of(rows[POS_ROWS : POS_ROWS + LIST_ROWS])
@@ -472,12 +496,11 @@
             pick = (iota((ATOMS, WIDE), 0) == lane_atom) & (lane_part == m)
             picks.append(jnp.where(pick, 1.0, 0.0).astype(BF16))
             placed.append(rows[:, :ATOMS].astype(BF16))
-        count = forward_x[n] + dot_nt(
-            jnp.concatenate(left, axis=1), jnp.concatenate(right, axis=1)
-        )
+        count = dot_nt(jnp.concatenate(left, axis=1), jnp.concatenate(right, axis=1))
         points = dot(jnp.concatenate(placed, axis=1), jnp.concatenate(picks, axis=0))
         points = points_of(points)
-        mine_t = mine_x[n]
+        pick = jnp.where(iota((FACE, ATOMS), 1) == my_atom, 1.0, 0.0).astype(BF16)
+        mine_t = picked_rows(pick, pos_t)
         dx = (points[0:1] + wrap(at_x, across_x, side, periods[0])) - mine_t[:, 0:1]
         dy = (points[1:2] + shift_y) - mine_t[:, 1:2]
         dz = (points[2:3] + z_shift(zi, zj)) - mine_t[:, 2:3]
@@ -523,7 +546,7 @@
 
     two = lax.ppermute(two, ("gx", "gy"), pairs(1))
     one = lax.ppermute(one, ("gx", "gy"), pairs(0))
-    return one, two
+    return two, one
 
 
 def over_wrap(message, step):
@@ -578,8 +601,7 @@
             )
         )
         + (pair_count,),
-        [message(2 * Y_SITES)]
-        + [message(Y_SITES)] * 3
+        [message(Y_SITES)] * 4
         + [message(Y_SITES)] * 2
         + [floats(4 * AUX, NV)],
         in_space=[HBM] * 4 + [SMEM],
@@ -587,18 +609,18 @@
             pltpu.VMEM((3 * SIDE * SIDE, DEPTH), F32),
             pltpu.VMEM((2, slots), jnp.int32),
             pltpu.VMEM((1, slots), jnp.int32),
-            pltpu.SemaphoreType.DMA((3 + 5 * SIDE + 2,)),
+            pltpu.SemaphoreType.DMA((3 + 4 * SIDE + 2,)),
         ],
     )
     half = across_y // 4 * 2
     pairs = swap(across_y, 0)
     early = lax.axis_index("gy") < half
+    y_two = lax.ppermute(two, "gy", swap(across_y, 1)[:-2])
     y_low = lax.ppermute(low, "gy", pairs[:half])
-    y_two = lax.ppermute(two, "gy", swap(across_y, 1)[:-2])
-    over = over_wrap(over, 0)
+    over_in = over_wrap(over, 0)
     over_up = over_wrap(over_up, 1)
     over_down = over_wrap(over_down, -1)
-    (acc,) = call(own, (mine, aux), [floats(4 * ATOMS, NV)], scratch_shapes=[wave(4 * ATOMS)])
+    (settled,) = call(settle, (y_two, y_low), [floats(8, LANES)], in_space=ANY)
 
     def x_messages(late, *given):
         return call(
@@ -610,60 +632,78 @@
             scratch_shapes=[pltpu.SemaphoreType.DMA((8,))],
         )
 
-    x_in = lax.cond(
-        early,
-        lambda: exchange_x(*x_messages(False, mine, two, y_low, y_two), range(half)),
-        lambda: (jnp.zeros((X_SITES, 4, NV), BF16),) * 2,
-    )
-    relay, top = call(
+    def own_atoms(y_message):
+        (acc,) = call(own, (mine, aux), [floats(4 * ATOMS, NV)], scratch_shapes=[wave(4 * ATOMS)])
+        return call(
+            functools.partial(first_half, periods, sizes),
+            (aux, y_message, acc),
+            [floats(4 * ATOMS, NV)],
+            scratch_shapes=[wave(4 * FACE)],
+        )
+
+    def nothing():
+        kinds = [message(X_SITES)] * 2 + [floats(4 * ATOMS, NV)]
+        return tuple(call(blank, (), kinds, out_space=ANY))
+
+    def early_ones():
+        messages = x_messages(False, settled, y_two, y_low, mine, low)
+        return (*exchange_x(*messages, range(half)), *own_atoms(y_low))
+
+    def late_ones():
+        messages = x_messages(True, beside[0], back, y_top, y_two, mine, low)
+        return (*exchange_x(*messages, range(half, across_y)), *own_atoms(y_top))
+
+    from_early = lax.cond(early, early_ones, nothing)
+    back, top = call(
         hand_on,
-        (x_in[0], y_low, top),
+        (from_early[0], over, top),
         [message(Y_SITES)] * 2,
         in_space=ANY,
         out_space=ANY,
         scratch_shapes=[pltpu.SemaphoreType.DMA((2,))],
     )
-    relayed = lax.ppermute(relay, "gy", [(1, across_y - 1)])
-    y_top = lax.ppermute(top, "gy", pairs[half:])
+    back = lax.ppermute(back, "gy", [(0, across_y - 1)])
+    (y_top,) = lax.cond(
+        early,
+        lambda: tuple(call(blank, (), [message(Y_SITES)], out_space=ANY)),
+        lambda: (lax.ppermute(top, "gy", pairs[half:]),),
+    )
     beside = call(
         functools.partial(crossed, sizes),
-        (over, over_up, over_down),
+        (over_in, over_up, over_down),
         [message(BLOCK)] * 2,
         in_space=ANY,
         out_space=ANY,
         scratch_shapes=[pltpu.SemaphoreType.DMA((2,))],
     )
-    x_late = x_messages(True, beside[0], relayed, mine, two, y_top, y_two)
-    x_in = lax.cond(
-        early,
-        lambda: tuple(x_in),
-        lambda: exchange_x(*x_late, range(half, across_y)),
-    )
-    acc, *ahead = call(
-        functools.partial(first_half, periods, sizes),
-        (aux, y_low, y_top, acc),
-        [
-            floats(4 * ATOMS, NV),
-            floats(FACE, FACE),
-            floats(FACE, 8),
-            floats(2, FACE, WIDE),
-            floats(2, FACE, 8),
-        ],
-        scratch_shapes=[wave(4 * FACE)],
-    )
-    (product,) = call(
-        functools.partial(second_half, periods, sizes),
-        (*ahead, acc, y_two, over, relayed, *beside, *x_in),
-        [floats(ATOMS, 4, NV)],
-        out_space=HBM,
-        scratch_shapes=[
-            pltpu.VMEM((4 * ATOMS, NV), F32),
-            wave(2 * ATOMS),
-            wave(4 * WIDE),
-            wave(4 * WIDE),
-            pltpu.VMEM((ATOMS, 4, NV), F32),
-            pltpu.SemaphoreType.DMA((3,)),
-        ],
+    def result(late, inputs, spaces, **options):
+        (product,) = call(
+            functools.partial(second_half, periods, sizes, late),
+            inputs,
+            [floats(ATOMS, 4, NV)],
+            in_space=spaces + [VMEM] * 5 + [VMEM if late else ANY] * 2 + [VMEM],
+            out_space=HBM,
+            scratch_shapes=[
+                pltpu.VMEM((4 * ATOMS, NV), F32),
+                wave(2 * ATOMS),
+                wave(4 * WIDE),
+                wave(4 * WIDE),
+                pltpu.VMEM((ATOMS, 4, NV), F32),
+                pltpu.VMEM((2, X_SITES, 4, NV), BF16),
+                pltpu.SemaphoreType.DMA((3,)),
+                pltpu.SemaphoreType.DMA((2,)),
+            ],
+            **options,
+        )
+        return product
+
+    product = result(False, (aux, y_two, over_in, *beside, *from_early), [])
+    from_late = lax.cond(early, nothing, late_ones)
+    product = result(
+        True,
+        (product, aux, y_two, back, *beside, *from_late),
+        [HBM],
+        input_output_aliases={0: 0},
     )
     return product.reshape(trial.shape)
 

time: 43.4 us -> 34.7 us (0.80)
  the two profiles are of different devices: /device:TPU:64 before, /device:TPU:960 now
where the time goes in v7:
time: 34.7 us; the launch traced here: 34.4 us
  starting transfers between devices  14.1 us (41%)
  waiting for transfers between devices  13.9 us (40%)
  Pallas kernels  5.44 us (16%)
  between operations  0.83 us (2%)
    ppermute x1, waiting for transfers between devices, shards(): back = lax.ppermute(back, 'gy', [(0, across_y - 1)])  5.59 us
    pallas_call x10, Pallas kernels, call(): pl.pallas_call(kernel, out_shape=outputs, in_specs=in_space if isinstance...  5.44 us
    ppermute x3, starting transfers between devices, over_wrap(): return lax.ppermute(message, ('gx', 'gy'), pairs)  5.32 us
    ppermute x1, waiting for transfers between devices, shards(): lax.ppermute(top, 'gy', pairs[half:])  4.32 us
    ppermute x1, waiting for transfers between devices, exchange_x(): two = lax.ppermute(two, ('gx', 'gy'), pairs(1))  4 us
    ppermute x1, starting transfers between devices, exchange_x(): two = lax.ppermute(two, ('gx', 'gy'), pairs(1))  2.31 us
    ppermute x1, starting transfers between devices, shards(): lax.ppermute(top, 'gy', pairs[half:])  1.92 us
    ppermute x1, starting transfers between devices, exchange_x(): one = lax.ppermute(one, ('gx', 'gy'), pairs(0))  1.92 us
  transfers between devices with their start and end apart: 9, of which 3 were waited for; matrix products, arithmetic and copies ran while one was open for 0% of the time, Pallas kernels for 5%

profile of v7, /device:TPU:960, one launch (start us, length us, event | category | flops | bytes accessed | tf_op | source)
XLA Modules:
  0.0 34.4 jit_solution(11849349682793059892)
XLA Ops:
  0.7 1.2 %shard_map.55 = (bf16[36,4,256]{2,1,0:T(4,128)(2,1)S(1)}, bf16[36,4,256]{2,1,0:T(4,128)(2,1)S(1)}, bf16[36,4,256]{2,1,0:T(4,128)(2,1)S(1)}, bf16[36,4,256]{2,1,0...) custom-call(bf16[128,4,256]{2,1,0:T(4,128)(2,1)} %bitcast.5, ...), custom_call_target="tpu_custom_call" | custom-call | tf_op jit(solution)/shard_map/pallas_call | solution.py:567
  1.9 0.7 %collective-permute-start.5 = (bf16[36,4,256]{2,1,0:T(4,128)(2,1)S(1)}, bf16[36,4,256]{2,1,0:T(4,128)(2,1)S(1)}, u32[]{:S(2)}, u32[]{:S(2)}) collective-permute-start(bf16[36,4,256]{2,1,0:T(4,128)(2,1)S(1)} %get-tuple-element.70), channel_id=1, source_target_pairs={{1,2},{2,1},{3,4},{4,3},{5,6},{6,5},{7,8},{8,7},{9,10},{10,9},{11,... | collective-permute-start | bytes 221192 | tf_op jit(solution)/shard_map/ppermute | solution.py:618
  2.6 0.7 %collective-permute-start.9 = (bf16[36,4,256]{2,1,0:T(4,128)(2,1)S(1)}, bf16[36,4,256]{2,1,0:T(4,128)(2,1)S(1)}, u32[]{:S(2)}, u32[]{:S(2)}) collective-permute-start(bf16[36,4,256]{2,1,0:T(4,128)(2,1)S(1)} %get-tuple-element.76), channel_id=1, source_target_pairs={{0,1},{1,0},{2,3},{3,2},{4,5},{5,4},{6,7},{7,6},{16,17},{17,16},{1... | collective-permute-start | bytes 221192 | tf_op jit(solution)/shard_map/ppermute | solution.py:619
  3.3 1.3 %collective-permute-start.7 = (bf16[36,4,256]{2,1,0:T(4,128)(2,1)S(1)}, bf16[36,4,256]{2,1,0:T(4,128)(2,1)S(1)}, u32[]{:S(2)}, u32[]{:S(2)}) collective-permute-start(bf16[36,4,256]{2,1,0:T(4,128)(2,1)S(1)} %get-tuple-element.72), channel_id=1, source_target_pairs={{15,16},{31,32},{47,48},{63,64},{79,80},{95,96},{111,112},{127,128... | collective-permute-start | bytes 221192 | tf_op jit(solution)/shard_map/ppermute | solution.py:557
  4.6 1.3 %collective-permute-start.8 = (bf16[36,4,256]{2,1,0:T(4,128)(2,1)S(1)}, bf16[36,4,256]{2,1,0:T(4,128)(2,1)S(1)}, u32[]{:S(2)}, u32[]{:S(2)}) collective-permute-start(bf16[36,4,256]{2,1,0:T(4,128)(2,1)S(1)} %get-tuple-element.73), channel_id=1, source_target_pairs={{15,1008},{31,0},{47,16},{63,32},{79,48},{95,64},{111,80},{127,96}... | collective-permute-start | bytes 221192 | tf_op jit(solution)/shard_map/ppermute | solution.py:557
  5.9 2.7 %collective-permute-start.6 = (bf16[36,4,256]{2,1,0:T(4,128)(2,1)S(1)}, bf16[36,4,256]{2,1,0:T(4,128)(2,1)S(1)}, u32[]{:S(2)}, u32[]{:S(2)}) collective-permute-start(bf16[36,4,256]{2,1,0:T(4,128)(2,1)S(1)} %get-tuple-element.71.over), channel_id=1, source_target_pairs={{15,0},{31,16},{47,32},{63,48},{79,64},{95,80},{111,96},{127,112},... | collective-permute-start | bytes 221192 | tf_op jit(solution)/shard_map/ppermute | solution.py:557
  8.6 0.0 collective-permute-done.5.y_two.refs_1_.refs_2_
  8.7 0.0 collective-permute-done.9.y_low
  8.7 0.2 shard_map.59
  8.9 1.3 %collective-permute-start.10 = (bf16[36,4,256]{2,1,0:T(4,128)(2,1)S(1)}, bf16[36,4,256]{2,1,0:T(4,128)(2,1)S(1)}, u32[]{:S(2)}, u32[]{:S(2)}) collective-permute-start(bf16[36,4,256]{2,1,0:T(4,128)(2,1)S(1)} %get-tuple-element.81), channel_id=1, source_target_pairs={{0,15},{16,31},{32,47},{48,63},{64,79},{80,95},{96,111},{112,127},... | collective-permute-start | bytes 221192 | tf_op jit(solution)/shard_map/ppermute | solution.py:665
  10.2 6.3 %conditional.4 = (bf16[36,4,256]{2,1,0:T(4,128)(2,1)S(1)}) conditional(s32[]{:T(128)} %convert_element_type.2, bf16[36,4,256]{2,1,0:T(4,128)(2,1)S(1)} %get-tuple-element.82, () %tuple.27), branch_computations={%region_2.0_spmd, %region_3.0_spmd} | conditional | bytes 294960 | solution.py:666
  10.2 1.9 %collective-permute-start.2 = (bf16[36,4,256]{2,1,0:T(4,128)(2,1)S(1)}, bf16[36,4,256]{2,1,0:T(4,128)(2,1)S(1)}, u32[]{:S(2)}, u32[]{:S(2)}) collective-permute-start(bf16[36,4,256]{2,1,0:T(4,128)(2,1)S(1)} %param.2), channel_id=1, source_target_pairs={{8,9},{9,8},{10,11},{11,10},{12,13},{13,12},{14,15},{15,14},{24,25... | collective-permute-start | bytes 221192 | tf_op jit(solution)/shard_map/cond/branch_0_fun/ppermute | solution.py:669
  12.2 4.3 %collective-permute-done.2 = bf16[36,4,256]{2,1,0:T(4,128)(2,1)S(1)} collective-permute-done((bf16[36,4,256]{2,1,0:T(4,128)(2,1)S(1)}, bf16[36,4,256]{2,1,0:T(4,128)(2,1)S(1)}, u32[]{:S(2)}, u32[]{:S(2)}) %collective-permute-start.2) | collective-permute-done | bytes 73760 | tf_op jit(solution)/shard_map/cond/branch_0_fun/ppermute | solution.py:669
  16.5 0.1 shard_map.56
  16.6 0.1 shard_map.58.refs_0_
  16.7 5.6 %collective-permute-done.10.refs_3_ = bf16[36,4,256]{2,1,0:T(4,128)(2,1)S(1)} collective-permute-done((bf16[36,4,256]{2,1,0:T(4,128)(2,1)S(1)}, bf16[36,4,256]{2,1,0:T(4,128)(2,1)S(1)}, u32[]{:S(2)}, u32[]{:S(2)}) %collective-permute-start.10) | collective-permute-done | bytes 73760 | tf_op jit(solution)/shard_map/ppermute | solution.py:665
  22.3 9.9 %conditional.5 = ((bf16[60,4,256]{2,1,0:T(4,128)(2,1)S(1)}, bf16[60,4,256]{2,1,0:T(4,128)(2,1)S(1)}, f32[512,256]{1,0:T(8,128)S(1)})) conditional(s32[]{:T(128)} %convert_element_type.2, (bf16[12,4,256]{2,1,0:T(4,128)(2,1)S(1)}, bf16[36,4,256]{2,1,0:T(4,128)(2,1)S(1)}, bf16[36,4,256]{2,1,0:T(4,128)(2,1)S(1)}, bf16[36,4,256]{2,1,0:T(4,128)(2,1)S(1)}, ...), branch_computations={%region_4.0_spmd, %region_5.0_spmd} | conditional | bytes 983152 | solution.py:701
  22.3 0.4 %branch_0_fun.5 = (bf16[60,4,256]{2,1,0:T(4,128)(2,1)S(1)}, bf16[60,4,256]{2,1,0:T(4,128)(2,1)S(1)}) custom-call(bf16[12,4,256]{2,1,0:T(4,128)(2,1)S(1)} %get-tuple-element.43.refs_0_, bf16[36,4,256]{2,1,0:T(4,128)(2,1)S(1)} %get-tuple-element.44.refs_1_, bf16[36,4,256]{2,1,0:T(4,128)(2,1)S(1)} %get-tuple-element.45.refs_2_.message, ...), custom_call_target="tpu_custom_call" | custom-call | tf_op jit(solution)/shard_map/cond/branch_0_fun/pallas_call | solution.py:567
  22.7 2.3 %collective-permute-start.3 = (bf16[60,4,256]{2,1,0:T(4,128)(2,1)S(1)}, bf16[60,4,256]{2,1,0:T(4,128)(2,1)S(1)}, u32[]{:S(2)}, u32[]{:S(2)}) collective-permute-start(bf16[60,4,256]{2,1,0:T(4,128)(2,1)S(1)} %get-tuple-element.49), channel_id=1, source_target_pairs={{24,40},{40,24},{56,72},{72,56},{88,104},{104,88},{120,136},{136,1... | collective-permute-start | bytes 368648 | tf_op jit(solution)/shard_map/cond/branch_0_fun/ppermute | solution.py:547
  25.0 1.9 %collective-permute-start.4 = (bf16[60,4,256]{2,1,0:T(4,128)(2,1)S(1)}, bf16[60,4,256]{2,1,0:T(4,128)(2,1)S(1)}, u32[]{:S(2)}, u32[]{:S(2)}) collective-permute-start(bf16[60,4,256]{2,1,0:T(4,128)(2,1)S(1)} %get-tuple-element.50), channel_id=1, source_target_pairs={{8,24},{24,8},{40,56},{56,40},{72,88},{88,72},{104,120},{120,104},... | collective-permute-start | bytes 368648 | tf_op jit(solution)/shard_map/cond/branch_0_fun/ppermute | solution.py:548
  26.9 0.7 %branch_0_fun.6.acc_in = f32[512,256]{1,0:T(8,128)S(1)} custom-call(bf16[128,4,256]{2,1,0:T(4,128)(2,1)S(1)} %get-tuple-element.47.refs_4_.trial, f32[16,256]{1,0:T(8,128)S(1)} %get-tuple-element.51.aux), custom_call_target="tpu_custom_call" | custom-call | tf_op jit(solution)/shard_map/cond/branch_0_fun/pallas_call | solution.py:567
  27.6 0.6 %branch_0_fun.7 = f32[512,256]{1,0:T(8,128)S(1)} custom-call(f32[16,256]{1,0:T(8,128)S(1)} %get-tuple-element.51.aux, bf16[36,4,256]{2,1,0:T(4,128)(2,1)S(1)} %get-tuple-element.45.refs_2_.message, f32[512,256]{1,0:T(8,128)S(1)} %branch_0_fun.6.acc_in), custom_call_target="tpu_custom_call" | custom-call | tf_op jit(solution)/shard_map/cond/branch_0_fun/pallas_call | solution.py:567
  28.2 4.0 %collective-permute-done.3 = bf16[60,4,256]{2,1,0:T(4,128)(2,1)S(1)} collective-permute-done((bf16[60,4,256]{2,1,0:T(4,128)(2,1)S(1)}, bf16[60,4,256]{2,1,0:T(4,128)(2,1)S(1)}, u32[]{:S(2)}, u32[]{:S(2)}) %collective-permute-start.3) | collective-permute-done | bytes 122912 | tf_op jit(solution)/shard_map/cond/branch_0_fun/ppermute | solution.py:547
  32.2 2.2 %shard_map.60 = f32[128,4,256]{2,1,0:T(4,128)} custom-call(f32[128,4,256]{2,1,0:T(4,128)} %shard_map.58.refs_0_, f32[16,256]{1,0:T(8,128)S(1)} %get-tuple-element.69.refs_0_.refs_1_, bf16[36,4,256]{2,1,0:T(4,128)(2,1)S(1)} %collective-permute-done.5.y_two.refs_1_.refs_2_, ...), custom_call_target="tpu_custom_call", output_to_operand_aliasing={{}: (0, {})} | custom-call | tf_op jit(solution)/shard_map/pallas_call | solution.py:567
  (9 shorter events, 0.0 us)
Async XLA Ops:
  0.0 8.7 %copy-start = (bf16[4,4,8,4,256]{4,3,2,1,0:T(4,128)(2,1)S(1)}, bf16[4,4,8,4,256]{4,3,2,1,0:T(4,128)(2,1)}, u32[]{:S(2)}) copy-start(bf16[4,4,8,4,256]{4,3,2,1,0:T(4,128)(2,1)} %param.12) | copy-start | bytes 786436
  1.9 6.7 %collective-permute-start.5 = (bf16[36,4,256]{2,1,0:T(4,128)(2,1)S(1)}, bf16[36,4,256]{2,1,0:T(4,128)(2,1)S(1)}, u32[]{:S(2)}, u32[]{:S(2)}) collective-permute-start(bf16[36,4,256]{2,1,0:T(4,128)(2,1)S(1)} %get-tuple-element.70), channel_id=1, source_target_pairs={{1,2},{2,1},{3,4},{4,3},{5,6},{6,5},{7,8},{8,7},{9,10},{10,9},{11,... | collective-permute-start | bytes 221192 | tf_op jit(solution)/shard_map/ppermute | solution.py:618
  2.6 6.0 %collective-permute-start.9 = (bf16[36,4,256]{2,1,0:T(4,128)(2,1)S(1)}, bf16[36,4,256]{2,1,0:T(4,128)(2,1)S(1)}, u32[]{:S(2)}, u32[]{:S(2)}) collective-permute-start(bf16[36,4,256]{2,1,0:T(4,128)(2,1)S(1)} %get-tuple-element.76), channel_id=1, source_target_pairs={{0,1},{1,0},{2,3},{3,2},{4,5},{5,4},{6,7},{7,6},{16,17},{17,16},{1... | collective-permute-start | bytes 221192 | tf_op jit(solution)/shard_map/ppermute | solution.py:619
  3.3 13.2 %collective-permute-start.7 = (bf16[36,4,256]{2,1,0:T(4,128)(2,1)S(1)}, bf16[36,4,256]{2,1,0:T(4,128)(2,1)S(1)}, u32[]{:S(2)}, u32[]{:S(2)}) collective-permute-start(bf16[36,4,256]{2,1,0:T(4,128)(2,1)S(1)} %get-tuple-element.72), channel_id=1, source_target_pairs={{15,16},{31,32},{47,48},{63,64},{79,80},{95,96},{111,112},{127,128... | collective-permute-start | bytes 221192 | tf_op jit(solution)/shard_map/ppermute | solution.py:557
  4.6 11.9 %collective-permute-start.8 = (bf16[36,4,256]{2,1,0:T(4,128)(2,1)S(1)}, bf16[36,4,256]{2,1,0:T(4,128)(2,1)S(1)}, u32[]{:S(2)}, u32[]{:S(2)}) collective-permute-start(bf16[36,4,256]{2,1,0:T(4,128)(2,1)S(1)} %get-tuple-element.73), channel_id=1, source_target_pairs={{15,1008},{31,0},{47,16},{63,32},{79,48},{95,64},{111,80},{127,96}... | collective-permute-start | bytes 221192 | tf_op jit(solution)/shard_map/ppermute | solution.py:557
  5.9 10.6 %collective-permute-start.6 = (bf16[36,4,256]{2,1,0:T(4,128)(2,1)S(1)}, bf16[36,4,256]{2,1,0:T(4,128)(2,1)S(1)}, u32[]{:S(2)}, u32[]{:S(2)}) collective-permute-start(bf16[36,4,256]{2,1,0:T(4,128)(2,1)S(1)} %get-tuple-element.71.over), channel_id=1, source_target_pairs={{15,0},{31,16},{47,32},{63,48},{79,64},{95,80},{111,96},{127,112},... | collective-permute-start | bytes 221192 | tf_op jit(solution)/shard_map/ppermute | solution.py:557
  8.9 13.3 %collective-permute-start.10 = (bf16[36,4,256]{2,1,0:T(4,128)(2,1)S(1)}, bf16[36,4,256]{2,1,0:T(4,128)(2,1)S(1)}, u32[]{:S(2)}, u32[]{:S(2)}) collective-permute-start(bf16[36,4,256]{2,1,0:T(4,128)(2,1)S(1)} %get-tuple-element.81), channel_id=1, source_target_pairs={{0,15},{16,31},{32,47},{48,63},{64,79},{80,95},{96,111},{112,127},... | collective-permute-start | bytes 221192 | tf_op jit(solution)/shard_map/ppermute | solution.py:665
  10.2 6.2 %collective-permute-start.2 = (bf16[36,4,256]{2,1,0:T(4,128)(2,1)S(1)}, bf16[36,4,256]{2,1,0:T(4,128)(2,1)S(1)}, u32[]{:S(2)}, u32[]{:S(2)}) collective-permute-start(bf16[36,4,256]{2,1,0:T(4,128)(2,1)S(1)} %param.2), channel_id=1, source_target_pairs={{8,9},{9,8},{10,11},{11,10},{12,13},{13,12},{14,15},{15,14},{24,25... | collective-permute-start | bytes 221192 | tf_op jit(solution)/shard_map/cond/branch_0_fun/ppermute | solution.py:669
  22.7 9.5 %collective-permute-start.3 = (bf16[60,4,256]{2,1,0:T(4,128)(2,1)S(1)}, bf16[60,4,256]{2,1,0:T(4,128)(2,1)S(1)}, u32[]{:S(2)}, u32[]{:S(2)}) collective-permute-start(bf16[60,4,256]{2,1,0:T(4,128)(2,1)S(1)} %get-tuple-element.49), channel_id=1, source_target_pairs={{24,40},{40,24},{56,72},{72,56},{88,104},{104,88},{120,136},{136,1... | collective-permute-start | bytes 368648 | tf_op jit(solution)/shard_map/cond/branch_0_fun/ppermute | solution.py:547
  25.0 7.2 %collective-permute-start.4 = (bf16[60,4,256]{2,1,0:T(4,128)(2,1)S(1)}, bf16[60,4,256]{2,1,0:T(4,128)(2,1)S(1)}, u32[]{:S(2)}, u32[]{:S(2)}) collective-permute-start(bf16[60,4,256]{2,1,0:T(4,128)(2,1)S(1)} %get-tuple-element.50), channel_id=1, source_target_pairs={{8,24},{24,8},{40,56},{56,40},{72,88},{88,72},{104,120},{120,104},... | collective-permute-start | bytes 368648 | tf_op jit(solution)/shard_map/cond/branch_0_fun/ppermute | solution.py:548

commit v8 on v7

--- a/solution.py
+++ b/solution.py
@@ -182,7 +182,7 @@
 
 
 def pack_y(sizes, trial, positions, atoms, owner, count, *refs):
-    low, two, top, over, over_up, over_down, aux, pos, pairs, owners, sem = refs
+    low, two, top, over, back, over_up, over_down, aux, pos, pairs, owners, sem = refs
     at_x, at_y, across_x, across_y = place_of(sizes)
     copies = [
         pltpu.make_async_copy(a, b, sem.at[k])
@@ -196,6 +196,7 @@
             (1, two, 0),
             (0, top, 0),
             (1, over, 0),
+            (1, back, 0),
         )
         for x in range(SIDE)
     ]
@@ -239,7 +240,7 @@
         for h in range(2):
             at = POS_ROWS + 2 * k + h
             aux[at : at + 1] = values[:, h * NV : (h + 1) * NV]
-    places = [(out, Y_AUX) for out in (low, two, top, over)]
+    places = [(out, Y_AUX) for out in (low, two, top, over, back)]
     places += [(over_up, 0), (over_down, DEPTH)]
     for k in range(AUX):
         site = aux[4 * k : 4 * k + 4].astype(BF16)
@@ -333,16 +334,8 @@
         copy.wait()
 
 
-def hand_on(after, over, top, back, top_out, sem):
-    del after
-    copies = [
-        pltpu.make_async_copy(over, back, sem.at[0]),
-        pltpu.make_async_copy(top, top_out, sem.at[1]),
-    ]
-    for copy in copies:
-        copy.start()
-    for copy in copies:
-        copy.wait()
+def hand_on(*_):
+    pass
 
 
 def settle(y_two, y_low, out):
@@ -417,11 +410,24 @@
     return atom, step, part
 
 
-def first_half(periods, sizes, aux, message, acc_in, acc, wave):
-    side = side_of(place_of(sizes)[1])[0]
-    forward, mine_t = y_ahead(side, *own_of(aux))
+def first_half(periods, sizes, aux, message, acc_in, acc, forward_y, mine_y, forward_x, mine_x, wave):
+    at_x, at_y, _, _ = place_of(sizes)
+    y_sides = side_of(at_y)
+    own_first, own_key, pos_t = own_of(aux)
+    forward_y[...], mine_y[...] = y_ahead(y_sides[1], own_first, own_key, pos_t)
+    for n, side in enumerate(side_of(at_x)):
+        mine, theirs = faces_of(side)
+        my_atom = iota((FACE, 1), 0) + mine * FACE
+        their_atom, step, _ = ghost(theirs, y_sides, (WIDE, 1), 0)
+        target = their_atom + ((side + 1) * 3 + step + 1) * ATOMS
+        left = onehot(own_first, my_atom.astype(F32))
+        forward_x[n] = dot_nt(left, onehot(own_key, target.astype(F32)))
+        pick = jnp.where(iota((FACE, ATOMS), 1) == my_atom, 1.0, 0.0).astype(BF16)
+        mine_x[n] = picked_rows(pick, pos_t)
+    forward, mine_t = y_ahead(y_sides[0], own_first, own_key, pos_t)
     acc[...] = acc_in[...]
-    y_add(acc, side, y_part(periods[1], sizes, side, reader_of(message), forward, mine_t, wave))
+    part = y_part(periods[1], sizes, y_sides[0], reader_of(message), forward, mine_t, wave)
+    y_add(acc, y_sides[0], part)
 
 
 def second_half(periods, sizes, late, *refs):
@@ -436,9 +442,10 @@
         finish(periods, sizes, late, *refs)
 
 
-def finish(periods, sizes, late, aux, y_two, other, *refs):
-    beside, given, acc_in = refs[:2], refs[2:4], refs[4]
-    out, acc, wave, one_wave, two_wave, result, x_messages, sem, x_sem = refs[5:]
+def finish(periods, sizes, late, y_two, other, *refs):
+    beside, given = refs[:2], refs[2:4]
+    acc_in, forward_y, mine_y, forward_x, mine_x = refs[4:9]
+    out, acc, wave, one_wave, two_wave, result, x_messages, sem, x_sem = refs[9:]
     at_x, at_y, across_x, across_y = place_of(sizes)
     arrivals = []
     if late:
@@ -452,13 +459,11 @@
     for arrival in arrivals:
         arrival.start()
     acc[...] = acc_in[...]
-    own_first, own_key, pos_t = own_of(aux)
     y_sides = side_of(at_y)
     x_sides = side_of(at_x)
 
     read = sum_of(reader_of(y_two), reader_of(other))
-    forward_y, mine_y = y_ahead(y_sides[1], own_first, own_key, pos_t)
-    added = y_part(periods[1], sizes, y_sides[1], read, forward_y, mine_y, wave)
+    added = y_part(periods[1], sizes, y_sides[1], read, forward_y[...], mine_y[...], wave)
     k = iota((FACE, 1), 0)
     zi = (k & (DEPTH - 1)).astype(F32)
     lane = iota((1, WIDE), 1)
@@ -481,12 +486,9 @@
             return plain((X_BLOCK[0] + at[0], at[1]))
 
         my_atom = k + mine * FACE
-        their_atom, step, part = ghost(theirs, y_sides, (WIDE, 1), 0)
-        target = their_atom + ((side + 1) * 3 + step + 1) * ATOMS
+        their_atom, _, part = ghost(theirs, y_sides, (WIDE, 1), 0)
         lane_atom, _, lane_part = ghost(theirs, y_sides, (ATOMS, WIDE), 1)
-        left = [onehot(own_first, my_atom.astype(F32))]
-        right = [onehot(own_key, target.astype(F32))]
-        picks, placed = [], []
+        left, right, picks, placed = [], [], [], []
         for m, y in enumerate((0, *y_sides)):
             rows = aux_of((plain, first, second)[m], aux_at if m else FACE)
             listed, key = list_of(rows[POS_ROWS : POS_ROWS + LIST_ROWS])
@@ -496,11 +498,12 @@
             pick = (iota((ATOMS, WIDE), 0) == lane_atom) & (lane_part == m)
             picks.append(jnp.where(pick, 1.0, 0.0).astype(BF16))
             placed.append(rows[:, :ATOMS].astype(BF16))
-        count = dot_nt(jnp.concatenate(left, axis=1), jnp.concatenate(right, axis=1))
+        count = forward_x[n] + dot_nt(
+            jnp.concatenate(left, axis=1), jnp.concatenate(right, axis=1)
+        )
         points = dot(jnp.concatenate(placed, axis=1), jnp.concatenate(picks, axis=0))
         points = points_of(points)
-        pick = jnp.where(iota((FACE, ATOMS), 1) == my_atom, 1.0, 0.0).astype(BF16)
-        mine_t = picked_rows(pick, pos_t)
+        mine_t = mine_x[n]
         dx = (points[0:1] + wrap(at_x, across_x, side, periods[0])) - mine_t[:, 0:1]
         dy = (points[1:2] + shift_y) - mine_t[:, 1:2]
         dz = (points[2:3] + z_shift(zi, zj)) - mine_t[:, 2:3]
@@ -589,7 +592,7 @@
     def wave(rows):
         return pltpu.VMEM((2, rows, LANES), F32)
 
-    low, two, top, over, over_up, over_down, aux = call(
+    low, two, top, over, back, over_up, over_down, aux = call(
         functools.partial(pack_y, sizes),
         tuple(
             pltpu.with_memory_space_constraint(array, pltpu.HBM)
@@ -601,7 +604,7 @@
             )
         )
         + (pair_count,),
-        [message(Y_SITES)] * 4
+        [message(Y_SITES)] * 5
         + [message(Y_SITES)] * 2
         + [floats(4 * AUX, NV)],
         in_space=[HBM] * 4 + [SMEM],
@@ -609,7 +612,7 @@
             pltpu.VMEM((3 * SIDE * SIDE, DEPTH), F32),
             pltpu.VMEM((2, slots), jnp.int32),
             pltpu.VMEM((1, slots), jnp.int32),
-            pltpu.SemaphoreType.DMA((3 + 4 * SIDE + 2,)),
+            pltpu.SemaphoreType.DMA((3 + 5 * SIDE + 2,)),
         ],
     )
     half = across_y // 4 * 2
@@ -632,17 +635,25 @@
             scratch_shapes=[pltpu.SemaphoreType.DMA((8,))],
         )
 
+    own_kinds = [
+        floats(4 * ATOMS, NV),
+        floats(FACE, FACE),
+        floats(FACE, 8),
+        floats(2, FACE, WIDE),
+        floats(2, FACE, 8),
+    ]
+
     def own_atoms(y_message):
         (acc,) = call(own, (mine, aux), [floats(4 * ATOMS, NV)], scratch_shapes=[wave(4 * ATOMS)])
         return call(
             functools.partial(first_half, periods, sizes),
             (aux, y_message, acc),
-            [floats(4 * ATOMS, NV)],
+            own_kinds,
             scratch_shapes=[wave(4 * FACE)],
         )
 
     def nothing():
-        kinds = [message(X_SITES)] * 2 + [floats(4 * ATOMS, NV)]
+        kinds = [message(X_SITES)] * 2 + own_kinds
         return tuple(call(blank, (), kinds, out_space=ANY))
 
     def early_ones():
@@ -656,11 +667,11 @@
     from_early = lax.cond(early, early_ones, nothing)
     back, top = call(
         hand_on,
-        (from_early[0], over, top),
+        (from_early[0], back, top),
         [message(Y_SITES)] * 2,
         in_space=ANY,
         out_space=ANY,
-        scratch_shapes=[pltpu.SemaphoreType.DMA((2,))],
+        input_output_aliases={1: 0, 2: 1},
     )
     back = lax.ppermute(back, "gy", [(0, across_y - 1)])
     (y_top,) = lax.cond(
@@ -681,7 +692,7 @@
             functools.partial(second_half, periods, sizes, late),
             inputs,
             [floats(ATOMS, 4, NV)],
-            in_space=spaces + [VMEM] * 5 + [VMEM if late else ANY] * 2 + [VMEM],
+            in_space=spaces + [VMEM] * 4 + [VMEM if late else ANY] * 2 + [VMEM] * 5,
             out_space=HBM,
             scratch_shapes=[
                 pltpu.VMEM((4 * ATOMS, NV), F32),
@@ -697,11 +708,11 @@
         )
         return product
 
-    product = result(False, (aux, y_two, over_in, *beside, *from_early), [])
+    product = result(False, (y_two, over_in, *beside, *from_early), [])
     from_late = lax.cond(early, nothing, late_ones)
     product = result(
         True,
-        (product, aux, y_two, back, *beside, *from_late),
+        (product, y_two, back, *beside, *from_late),
         [HBM],
         input_output_aliases={0: 0},
     )

time: 34.7 us -> 34.1 us (0.983)
  Pallas kernels: 5.44 us -> 4.78 us
    pallas_call x10, Pallas kernels: 5.44 us -> 4.78 us  [call(): pl.pallas_call(kernel, out_shape=outputs, in_specs=in_space if isinstance...]
  transfers between devices with their start and end apart: 9 -> 9, of which waited for: 3 -> 3; matrix products, arithmetic and copies ran while one was open for 0% -> 0% of each run, Pallas kernels for 5% -> 4%
where the time goes in v8:
time: 34.1 us; the launch traced here: 33.8 us
  starting transfers between devices  14.1 us (41%)
  waiting for transfers between devices  14 us (41%)
  Pallas kernels  4.78 us (14%)
  between operations  0.83 us (2%)
    ppermute x1, waiting for transfers between devices, shards(): back = lax.ppermute(back, 'gy', [(0, across_y - 1)])  5.71 us
    ppermute x3, starting transfers between devices, over_wrap(): return lax.ppermute(message, ('gx', 'gy'), pairs)  5.32 us
    pallas_call x10, Pallas kernels, call(): pl.pallas_call(kernel, out_shape=outputs, in_specs=in_space if isinstance...  4.78 us
    ppermute x1, waiting for transfers between devices, shards(): lax.ppermute(top, 'gy', pairs[half:])  4.32 us
    ppermute x1, waiting for transfers between devices, exchange_x(): two = lax.ppermute(two, ('gx', 'gy'), pairs(1))  3.91 us
    ppermute x1, starting transfers between devices, exchange_x(): two = lax.ppermute(two, ('gx', 'gy'), pairs(1))  2.34 us
    ppermute x1, starting transfers between devices, shards(): lax.ppermute(top, 'gy', pairs[half:])  1.92 us
    ppermute x1, starting transfers between devices, exchange_x(): one = lax.ppermute(one, ('gx', 'gy'), pairs(0))  1.92 us
  transfers between devices with their start and end apart: 9, of which 3 were waited for; matrix products, arithmetic and copies ran while one was open for 0% of the time, Pallas kernels for 4%

profile of v8, /device:TPU:960, one launch (start us, length us, event | category | flops | bytes accessed | tf_op | source)
XLA Modules:
  0.0 33.8 jit_solution(1828504047866951522)
XLA Ops:
  0.7 1.3 %shard_map.55 = (bf16[36,4,256]{2,1,0:T(4,128)(2,1)S(1)}, bf16[36,4,256]{2,1,0:T(4,128)(2,1)S(1)}, bf16[36,4,256]{2,1,0:T(4,128)(2,1)S(1)}, bf16[36,4,256]{2,1,0...) custom-call(bf16[128,4,256]{2,1,0:T(4,128)(2,1)} %bitcast.5, ...), custom_call_target="tpu_custom_call" | custom-call | tf_op jit(solution)/shard_map/pallas_call | solution.py:570
  2.0 0.7 %collective-permute-start.5 = (bf16[36,4,256]{2,1,0:T(4,128)(2,1)S(1)}, bf16[36,4,256]{2,1,0:T(4,128)(2,1)S(1)}, u32[]{:S(2)}, u32[]{:S(2)}) collective-permute-start(bf16[36,4,256]{2,1,0:T(4,128)(2,1)S(1)} %get-tuple-element.88), channel_id=1, source_target_pairs={{1,2},{2,1},{3,4},{4,3},{5,6},{6,5},{7,8},{8,7},{9,10},{10,9},{11,... | collective-permute-start | bytes 221192 | tf_op jit(solution)/shard_map/ppermute | solution.py:621
  2.7 0.7 %collective-permute-start.9 = (bf16[36,4,256]{2,1,0:T(4,128)(2,1)S(1)}, bf16[36,4,256]{2,1,0:T(4,128)(2,1)S(1)}, u32[]{:S(2)}, u32[]{:S(2)}) collective-permute-start(bf16[36,4,256]{2,1,0:T(4,128)(2,1)S(1)} %get-tuple-element.94), channel_id=1, source_target_pairs={{0,1},{1,0},{2,3},{3,2},{4,5},{5,4},{6,7},{7,6},{16,17},{17,16},{1... | collective-permute-start | bytes 221192 | tf_op jit(solution)/shard_map/ppermute | solution.py:622
  3.3 2.7 %collective-permute-start.6 = (bf16[36,4,256]{2,1,0:T(4,128)(2,1)S(1)}, bf16[36,4,256]{2,1,0:T(4,128)(2,1)S(1)}, u32[]{:S(2)}, u32[]{:S(2)}) collective-permute-start(bf16[36,4,256]{2,1,0:T(4,128)(2,1)S(1)} %get-tuple-element.89), channel_id=1, source_target_pairs={{15,0},{31,16},{47,32},{63,48},{79,64},{95,80},{111,96},{127,112},... | collective-permute-start | bytes 221192 | tf_op jit(solution)/shard_map/ppermute | solution.py:560
  6.1 1.3 %collective-permute-start.7 = (bf16[36,4,256]{2,1,0:T(4,128)(2,1)S(1)}, bf16[36,4,256]{2,1,0:T(4,128)(2,1)S(1)}, u32[]{:S(2)}, u32[]{:S(2)}) collective-permute-start(bf16[36,4,256]{2,1,0:T(4,128)(2,1)S(1)} %get-tuple-element.90), channel_id=1, source_target_pairs={{15,16},{31,32},{47,48},{63,64},{79,80},{95,96},{111,112},{127,128... | collective-permute-start | bytes 221192 | tf_op jit(solution)/shard_map/ppermute | solution.py:560
  7.4 1.3 %collective-permute-start.8 = (bf16[36,4,256]{2,1,0:T(4,128)(2,1)S(1)}, bf16[36,4,256]{2,1,0:T(4,128)(2,1)S(1)}, u32[]{:S(2)}, u32[]{:S(2)}) collective-permute-start(bf16[36,4,256]{2,1,0:T(4,128)(2,1)S(1)} %get-tuple-element.91), channel_id=1, source_target_pairs={{15,1008},{31,0},{47,16},{63,32},{79,48},{95,64},{111,80},{127,96}... | collective-permute-start | bytes 221192 | tf_op jit(solution)/shard_map/ppermute | solution.py:560
  8.7 0.0 collective-permute-done.5.y_two.refs_0_.refs_1_
  8.8 1.3 %collective-permute-start.10 = (bf16[36,4,256]{2,1,0:T(4,128)(2,1)S(1)}, bf16[36,4,256]{2,1,0:T(4,128)(2,1)S(1)}, u32[]{:S(2)}, u32[]{:S(2)}) collective-permute-start(bf16[36,4,256]{2,1,0:T(4,128)(2,1)S(1)} %get-tuple-element.105), channel_id=1, source_target_pairs={{0,15},{16,31},{32,47},{48,63},{64,79},{80,95},{96,111},{112,127},... | collective-permute-start | bytes 221192 | tf_op jit(solution)/shard_map/ppermute | solution.py:676
  10.1 6.3 %conditional.4 = (bf16[36,4,256]{2,1,0:T(4,128)(2,1)S(1)}) conditional(s32[]{:T(128)} %convert_element_type.2, bf16[36,4,256]{2,1,0:T(4,128)(2,1)S(1)} %get-tuple-element.106, () %tuple.27), branch_computations={%region_2.0_spmd, %region_3.0_spmd} | conditional | bytes 294960 | solution.py:677
  10.1 1.9 %collective-permute-start.2 = (bf16[36,4,256]{2,1,0:T(4,128)(2,1)S(1)}, bf16[36,4,256]{2,1,0:T(4,128)(2,1)S(1)}, u32[]{:S(2)}, u32[]{:S(2)}) collective-permute-start(bf16[36,4,256]{2,1,0:T(4,128)(2,1)S(1)} %param.2), channel_id=1, source_target_pairs={{8,9},{9,8},{10,11},{11,10},{12,13},{13,12},{14,15},{15,14},{24,25... | collective-permute-start | bytes 221192 | tf_op jit(solution)/shard_map/cond/branch_0_fun/ppermute | solution.py:680
  12.0 4.3 %collective-permute-done.2 = bf16[36,4,256]{2,1,0:T(4,128)(2,1)S(1)} collective-permute-done((bf16[36,4,256]{2,1,0:T(4,128)(2,1)S(1)}, bf16[36,4,256]{2,1,0:T(4,128)(2,1)S(1)}, u32[]{:S(2)}, u32[]{:S(2)}) %collective-permute-start.2) | collective-permute-done | bytes 73760 | tf_op jit(solution)/shard_map/cond/branch_0_fun/ppermute | solution.py:680
  16.3 0.0 collective-permute-done.6.over.refs_1_
  16.3 0.1 shard_map.56
  16.5 0.1 shard_map.58.refs_0_
  16.5 5.7 %collective-permute-done.10.refs_2_ = bf16[36,4,256]{2,1,0:T(4,128)(2,1)S(1)} collective-permute-done((bf16[36,4,256]{2,1,0:T(4,128)(2,1)S(1)}, bf16[36,4,256]{2,1,0:T(4,128)(2,1)S(1)}, u32[]{:S(2)}, u32[]{:S(2)}) %collective-permute-start.10) | collective-permute-done | bytes 73760 | tf_op jit(solution)/shard_map/ppermute | solution.py:676
  22.2 9.9 %conditional.5 = ((bf16[60,4,256]{2,1,0:T(4,128)(2,1)S(1)}, bf16[60,4,256]{2,1,0:T(4,128)(2,1)S(1)}, f32[512,256]{1,0:T(8,128)S(1)}, f32[32,32]{1,0:T(8,128)S(1)...) conditional(s32[]{:T(128)} %convert_element_type.2, ...), branch_computations={%region_4.0_spmd, %region_5.0_spmd} | conditional | bytes 983184 | solution.py:712
  22.2 0.4 %branch_0_fun.5 = (bf16[60,4,256]{2,1,0:T(4,128)(2,1)S(1)}, bf16[60,4,256]{2,1,0:T(4,128)(2,1)S(1)}) custom-call(bf16[12,4,256]{2,1,0:T(4,128)(2,1)S(1)} %get-tuple-element.48.refs_0_, bf16[36,4,256]{2,1,0:T(4,128)(2,1)S(1)} %get-tuple-element.49.refs_1_, bf16[36,4,256]{2,1,0:T(4,128)(2,1)S(1)} %get-tuple-element.50.refs_2_.message, ...), custom_call_target="tpu_custom_call" | custom-call | tf_op jit(solution)/shard_map/cond/branch_0_fun/pallas_call | solution.py:570
  22.6 2.3 %collective-permute-start.3 = (bf16[60,4,256]{2,1,0:T(4,128)(2,1)S(1)}, bf16[60,4,256]{2,1,0:T(4,128)(2,1)S(1)}, u32[]{:S(2)}, u32[]{:S(2)}) collective-permute-start(bf16[60,4,256]{2,1,0:T(4,128)(2,1)S(1)} %get-tuple-element.54), channel_id=1, source_target_pairs={{24,40},{40,24},{56,72},{72,56},{88,104},{104,88},{120,136},{136,1... | collective-permute-start | bytes 368648 | tf_op jit(solution)/shard_map/cond/branch_0_fun/ppermute | solution.py:550
  25.0 1.9 %collective-permute-start.4 = (bf16[60,4,256]{2,1,0:T(4,128)(2,1)S(1)}, bf16[60,4,256]{2,1,0:T(4,128)(2,1)S(1)}, u32[]{:S(2)}, u32[]{:S(2)}) collective-permute-start(bf16[60,4,256]{2,1,0:T(4,128)(2,1)S(1)} %get-tuple-element.55), channel_id=1, source_target_pairs={{8,24},{24,8},{40,56},{56,40},{72,88},{88,72},{104,120},{120,104},... | collective-permute-start | bytes 368648 | tf_op jit(solution)/shard_map/cond/branch_0_fun/ppermute | solution.py:551
  26.9 0.7 %branch_0_fun.6.acc_in = f32[512,256]{1,0:T(8,128)S(1)} custom-call(bf16[128,4,256]{2,1,0:T(4,128)(2,1)S(1)} %get-tuple-element.52.refs_4_.trial, f32[16,256]{1,0:T(8,128)S(1)} %get-tuple-element.56.aux), custom_call_target="tpu_custom_call" | custom-call | tf_op jit(solution)/shard_map/cond/branch_0_fun/pallas_call | solution.py:570
  27.6 0.6 %branch_0_fun.7 = (f32[512,256]{1,0:T(8,128)S(1)}, f32[32,32]{1,0:T(8,128)S(1)}, f32[32,8]{1,0:T(8,128)S(1)}, f32[2,32,48]{2,1,0:T(8,128)S(1)}, f32[2,32,8]{2,1,0:T(8,128)S(1)}) custom-call(f32[16,256]{1,0:T(8,128)S(1)} %get-tuple-element.56.aux, bf16[36,4,256]{2,1,0:T(4,128)(2,1)S(1)} %get-tuple-element.50.refs_2_.message, f32[512,256]{1,0:T(8,128)S(1)} %branch_0_fun.6.acc_in), custom_call_target="tpu_custom_call" | custom-call | tf_op jit(solution)/shard_map/cond/branch_0_fun/pallas_call | solution.py:570
  28.2 3.9 %collective-permute-done.3 = bf16[60,4,256]{2,1,0:T(4,128)(2,1)S(1)} collective-permute-done((bf16[60,4,256]{2,1,0:T(4,128)(2,1)S(1)}, bf16[60,4,256]{2,1,0:T(4,128)(2,1)S(1)}, u32[]{:S(2)}, u32[]{:S(2)}) %collective-permute-start.3) | collective-permute-done | bytes 122912 | tf_op jit(solution)/shard_map/cond/branch_0_fun/ppermute | solution.py:550
  32.2 0.0 collective-permute-done.4
  32.2 1.6 %shard_map.60 = f32[128,4,256]{2,1,0:T(4,128)} custom-call(f32[128,4,256]{2,1,0:T(4,128)} %shard_map.58.refs_0_, bf16[36,4,256]{2,1,0:T(4,128)(2,1)S(1)} %collective-permute-done.5.y_two.refs_0_.refs_1_, bf16[36,4,256]{2,1,0:T(4,128)(2,1)S(1)} %collective-permute-done.10.refs_2_, ...), custom_call_target="tpu_custom_call", output_to_operand_aliasing={{}: (0, {})} | custom-call | tf_op jit(solution)/shard_map/pallas_call | solution.py:570
  (9 shorter events, 0.0 us)
Async XLA Ops:
  0.0 8.7 %copy-start = (bf16[4,4,8,4,256]{4,3,2,1,0:T(4,128)(2,1)S(1)}, bf16[4,4,8,4,256]{4,3,2,1,0:T(4,128)(2,1)}, u32[]{:S(2)}) copy-start(bf16[4,4,8,4,256]{4,3,2,1,0:T(4,128)(2,1)} %param.12) | copy-start | bytes 786436
  2.0 6.7 %collective-permute-start.5 = (bf16[36,4,256]{2,1,0:T(4,128)(2,1)S(1)}, bf16[36,4,256]{2,1,0:T(4,128)(2,1)S(1)}, u32[]{:S(2)}, u32[]{:S(2)}) collective-permute-start(bf16[36,4,256]{2,1,0:T(4,128)(2,1)S(1)} %get-tuple-element.88), channel_id=1, source_target_pairs={{1,2},{2,1},{3,4},{4,3},{5,6},{6,5},{7,8},{8,7},{9,10},{10,9},{11,... | collective-permute-start | bytes 221192 | tf_op jit(solution)/shard_map/ppermute | solution.py:621
  2.7 6.0 %collective-permute-start.9 = (bf16[36,4,256]{2,1,0:T(4,128)(2,1)S(1)}, bf16[36,4,256]{2,1,0:T(4,128)(2,1)S(1)}, u32[]{:S(2)}, u32[]{:S(2)}) collective-permute-start(bf16[36,4,256]{2,1,0:T(4,128)(2,1)S(1)} %get-tuple-element.94), channel_id=1, source_target_pairs={{0,1},{1,0},{2,3},{3,2},{4,5},{5,4},{6,7},{7,6},{16,17},{17,16},{1... | collective-permute-start | bytes 221192 | tf_op jit(solution)/shard_map/ppermute | solution.py:622
  3.3 13.0 %collective-permute-start.6 = (bf16[36,4,256]{2,1,0:T(4,128)(2,1)S(1)}, bf16[36,4,256]{2,1,0:T(4,128)(2,1)S(1)}, u32[]{:S(2)}, u32[]{:S(2)}) collective-permute-start(bf16[36,4,256]{2,1,0:T(4,128)(2,1)S(1)} %get-tuple-element.89), channel_id=1, source_target_pairs={{15,0},{31,16},{47,32},{63,48},{79,64},{95,80},{111,96},{127,112},... | collective-permute-start | bytes 221192 | tf_op jit(solution)/shard_map/ppermute | solution.py:560
  6.1 10.3 %collective-permute-start.7 = (bf16[36,4,256]{2,1,0:T(4,128)(2,1)S(1)}, bf16[36,4,256]{2,1,0:T(4,128)(2,1)S(1)}, u32[]{:S(2)}, u32[]{:S(2)}) collective-permute-start(bf16[36,4,256]{2,1,0:T(4,128)(2,1)S(1)} %get-tuple-element.90), channel_id=1, source_target_pairs={{15,16},{31,32},{47,48},{63,64},{79,80},{95,96},{111,112},{127,128... | collective-permute-start | bytes 221192 | tf_op jit(solution)/shard_map/ppermute | solution.py:560
  7.4 9.0 %collective-permute-start.8 = (bf16[36,4,256]{2,1,0:T(4,128)(2,1)S(1)}, bf16[36,4,256]{2,1,0:T(4,128)(2,1)S(1)}, u32[]{:S(2)}, u32[]{:S(2)}) collective-permute-start(bf16[36,4,256]{2,1,0:T(4,128)(2,1)S(1)} %get-tuple-element.91), channel_id=1, source_target_pairs={{15,1008},{31,0},{47,16},{63,32},{79,48},{95,64},{111,80},{127,96}... | collective-permute-start | bytes 221192 | tf_op jit(solution)/shard_map/ppermute | solution.py:560
  8.8 13.5 %collective-permute-start.10 = (bf16[36,4,256]{2,1,0:T(4,128)(2,1)S(1)}, bf16[36,4,256]{2,1,0:T(4,128)(2,1)S(1)}, u32[]{:S(2)}, u32[]{:S(2)}) collective-permute-start(bf16[36,4,256]{2,1,0:T(4,128)(2,1)S(1)} %get-tuple-element.105), channel_id=1, source_target_pairs={{0,15},{16,31},{32,47},{48,63},{64,79},{80,95},{96,111},{112,127},... | collective-permute-start | bytes 221192 | tf_op jit(solution)/shard_map/ppermute | solution.py:676
  10.1 6.2 %collective-permute-start.2 = (bf16[36,4,256]{2,1,0:T(4,128)(2,1)S(1)}, bf16[36,4,256]{2,1,0:T(4,128)(2,1)S(1)}, u32[]{:S(2)}, u32[]{:S(2)}) collective-permute-start(bf16[36,4,256]{2,1,0:T(4,128)(2,1)S(1)} %param.2), channel_id=1, source_target_pairs={{8,9},{9,8},{10,11},{11,10},{12,13},{13,12},{14,15},{15,14},{24,25... | collective-permute-start | bytes 221192 | tf_op jit(solution)/shard_map/cond/branch_0_fun/ppermute | solution.py:680
  22.6 9.5 %collective-permute-start.3 = (bf16[60,4,256]{2,1,0:T(4,128)(2,1)S(1)}, bf16[60,4,256]{2,1,0:T(4,128)(2,1)S(1)}, u32[]{:S(2)}, u32[]{:S(2)}) collective-permute-start(bf16[60,4,256]{2,1,0:T(4,128)(2,1)S(1)} %get-tuple-element.54), channel_id=1, source_target_pairs={{24,40},{40,24},{56,72},{72,56},{88,104},{104,88},{120,136},{136,1... | collective-permute-start | bytes 368648 | tf_op jit(solution)/shard_map/cond/branch_0_fun/ppermute | solution.py:550
  25.0 7.2 %collective-permute-start.4 = (bf16[60,4,256]{2,1,0:T(4,128)(2,1)S(1)}, bf16[60,4,256]{2,1,0:T(4,128)(2,1)S(1)}, u32[]{:S(2)}, u32[]{:S(2)}) collective-permute-start(bf16[60,4,256]{2,1,0:T(4,128)(2,1)S(1)} %get-tuple-element.55), channel_id=1, source_target_pairs={{8,24},{24,8},{40,56},{56,40},{72,88},{88,72},{104,120},{120,104},... | collective-permute-start | bytes 368648 | tf_op jit(solution)/shard_map/cond/branch_0_fun/ppermute | solution.py:551

commit v9 on v8

--- a/solution.py
+++ b/solution.py
@@ -464,6 +464,12 @@
 
     read = sum_of(reader_of(y_two), reader_of(other))
     added = y_part(periods[1], sizes, y_sides[1], read, forward_y[...], mine_y[...], wave)
+    y_add(acc, y_sides[1], added)
+    planes = [acc[a * ATOMS + FACE : a * ATOMS + 3 * FACE] for a in range(4)]
+    result[FACE : 3 * FACE] = atoms_of(planes, wave)
+    middle = pl.ds(FACE, 2 * FACE)
+    copies = [pltpu.make_async_copy(result.at[middle], out.at[middle], sem.at[2])]
+    copies[0].start()
     k = iota((FACE, 1), 0)
     zi = (k & (DEPTH - 1)).astype(F32)
     lane = iota((1, WIDE), 1)
@@ -511,12 +517,6 @@
         block = [plain((0, FACE)), first((corner_at, DEPTH)), second((corner_at, DEPTH))]
         planes = planes_of((one_wave, two_wave)[n], jnp.concatenate(block, axis=0))
         parts.append(applied(grid, planes))
-    y_add(acc, y_sides[1], added)
-    planes = [acc[a * ATOMS + FACE : a * ATOMS + 3 * FACE] for a in range(4)]
-    result[FACE : 3 * FACE] = atoms_of(planes, wave)
-    middle = pl.ds(FACE, 2 * FACE)
-    copies = [pltpu.make_async_copy(result.at[middle], out.at[middle], sem.at[2])]
-    copies[0].start()
     for n, side in enumerate(x_sides):
         mine, _ = faces_of(side)
         planes = []

time: 34.1 us -> 34.1 us (level)
  no operation moved by 1% of the time
where the time goes in v9:
time: 34.1 us; the launch traced here: 33.8 us
  starting transfers between devices  14.1 us (41%)
  waiting for transfers between devices  14 us (41%)
  Pallas kernels  4.78 us (14%)
  between operations  0.83 us (2%)
    ppermute x1, waiting for transfers between devices, shards(): back = lax.ppermute(back, 'gy', [(0, across_y - 1)])  5.71 us
    ppermute x3, starting transfers between devices, over_wrap(): return lax.ppermute(message, ('gx', 'gy'), pairs)  5.32 us
    pallas_call x10, Pallas kernels, call(): pl.pallas_call(kernel, out_shape=outputs, in_specs=in_space if isinstance...  4.78 us
    ppermute x1, waiting for transfers between devices, shards(): lax.ppermute(top, 'gy', pairs[half:])  4.32 us
    ppermute x1, waiting for transfers between devices, exchange_x(): two = lax.ppermute(two, ('gx', 'gy'), pairs(1))  3.91 us
    ppermute x1, starting transfers between devices, exchange_x(): two = lax.ppermute(two, ('gx', 'gy'), pairs(1))  2.34 us
    ppermute x1, starting transfers between devices, shards(): lax.ppermute(top, 'gy', pairs[half:])  1.92 us
    ppermute x1, starting transfers between devices, exchange_x(): one = lax.ppermute(one, ('gx', 'gy'), pairs(0))  1.92 us
  transfers between devices with their start and end apart: 9, of which 3 were waited for; matrix products, arithmetic and copies ran while one was open for 0% of the time, Pallas kernels for 4%

profile of v9, /device:TPU:960, one launch (start us, length us, event | category | flops | bytes accessed | tf_op | source)
XLA Modules:
  0.0 33.8 jit_solution(10081991429949173144)
XLA Ops:
  0.7 1.3 %shard_map.55 = (bf16[36,4,256]{2,1,0:T(4,128)(2,1)S(1)}, bf16[36,4,256]{2,1,0:T(4,128)(2,1)S(1)}, bf16[36,4,256]{2,1,0:T(4,128)(2,1)S(1)}, bf16[36,4,256]{2,1,0...) custom-call(bf16[128,4,256]{2,1,0:T(4,128)(2,1)} %bitcast.5, ...), custom_call_target="tpu_custom_call" | custom-call | tf_op jit(solution)/shard_map/pallas_call | solution.py:570
  2.0 0.7 %collective-permute-start.5 = (bf16[36,4,256]{2,1,0:T(4,128)(2,1)S(1)}, bf16[36,4,256]{2,1,0:T(4,128)(2,1)S(1)}, u32[]{:S(2)}, u32[]{:S(2)}) collective-permute-start(bf16[36,4,256]{2,1,0:T(4,128)(2,1)S(1)} %get-tuple-element.88), channel_id=1, source_target_pairs={{1,2},{2,1},{3,4},{4,3},{5,6},{6,5},{7,8},{8,7},{9,10},{10,9},{11,... | collective-permute-start | bytes 221192 | tf_op jit(solution)/shard_map/ppermute | solution.py:621
  2.7 0.7 %collective-permute-start.9 = (bf16[36,4,256]{2,1,0:T(4,128)(2,1)S(1)}, bf16[36,4,256]{2,1,0:T(4,128)(2,1)S(1)}, u32[]{:S(2)}, u32[]{:S(2)}) collective-permute-start(bf16[36,4,256]{2,1,0:T(4,128)(2,1)S(1)} %get-tuple-element.94), channel_id=1, source_target_pairs={{0,1},{1,0},{2,3},{3,2},{4,5},{5,4},{6,7},{7,6},{16,17},{17,16},{1... | collective-permute-start | bytes 221192 | tf_op jit(solution)/shard_map/ppermute | solution.py:622
  3.3 2.7 %collective-permute-start.6 = (bf16[36,4,256]{2,1,0:T(4,128)(2,1)S(1)}, bf16[36,4,256]{2,1,0:T(4,128)(2,1)S(1)}, u32[]{:S(2)}, u32[]{:S(2)}) collective-permute-start(bf16[36,4,256]{2,1,0:T(4,128)(2,1)S(1)} %get-tuple-element.89), channel_id=1, source_target_pairs={{15,0},{31,16},{47,32},{63,48},{79,64},{95,80},{111,96},{127,112},... | collective-permute-start | bytes 221192 | tf_op jit(solution)/shard_map/ppermute | solution.py:560
  6.1 1.3 %collective-permute-start.7 = (bf16[36,4,256]{2,1,0:T(4,128)(2,1)S(1)}, bf16[36,4,256]{2,1,0:T(4,128)(2,1)S(1)}, u32[]{:S(2)}, u32[]{:S(2)}) collective-permute-start(bf16[36,4,256]{2,1,0:T(4,128)(2,1)S(1)} %get-tuple-element.90), channel_id=1, source_target_pairs={{15,16},{31,32},{47,48},{63,64},{79,80},{95,96},{111,112},{127,128... | collective-permute-start | bytes 221192 | tf_op jit(solution)/shard_map/ppermute | solution.py:560
  7.4 1.3 %collective-permute-start.8 = (bf16[36,4,256]{2,1,0:T(4,128)(2,1)S(1)}, bf16[36,4,256]{2,1,0:T(4,128)(2,1)S(1)}, u32[]{:S(2)}, u32[]{:S(2)}) collective-permute-start(bf16[36,4,256]{2,1,0:T(4,128)(2,1)S(1)} %get-tuple-element.91), channel_id=1, source_target_pairs={{15,1008},{31,0},{47,16},{63,32},{79,48},{95,64},{111,80},{127,96}... | collective-permute-start | bytes 221192 | tf_op jit(solution)/shard_map/ppermute | solution.py:560
  8.7 0.0 collective-permute-done.9.y_low
  8.8 1.3 %collective-permute-start.10 = (bf16[36,4,256]{2,1,0:T(4,128)(2,1)S(1)}, bf16[36,4,256]{2,1,0:T(4,128)(2,1)S(1)}, u32[]{:S(2)}, u32[]{:S(2)}) collective-permute-start(bf16[36,4,256]{2,1,0:T(4,128)(2,1)S(1)} %get-tuple-element.105), channel_id=1, source_target_pairs={{0,15},{16,31},{32,47},{48,63},{64,79},{80,95},{96,111},{112,127},... | collective-permute-start | bytes 221192 | tf_op jit(solution)/shard_map/ppermute | solution.py:676
  10.1 6.3 %conditional.4 = (bf16[36,4,256]{2,1,0:T(4,128)(2,1)S(1)}) conditional(s32[]{:T(128)} %convert_element_type.2, bf16[36,4,256]{2,1,0:T(4,128)(2,1)S(1)} %get-tuple-element.106, () %tuple.27), branch_computations={%region_2.0_spmd, %region_3.0_spmd} | conditional | bytes 294960 | solution.py:677
  10.1 1.9 %collective-permute-start.2 = (bf16[36,4,256]{2,1,0:T(4,128)(2,1)S(1)}, bf16[36,4,256]{2,1,0:T(4,128)(2,1)S(1)}, u32[]{:S(2)}, u32[]{:S(2)}) collective-permute-start(bf16[36,4,256]{2,1,0:T(4,128)(2,1)S(1)} %param.2), channel_id=1, source_target_pairs={{8,9},{9,8},{10,11},{11,10},{12,13},{13,12},{14,15},{15,14},{24,25... | collective-permute-start | bytes 221192 | tf_op jit(solution)/shard_map/cond/branch_0_fun/ppermute | solution.py:680
  12.0 4.3 %collective-permute-done.2 = bf16[36,4,256]{2,1,0:T(4,128)(2,1)S(1)} collective-permute-done((bf16[36,4,256]{2,1,0:T(4,128)(2,1)S(1)}, bf16[36,4,256]{2,1,0:T(4,128)(2,1)S(1)}, u32[]{:S(2)}, u32[]{:S(2)}) %collective-permute-start.2) | collective-permute-done | bytes 73760 | tf_op jit(solution)/shard_map/cond/branch_0_fun/ppermute | solution.py:680
  16.3 0.0 collective-permute-done.6.over.refs_1_
  16.3 0.0 collective-permute-done.7.up
  16.3 0.1 shard_map.56
  16.5 0.1 shard_map.58.refs_0_
  16.5 5.7 %collective-permute-done.10.refs_2_ = bf16[36,4,256]{2,1,0:T(4,128)(2,1)S(1)} collective-permute-done((bf16[36,4,256]{2,1,0:T(4,128)(2,1)S(1)}, bf16[36,4,256]{2,1,0:T(4,128)(2,1)S(1)}, u32[]{:S(2)}, u32[]{:S(2)}) %collective-permute-start.10) | collective-permute-done | bytes 73760 | tf_op jit(solution)/shard_map/ppermute | solution.py:676
  22.2 9.9 %conditional.5 = ((bf16[60,4,256]{2,1,0:T(4,128)(2,1)S(1)}, bf16[60,4,256]{2,1,0:T(4,128)(2,1)S(1)}, f32[512,256]{1,0:T(8,128)S(1)}, f32[32,32]{1,0:T(8,128)S(1)...) conditional(s32[]{:T(128)} %convert_element_type.2, ...), branch_computations={%region_4.0_spmd, %region_5.0_spmd} | conditional | bytes 983184 | solution.py:712
  22.2 0.4 %branch_0_fun.5 = (bf16[60,4,256]{2,1,0:T(4,128)(2,1)S(1)}, bf16[60,4,256]{2,1,0:T(4,128)(2,1)S(1)}) custom-call(bf16[12,4,256]{2,1,0:T(4,128)(2,1)S(1)} %get-tuple-element.48.refs_0_, bf16[36,4,256]{2,1,0:T(4,128)(2,1)S(1)} %get-tuple-element.49.refs_1_, bf16[36,4,256]{2,1,0:T(4,128)(2,1)S(1)} %get-tuple-element.50.refs_2_.message, ...), custom_call_target="tpu_custom_call" | custom-call | tf_op jit(solution)/shard_map/cond/branch_0_fun/pallas_call | solution.py:570
  22.6 2.3 %collective-permute-start.3 = (bf16[60,4,256]{2,1,0:T(4,128)(2,1)S(1)}, bf16[60,4,256]{2,1,0:T(4,128)(2,1)S(1)}, u32[]{:S(2)}, u32[]{:S(2)}) collective-permute-start(bf16[60,4,256]{2,1,0:T(4,128)(2,1)S(1)} %get-tuple-element.54), channel_id=1, source_target_pairs={{24,40},{40,24},{56,72},{72,56},{88,104},{104,88},{120,136},{136,1... | collective-permute-start | bytes 368648 | tf_op jit(solution)/shard_map/cond/branch_0_fun/ppermute | solution.py:550
  25.0 1.9 %collective-permute-start.4 = (bf16[60,4,256]{2,1,0:T(4,128)(2,1)S(1)}, bf16[60,4,256]{2,1,0:T(4,128)(2,1)S(1)}, u32[]{:S(2)}, u32[]{:S(2)}) collective-permute-start(bf16[60,4,256]{2,1,0:T(4,128)(2,1)S(1)} %get-tuple-element.55), channel_id=1, source_target_pairs={{8,24},{24,8},{40,56},{56,40},{72,88},{88,72},{104,120},{120,104},... | collective-permute-start | bytes 368648 | tf_op jit(solution)/shard_map/cond/branch_0_fun/ppermute | solution.py:551
  26.9 0.7 %branch_0_fun.6.acc_in = f32[512,256]{1,0:T(8,128)S(1)} custom-call(bf16[128,4,256]{2,1,0:T(4,128)(2,1)S(1)} %get-tuple-element.52.refs_4_.trial, f32[16,256]{1,0:T(8,128)S(1)} %get-tuple-element.56.aux), custom_call_target="tpu_custom_call" | custom-call | tf_op jit(solution)/shard_map/cond/branch_0_fun/pallas_call | solution.py:570
  27.6 0.6 %branch_0_fun.7 = (f32[512,256]{1,0:T(8,128)S(1)}, f32[32,32]{1,0:T(8,128)S(1)}, f32[32,8]{1,0:T(8,128)S(1)}, f32[2,32,48]{2,1,0:T(8,128)S(1)}, f32[2,32,8]{2,1,0:T(8,128)S(1)}) custom-call(f32[16,256]{1,0:T(8,128)S(1)} %get-tuple-element.56.aux, bf16[36,4,256]{2,1,0:T(4,128)(2,1)S(1)} %get-tuple-element.50.refs_2_.message, f32[512,256]{1,0:T(8,128)S(1)} %branch_0_fun.6.acc_in), custom_call_target="tpu_custom_call" | custom-call | tf_op jit(solution)/shard_map/cond/branch_0_fun/pallas_call | solution.py:570
  28.2 3.9 %collective-permute-done.3 = bf16[60,4,256]{2,1,0:T(4,128)(2,1)S(1)} collective-permute-done((bf16[60,4,256]{2,1,0:T(4,128)(2,1)S(1)}, bf16[60,4,256]{2,1,0:T(4,128)(2,1)S(1)}, u32[]{:S(2)}, u32[]{:S(2)}) %collective-permute-start.3) | collective-permute-done | bytes 122912 | tf_op jit(solution)/shard_map/cond/branch_0_fun/ppermute | solution.py:550
  32.2 1.6 %shard_map.60 = f32[128,4,256]{2,1,0:T(4,128)} custom-call(f32[128,4,256]{2,1,0:T(4,128)} %shard_map.58.refs_0_, bf16[36,4,256]{2,1,0:T(4,128)(2,1)S(1)} %collective-permute-done.5.y_two.refs_0_.refs_1_, bf16[36,4,256]{2,1,0:T(4,128)(2,1)S(1)} %collective-permute-done.10.refs_2_, ...), custom_call_target="tpu_custom_call", output_to_operand_aliasing={{}: (0, {})} | custom-call | tf_op jit(solution)/shard_map/pallas_call | solution.py:570
  (9 shorter events, 0.0 us)
Async XLA Ops:
  0.0 8.7 %copy-start = (bf16[4,4,8,4,256]{4,3,2,1,0:T(4,128)(2,1)S(1)}, bf16[4,4,8,4,256]{4,3,2,1,0:T(4,128)(2,1)}, u32[]{:S(2)}) copy-start(bf16[4,4,8,4,256]{4,3,2,1,0:T(4,128)(2,1)} %param.12) | copy-start | bytes 786436
  2.0 6.7 %collective-permute-start.5 = (bf16[36,4,256]{2,1,0:T(4,128)(2,1)S(1)}, bf16[36,4,256]{2,1,0:T(4,128)(2,1)S(1)}, u32[]{:S(2)}, u32[]{:S(2)}) collective-permute-start(bf16[36,4,256]{2,1,0:T(4,128)(2,1)S(1)} %get-tuple-element.88), channel_id=1, source_target_pairs={{1,2},{2,1},{3,4},{4,3},{5,6},{6,5},{7,8},{8,7},{9,10},{10,9},{11,... | collective-permute-start | bytes 221192 | tf_op jit(solution)/shard_map/ppermute | solution.py:621
  2.7 6.0 %collective-permute-start.9 = (bf16[36,4,256]{2,1,0:T(4,128)(2,1)S(1)}, bf16[36,4,256]{2,1,0:T(4,128)(2,1)S(1)}, u32[]{:S(2)}, u32[]{:S(2)}) collective-permute-start(bf16[36,4,256]{2,1,0:T(4,128)(2,1)S(1)} %get-tuple-element.94), channel_id=1, source_target_pairs={{0,1},{1,0},{2,3},{3,2},{4,5},{5,4},{6,7},{7,6},{16,17},{17,16},{1... | collective-permute-start | bytes 221192 | tf_op jit(solution)/shard_map/ppermute | solution.py:622
  3.3 13.0 %collective-permute-start.6 = (bf16[36,4,256]{2,1,0:T(4,128)(2,1)S(1)}, bf16[36,4,256]{2,1,0:T(4,128)(2,1)S(1)}, u32[]{:S(2)}, u32[]{:S(2)}) collective-permute-start(bf16[36,4,256]{2,1,0:T(4,128)(2,1)S(1)} %get-tuple-element.89), channel_id=1, source_target_pairs={{15,0},{31,16},{47,32},{63,48},{79,64},{95,80},{111,96},{127,112},... | collective-permute-start | bytes 221192 | tf_op jit(solution)/shard_map/ppermute | solution.py:560
  6.1 10.3 %collective-permute-start.7 = (bf16[36,4,256]{2,1,0:T(4,128)(2,1)S(1)}, bf16[36,4,256]{2,1,0:T(4,128)(2,1)S(1)}, u32[]{:S(2)}, u32[]{:S(2)}) collective-permute-start(bf16[36,4,256]{2,1,0:T(4,128)(2,1)S(1)} %get-tuple-element.90), channel_id=1, source_target_pairs={{15,16},{31,32},{47,48},{63,64},{79,80},{95,96},{111,112},{127,128... | collective-permute-start | bytes 221192 | tf_op jit(solution)/shard_map/ppermute | solution.py:560
  7.4 9.0 %collective-permute-start.8 = (bf16[36,4,256]{2,1,0:T(4,128)(2,1)S(1)}, bf16[36,4,256]{2,1,0:T(4,128)(2,1)S(1)}, u32[]{:S(2)}, u32[]{:S(2)}) collective-permute-start(bf16[36,4,256]{2,1,0:T(4,128)(2,1)S(1)} %get-tuple-element.91), channel_id=1, source_target_pairs={{15,1008},{31,0},{47,16},{63,32},{79,48},{95,64},{111,80},{127,96}... | collective-permute-start | bytes 221192 | tf_op jit(solution)/shard_map/ppermute | solution.py:560
  8.8 13.5 %collective-permute-start.10 = (bf16[36,4,256]{2,1,0:T(4,128)(2,1)S(1)}, bf16[36,4,256]{2,1,0:T(4,128)(2,1)S(1)}, u32[]{:S(2)}, u32[]{:S(2)}) collective-permute-start(bf16[36,4,256]{2,1,0:T(4,128)(2,1)S(1)} %get-tuple-element.105), channel_id=1, source_target_pairs={{0,15},{16,31},{32,47},{48,63},{64,79},{80,95},{96,111},{112,127},... | collective-permute-start | bytes 221192 | tf_op jit(solution)/shard_map/ppermute | solution.py:676
  10.1 6.2 %collective-permute-start.2 = (bf16[36,4,256]{2,1,0:T(4,128)(2,1)S(1)}, bf16[36,4,256]{2,1,0:T(4,128)(2,1)S(1)}, u32[]{:S(2)}, u32[]{:S(2)}) collective-permute-start(bf16[36,4,256]{2,1,0:T(4,128)(2,1)S(1)} %param.2), channel_id=1, source_target_pairs={{8,9},{9,8},{10,11},{11,10},{12,13},{13,12},{14,15},{15,14},{24,25... | collective-permute-start | bytes 221192 | tf_op jit(solution)/shard_map/cond/branch_0_fun/ppermute | solution.py:680
  22.6 9.5 %collective-permute-start.3 = (bf16[60,4,256]{2,1,0:T(4,128)(2,1)S(1)}, bf16[60,4,256]{2,1,0:T(4,128)(2,1)S(1)}, u32[]{:S(2)}, u32[]{:S(2)}) collective-permute-start(bf16[60,4,256]{2,1,0:T(4,128)(2,1)S(1)} %get-tuple-element.54), channel_id=1, source_target_pairs={{24,40},{40,24},{56,72},{72,56},{88,104},{104,88},{120,136},{136,1... | collective-permute-start | bytes 368648 | tf_op jit(solution)/shard_map/cond/branch_0_fun/ppermute | solution.py:550
  25.0 7.2 %collective-permute-start.4 = (bf16[60,4,256]{2,1,0:T(4,128)(2,1)S(1)}, bf16[60,4,256]{2,1,0:T(4,128)(2,1)S(1)}, u32[]{:S(2)}, u32[]{:S(2)}) collective-permute-start(bf16[60,4,256]{2,1,0:T(4,128)(2,1)S(1)} %get-tuple-element.55), channel_id=1, source_target_pairs={{8,24},{24,8},{40,56},{56,40},{72,88},{88,72},{104,120},{120,104},... | collective-permute-start | bytes 368648 | tf_op jit(solution)/shard_map/cond/branch_0_fun/ppermute | solution.py:551

commit v10 on v8

--- a/solution.py
+++ b/solution.py
@@ -315,25 +315,6 @@
         copy.wait()
 
 
-def crossed(sizes, over, up, down, one, two, sem):
-    del over
-    copies = []
-    for n, (side, out) in enumerate(zip(side_of(place_of(sizes)[0]), (one, two))):
-        low, high = (pltpu.make_async_copy(source.at[pl.ds(0, BLOCK)], out, sem.at[n]) for source in (up, down))
-
-        @pl.when(side < 0)
-        def _():
-            low.start()
-
-        @pl.when(side > 0)
-        def _():
-            high.start()
-
-        copies.append(low)
-    for copy in copies:
-        copy.wait()
-
-
 def hand_on(*_):
     pass
 
@@ -479,8 +460,9 @@
         aux_at = jnp.where(theirs == 0, DEPTH, 0)
         plain = reader_of(x_messages[n])
 
-        def second(at, plain=plain, other=reader_of(beside[n])):
-            return plain((X_BLOCK[1] + at[0], at[1])) + other(at)
+        def second(at, plain=plain, side=side):
+            up, down = (reader_of(message)(at) for message in beside)
+            return plain((X_BLOCK[1] + at[0], at[1])) + jnp.where(side < 0, up, down)
 
         def first(at, plain=plain):
             return plain((X_BLOCK[0] + at[0], at[1]))
@@ -661,7 +643,7 @@
         return (*exchange_x(*messages, range(half)), *own_atoms(y_low))
 
     def late_ones():
-        messages = x_messages(True, beside[0], back, y_top, y_two, mine, low)
+        messages = x_messages(True, product, back, y_top, y_two, mine, low)
         return (*exchange_x(*messages, range(half, across_y)), *own_atoms(y_top))
 
     from_early = lax.cond(early, early_ones, nothing)
@@ -678,14 +660,6 @@
         early,
         lambda: tuple(call(blank, (), [message(Y_SITES)], out_space=ANY)),
         lambda: (lax.ppermute(top, "gy", pairs[half:]),),
-    )
-    beside = call(
-        functools.partial(crossed, sizes),
-        (over_in, over_up, over_down),
-        [message(BLOCK)] * 2,
-        in_space=ANY,
-        out_space=ANY,
-        scratch_shapes=[pltpu.SemaphoreType.DMA((2,))],
     )
     def result(late, inputs, spaces, **options):
         (product,) = call(
@@ -708,11 +682,11 @@
         )
         return product
 
-    product = result(False, (y_two, over_in, *beside, *from_early), [])
+    product = result(False, (y_two, over_in, over_up, over_down, *from_early), [])
     from_late = lax.cond(early, nothing, late_ones)
     product = result(
         True,
-        (product, y_two, back, *beside, *from_late),
+        (product, y_two, back, over_up, over_down, *from_late),
         [HBM],
         input_output_aliases={0: 0},
     )

time: 34.1 us -> 34.7 us (1.018)
  local copies, waits for them, and re-layouts: 0.01 us -> 0.79 us
  Pallas kernels: 4.78 us -> 4.4 us
    unnamed x2 -> x4, local copies, waits for them, and re-layouts: 0.01 us -> 0.79 us
    pallas_call x10 -> x9, Pallas kernels: 4.78 us -> 4.4 us  [call(): pl.pallas_call(kernel, out_shape=outputs, in_specs=in_space if isinstance...]
where the time goes in v10:
time: 34.7 us; the launch traced here: 34.3 us
  starting transfers between devices  14.1 us (41%)
  waiting for transfers between devices  14.1 us (41%)
  Pallas kernels  4.4 us (13%)
  between operations  0.84 us (2%)
  local copies, waits for them, and re-layouts  0.79 us (2%)
    ppermute x1, waiting for transfers between devices, shards(): back = lax.ppermute(back, 'gy', [(0, across_y - 1)])  5.83 us
    ppermute x3, starting transfers between devices, over_wrap(): return lax.ppermute(message, ('gx', 'gy'), pairs)  5.32 us
    pallas_call x9, Pallas kernels, call(): pl.pallas_call(kernel, out_shape=outputs, in_specs=in_space if isinstance...  4.4 us
    ppermute x1, waiting for transfers between devices, shards(): lax.ppermute(top, 'gy', pairs[half:])  4.32 us
    ppermute x1, waiting for transfers between devices, exchange_x(): two = lax.ppermute(two, ('gx', 'gy'), pairs(1))  3.92 us
    ppermute x1, starting transfers between devices, exchange_x(): two = lax.ppermute(two, ('gx', 'gy'), pairs(1))  2.33 us
    ppermute x1, starting transfers between devices, shards(): lax.ppermute(top, 'gy', pairs[half:])  1.92 us
    ppermute x1, starting transfers between devices, exchange_x(): one = lax.ppermute(one, ('gx', 'gy'), pairs(0))  1.92 us
  transfers between devices with their start and end apart: 9, of which 3 were waited for; matrix products, arithmetic and copies ran while one was open for 0% of the time, Pallas kernels for 4%

profile of v10, /device:TPU:960, one launch (start us, length us, event | category | flops | bytes accessed | tf_op | source)
XLA Modules:
  0.0 34.3 jit_solution(5418335233540959767)
XLA Ops:
  0.7 1.3 %shard_map.55 = (bf16[36,4,256]{2,1,0:T(4,128)(2,1)S(1)}, bf16[36,4,256]{2,1,0:T(4,128)(2,1)S(1)}, bf16[36,4,256]{2,1,0:T(4,128)(2,1)S(1)}, bf16[36,4,256]{2,1,0...) custom-call(bf16[128,4,256]{2,1,0:T(4,128)(2,1)} %bitcast.5, ...), custom_call_target="tpu_custom_call" | custom-call | tf_op jit(solution)/shard_map/pallas_call | solution.py:552
  2.0 0.7 %collective-permute-start.5 = (bf16[36,4,256]{2,1,0:T(4,128)(2,1)S(1)}, bf16[36,4,256]{2,1,0:T(4,128)(2,1)S(1)}, u32[]{:S(2)}, u32[]{:S(2)}) collective-permute-start(bf16[36,4,256]{2,1,0:T(4,128)(2,1)S(1)} %get-tuple-element.86), channel_id=1, source_target_pairs={{1,2},{2,1},{3,4},{4,3},{5,6},{6,5},{7,8},{8,7},{9,10},{10,9},{11,... | collective-permute-start | bytes 221192 | tf_op jit(solution)/shard_map/ppermute | solution.py:603
  2.7 0.7 %collective-permute-start.9 = (bf16[36,4,256]{2,1,0:T(4,128)(2,1)S(1)}, bf16[36,4,256]{2,1,0:T(4,128)(2,1)S(1)}, u32[]{:S(2)}, u32[]{:S(2)}) collective-permute-start(bf16[36,4,256]{2,1,0:T(4,128)(2,1)S(1)} %get-tuple-element.90), channel_id=1, source_target_pairs={{0,1},{1,0},{2,3},{3,2},{4,5},{5,4},{6,7},{7,6},{16,17},{17,16},{1... | collective-permute-start | bytes 221192 | tf_op jit(solution)/shard_map/ppermute | solution.py:604
  3.3 2.7 %collective-permute-start.6 = (bf16[36,4,256]{2,1,0:T(4,128)(2,1)S(1)}, bf16[36,4,256]{2,1,0:T(4,128)(2,1)S(1)}, u32[]{:S(2)}, u32[]{:S(2)}) collective-permute-start(bf16[36,4,256]{2,1,0:T(4,128)(2,1)S(1)} %get-tuple-element.87), channel_id=1, source_target_pairs={{15,0},{31,16},{47,32},{63,48},{79,64},{95,80},{111,96},{127,112},... | collective-permute-start | bytes 221192 | tf_op jit(solution)/shard_map/ppermute | solution.py:542
  6.1 1.3 %collective-permute-start.7 = (bf16[36,4,256]{2,1,0:T(4,128)(2,1)S(1)}, bf16[36,4,256]{2,1,0:T(4,128)(2,1)S(1)}, u32[]{:S(2)}, u32[]{:S(2)}) collective-permute-start(bf16[36,4,256]{2,1,0:T(4,128)(2,1)S(1)} %get-tuple-element.88), channel_id=1, source_target_pairs={{15,16},{31,32},{47,48},{63,64},{79,80},{95,96},{111,112},{127,128... | collective-permute-start | bytes 221192 | tf_op jit(solution)/shard_map/ppermute | solution.py:542
  7.4 1.3 %collective-permute-start.8 = (bf16[36,4,256]{2,1,0:T(4,128)(2,1)S(1)}, bf16[36,4,256]{2,1,0:T(4,128)(2,1)S(1)}, u32[]{:S(2)}, u32[]{:S(2)}) collective-permute-start(bf16[36,4,256]{2,1,0:T(4,128)(2,1)S(1)} %get-tuple-element.89), channel_id=1, source_target_pairs={{15,1008},{31,0},{47,16},{63,32},{79,48},{95,64},{111,80},{127,96}... | collective-permute-start | bytes 221192 | tf_op jit(solution)/shard_map/ppermute | solution.py:542
  8.7 0.0 collective-permute-done.9.y_low
  8.8 1.3 %collective-permute-start.10 = (bf16[36,4,256]{2,1,0:T(4,128)(2,1)S(1)}, bf16[36,4,256]{2,1,0:T(4,128)(2,1)S(1)}, u32[]{:S(2)}, u32[]{:S(2)}) collective-permute-start(bf16[36,4,256]{2,1,0:T(4,128)(2,1)S(1)} %get-tuple-element.101), channel_id=1, source_target_pairs={{0,15},{16,31},{32,47},{48,63},{64,79},{80,95},{96,111},{112,127},... | collective-permute-start | bytes 221192 | tf_op jit(solution)/shard_map/ppermute | solution.py:658
  10.1 6.3 %conditional.4 = (bf16[36,4,256]{2,1,0:T(4,128)(2,1)S(1)}) conditional(s32[]{:T(128)} %convert_element_type.2, bf16[36,4,256]{2,1,0:T(4,128)(2,1)S(1)} %get-tuple-element.102, () %tuple.27), branch_computations={%region_2.0_spmd, %region_3.0_spmd} | conditional | bytes 294960 | solution.py:659
  10.1 1.9 %collective-permute-start.2 = (bf16[36,4,256]{2,1,0:T(4,128)(2,1)S(1)}, bf16[36,4,256]{2,1,0:T(4,128)(2,1)S(1)}, u32[]{:S(2)}, u32[]{:S(2)}) collective-permute-start(bf16[36,4,256]{2,1,0:T(4,128)(2,1)S(1)} %param.2), channel_id=1, source_target_pairs={{8,9},{9,8},{10,11},{11,10},{12,13},{13,12},{14,15},{15,14},{24,25... | collective-permute-start | bytes 221192 | tf_op jit(solution)/shard_map/cond/branch_0_fun/ppermute | solution.py:662
  12.0 4.3 %collective-permute-done.2 = bf16[36,4,256]{2,1,0:T(4,128)(2,1)S(1)} collective-permute-done((bf16[36,4,256]{2,1,0:T(4,128)(2,1)S(1)}, bf16[36,4,256]{2,1,0:T(4,128)(2,1)S(1)}, u32[]{:S(2)}, u32[]{:S(2)}) %collective-permute-start.2) | collective-permute-done | bytes 73760 | tf_op jit(solution)/shard_map/cond/branch_0_fun/ppermute | solution.py:662
  16.3 0.0 collective-permute-done.6.refs_1_
  16.3 0.1 shard_map.57.refs_0_
  16.4 5.8 %collective-permute-done.10.refs_2_ = bf16[36,4,256]{2,1,0:T(4,128)(2,1)S(1)} collective-permute-done((bf16[36,4,256]{2,1,0:T(4,128)(2,1)S(1)}, bf16[36,4,256]{2,1,0:T(4,128)(2,1)S(1)}, u32[]{:S(2)}, u32[]{:S(2)}) %collective-permute-start.10) | collective-permute-done | bytes 73760 | tf_op jit(solution)/shard_map/ppermute | solution.py:658
  22.2 9.9 %conditional.5 = ((bf16[60,4,256]{2,1,0:T(4,128)(2,1)S(1)}, bf16[60,4,256]{2,1,0:T(4,128)(2,1)S(1)}, f32[512,256]{1,0:T(8,128)S(1)}, f32[32,32]{1,0:T(8,128)S(1)...) conditional(s32[]{:T(128)} %convert_element_type.2, ...), branch_computations={%region_4.0_spmd, %region_5.0_spmd} | conditional | bytes 983184 | solution.py:686
  22.2 0.4 %branch_0_fun.5 = (bf16[60,4,256]{2,1,0:T(4,128)(2,1)S(1)}, bf16[60,4,256]{2,1,0:T(4,128)(2,1)S(1)}) custom-call(f32[128,4,256]{2,1,0:T(4,128)S(1)} %get-tuple-element.48.refs_0_, bf16[36,4,256]{2,1,0:T(4,128)(2,1)S(1)} %get-tuple-element.49.refs_1_, bf16[36,4,256]{2,1,0:T(4,128)(2,1)S(1)} %get-tuple-element.50.refs_2_.message, ...), custom_call_target="tpu_custom_call" | custom-call | tf_op jit(solution)/shard_map/cond/branch_0_fun/pallas_call | solution.py:552
  22.6 2.3 %collective-permute-start.3 = (bf16[60,4,256]{2,1,0:T(4,128)(2,1)S(1)}, bf16[60,4,256]{2,1,0:T(4,128)(2,1)S(1)}, u32[]{:S(2)}, u32[]{:S(2)}) collective-permute-start(bf16[60,4,256]{2,1,0:T(4,128)(2,1)S(1)} %get-tuple-element.54), channel_id=1, source_target_pairs={{24,40},{40,24},{56,72},{72,56},{88,104},{104,88},{120,136},{136,1... | collective-permute-start | bytes 368648 | tf_op jit(solution)/shard_map/cond/branch_0_fun/ppermute | solution.py:532
  25.0 1.9 %collective-permute-start.4 = (bf16[60,4,256]{2,1,0:T(4,128)(2,1)S(1)}, bf16[60,4,256]{2,1,0:T(4,128)(2,1)S(1)}, u32[]{:S(2)}, u32[]{:S(2)}) collective-permute-start(bf16[60,4,256]{2,1,0:T(4,128)(2,1)S(1)} %get-tuple-element.55), channel_id=1, source_target_pairs={{8,24},{24,8},{40,56},{56,40},{72,88},{88,72},{104,120},{120,104},... | collective-permute-start | bytes 368648 | tf_op jit(solution)/shard_map/cond/branch_0_fun/ppermute | solution.py:533
  26.9 0.7 %branch_0_fun.6.acc_in = f32[512,256]{1,0:T(8,128)S(1)} custom-call(bf16[128,4,256]{2,1,0:T(4,128)(2,1)S(1)} %get-tuple-element.52.refs_4_.trial, f32[16,256]{1,0:T(8,128)S(1)} %get-tuple-element.56.aux), custom_call_target="tpu_custom_call" | custom-call | tf_op jit(solution)/shard_map/cond/branch_0_fun/pallas_call | solution.py:552
  27.6 0.6 %branch_0_fun.7 = (f32[512,256]{1,0:T(8,128)S(1)}, f32[32,32]{1,0:T(8,128)S(1)}, f32[32,8]{1,0:T(8,128)S(1)}, f32[2,32,48]{2,1,0:T(8,128)S(1)}, f32[2,32,8]{2,1,0:T(8,128)S(1)}) custom-call(f32[16,256]{1,0:T(8,128)S(1)} %get-tuple-element.56.aux, bf16[36,4,256]{2,1,0:T(4,128)(2,1)S(1)} %get-tuple-element.50.refs_2_.message, f32[512,256]{1,0:T(8,128)S(1)} %branch_0_fun.6.acc_in), custom_call_target="tpu_custom_call" | custom-call | tf_op jit(solution)/shard_map/cond/branch_0_fun/pallas_call | solution.py:552
  28.2 3.9 %collective-permute-done.3 = bf16[60,4,256]{2,1,0:T(4,128)(2,1)S(1)} collective-permute-done((bf16[60,4,256]{2,1,0:T(4,128)(2,1)S(1)}, bf16[60,4,256]{2,1,0:T(4,128)(2,1)S(1)}, u32[]{:S(2)}, u32[]{:S(2)}) %collective-permute-start.3) | collective-permute-done | bytes 122912 | tf_op jit(solution)/shard_map/cond/branch_0_fun/ppermute | solution.py:532
  32.2 1.3 %shard_map.59 = f32[128,4,256]{2,1,0:T(4,128)S(1)} custom-call(f32[128,4,256]{2,1,0:T(4,128)S(1)} %shard_map.57.refs_0_, bf16[36,4,256]{2,1,0:T(4,128)(2,1)S(1)} %collective-permute-done.5.y_two.refs_0_.refs_1_, bf16[36,4,256]{2,1,0:T(4,128)(2,1)S(1)} %collective-permute-done.10.refs_2_, ...), custom_call_target="tpu_custom_call", output_to_operand_aliasing={{}: (0, {})} | custom-call | tf_op jit(solution)/shard_map/pallas_call | solution.py:552
  33.5 0.0 copy-start.1
  33.5 0.8 %copy-done.1 = f32[128,4,256]{2,1,0:T(4,128)} copy-done((f32[128,4,256]{2,1,0:T(4,128)}, f32[128,4,256]{2,1,0:T(4,128)S(1)}, u32[]{:S(2)}) %copy-start.1) | copy-done | bytes 524312
  (10 shorter events, 0.0 us)
Async XLA Ops:
  0.0 8.7 %copy-start = (bf16[4,4,8,4,256]{4,3,2,1,0:T(4,128)(2,1)S(1)}, bf16[4,4,8,4,256]{4,3,2,1,0:T(4,128)(2,1)}, u32[]{:S(2)}) copy-start(bf16[4,4,8,4,256]{4,3,2,1,0:T(4,128)(2,1)} %param.12) | copy-start | bytes 786436
  2.0 6.7 %collective-permute-start.5 = (bf16[36,4,256]{2,1,0:T(4,128)(2,1)S(1)}, bf16[36,4,256]{2,1,0:T(4,128)(2,1)S(1)}, u32[]{:S(2)}, u32[]{:S(2)}) collective-permute-start(bf16[36,4,256]{2,1,0:T(4,128)(2,1)S(1)} %get-tuple-element.86), channel_id=1, source_target_pairs={{1,2},{2,1},{3,4},{4,3},{5,6},{6,5},{7,8},{8,7},{9,10},{10,9},{11,... | collective-permute-start | bytes 221192 | tf_op jit(solution)/shard_map/ppermute | solution.py:603
  2.7 6.0 %collective-permute-start.9 = (bf16[36,4,256]{2,1,0:T(4,128)(2,1)S(1)}, bf16[36,4,256]{2,1,0:T(4,128)(2,1)S(1)}, u32[]{:S(2)}, u32[]{:S(2)}) collective-permute-start(bf16[36,4,256]{2,1,0:T(4,128)(2,1)S(1)} %get-tuple-element.90), channel_id=1, source_target_pairs={{0,1},{1,0},{2,3},{3,2},{4,5},{5,4},{6,7},{7,6},{16,17},{17,16},{1... | collective-permute-start | bytes 221192 | tf_op jit(solution)/shard_map/ppermute | solution.py:604
  3.3 13.0 %collective-permute-start.6 = (bf16[36,4,256]{2,1,0:T(4,128)(2,1)S(1)}, bf16[36,4,256]{2,1,0:T(4,128)(2,1)S(1)}, u32[]{:S(2)}, u32[]{:S(2)}) collective-permute-start(bf16[36,4,256]{2,1,0:T(4,128)(2,1)S(1)} %get-tuple-element.87), channel_id=1, source_target_pairs={{15,0},{31,16},{47,32},{63,48},{79,64},{95,80},{111,96},{127,112},... | collective-permute-start | bytes 221192 | tf_op jit(solution)/shard_map/ppermute | solution.py:542
  6.1 10.3 %collective-permute-start.7 = (bf16[36,4,256]{2,1,0:T(4,128)(2,1)S(1)}, bf16[36,4,256]{2,1,0:T(4,128)(2,1)S(1)}, u32[]{:S(2)}, u32[]{:S(2)}) collective-permute-start(bf16[36,4,256]{2,1,0:T(4,128)(2,1)S(1)} %get-tuple-element.88), channel_id=1, source_target_pairs={{15,16},{31,32},{47,48},{63,64},{79,80},{95,96},{111,112},{127,128... | collective-permute-start | bytes 221192 | tf_op jit(solution)/shard_map/ppermute | solution.py:542
  7.4 9.0 %collective-permute-start.8 = (bf16[36,4,256]{2,1,0:T(4,128)(2,1)S(1)}, bf16[36,4,256]{2,1,0:T(4,128)(2,1)S(1)}, u32[]{:S(2)}, u32[]{:S(2)}) collective-permute-start(bf16[36,4,256]{2,1,0:T(4,128)(2,1)S(1)} %get-tuple-element.89), channel_id=1, source_target_pairs={{15,1008},{31,0},{47,16},{63,32},{79,48},{95,64},{111,80},{127,96}... | collective-permute-start | bytes 221192 | tf_op jit(solution)/shard_map/ppermute | solution.py:542
  8.8 13.5 %collective-permute-start.10 = (bf16[36,4,256]{2,1,0:T(4,128)(2,1)S(1)}, bf16[36,4,256]{2,1,0:T(4,128)(2,1)S(1)}, u32[]{:S(2)}, u32[]{:S(2)}) collective-permute-start(bf16[36,4,256]{2,1,0:T(4,128)(2,1)S(1)} %get-tuple-element.101), channel_id=1, source_target_pairs={{0,15},{16,31},{32,47},{48,63},{64,79},{80,95},{96,111},{112,127},... | collective-permute-start | bytes 221192 | tf_op jit(solution)/shard_map/ppermute | solution.py:658
  10.1 6.2 %collective-permute-start.2 = (bf16[36,4,256]{2,1,0:T(4,128)(2,1)S(1)}, bf16[36,4,256]{2,1,0:T(4,128)(2,1)S(1)}, u32[]{:S(2)}, u32[]{:S(2)}) collective-permute-start(bf16[36,4,256]{2,1,0:T(4,128)(2,1)S(1)} %param.2), channel_id=1, source_target_pairs={{8,9},{9,8},{10,11},{11,10},{12,13},{13,12},{14,15},{15,14},{24,25... | collective-permute-start | bytes 221192 | tf_op jit(solution)/shard_map/cond/branch_0_fun/ppermute | solution.py:662
  22.6 9.5 %collective-permute-start.3 = (bf16[60,4,256]{2,1,0:T(4,128)(2,1)S(1)}, bf16[60,4,256]{2,1,0:T(4,128)(2,1)S(1)}, u32[]{:S(2)}, u32[]{:S(2)}) collective-permute-start(bf16[60,4,256]{2,1,0:T(4,128)(2,1)S(1)} %get-tuple-element.54), channel_id=1, source_target_pairs={{24,40},{40,24},{56,72},{72,56},{88,104},{104,88},{120,136},{136,1... | collective-permute-start | bytes 368648 | tf_op jit(solution)/shard_map/cond/branch_0_fun/ppermute | solution.py:532
  25.0 7.2 %collective-permute-start.4 = (bf16[60,4,256]{2,1,0:T(4,128)(2,1)S(1)}, bf16[60,4,256]{2,1,0:T(4,128)(2,1)S(1)}, u32[]{:S(2)}, u32[]{:S(2)}) collective-permute-start(bf16[60,4,256]{2,1,0:T(4,128)(2,1)S(1)} %get-tuple-element.55), channel_id=1, source_target_pairs={{8,24},{24,8},{40,56},{56,40},{72,88},{88,72},{104,120},{120,104},... | collective-permute-start | bytes 368648 | tf_op jit(solution)/shard_map/cond/branch_0_fun/ppermute | solution.py:533
  33.5 0.8 %copy-start.1 = (f32[128,4,256]{2,1,0:T(4,128)}, f32[128,4,256]{2,1,0:T(4,128)S(1)}, u32[]{:S(2)}) copy-start(f32[128,4,256]{2,1,0:T(4,128)S(1)} %shard_map.59) | copy-start | bytes 1572868
